TPU v7x, 128 devices: a whole 4x4x4 slice. The times are simulated.
128 devices in a mesh: row: 16 (over x, z), col: 8 (over y, core).
Axes of the slice: x: 4, y: 4, z: 4, core: 2. Of those that a mesh axis runs over, the one named last changes fastest.
Arguments:
- ancestor_inv: float32 [6144, 6144], P('row', 'col'), as said below
- panel_one: float32 [6144, 2048], P('col', 'row'), may hold values from -0.078125 to 0.078125
- panel_two: float32 [6144, 4096], P('col', 'row'), may hold values from -0.078125 to 0.078125
- parent_block: float32 [16, 256, 256], P('col'), may hold values from -0.375 to 0.375
- diag_one: float32 [8, 256, 256], P('col'), may hold values from -6 to 6
- diag_two: float32 [16, 256, 256], P('col'), may hold values from -6 to 6
- pattern_one: int32 [24, 8], replicated, may hold values 0 or 1
- pattern_two: int32 [24, 16], replicated, may hold values 0 or 1
Outputs:
- inv_one: float32 [6144, 2048], P('row', 'col')
- diag_inv_one: float32 [8, 256, 256], P('col')
- inv_two: float32 [6144, 4096], P('row', 'col')
- inv_par: float32 [16, 256, 256], P('col')
- diag_inv_two: float32 [16, 256, 256], P('col')
Inputs may be any that keep to these rules, and one draw needn't show every extreme that they name: `ancestor_inv`: equal to its own transpose.
All inputs are finite; a program needn't handle non-finite values.
Results may differ from a plain program's by a relative error of at most 0.000071.
Values sent between devices are 32-bit elements; how exact they have to be, the bound alone decides.
No kernel may reach another device: no remote copies, remote signals or barrier semaphores. Data moves between devices by JAX's collectives and lax.ppermute only.
A program may use at most 128 MiB of HBM per device.

v0:
```python
import functools

import jax
import jax.numpy as jnp
from jax import lax
from jax.experimental import pallas as pl
from jax.experimental.pallas import tpu as pltpu
from jax.sharding import Mesh, PartitionSpec as P

BLOCK = 256
CHILDREN = 2
HIGH = lax.Precision.HIGH
HIGHEST = lax.Precision.HIGHEST


def fetch(value, axis, shift):
    size = lax.axis_size(axis)
    return lax.ppermute(value, axis, [((i + shift) % size, i) for i in range(size)])


def swap(value):
    return lax.ppermute(value, "core", [(0, 1), (1, 0)])


def split_pairs(step):
    return [(i * 2 + c, (i + (step, -step)[c]) % 4 * 2 + c) for i in range(4) for c in range(2)]


def send(value, axis, step):
    return lax.ppermute(value, (axis, "core"), split_pairs(step))


def after(value, *deps):
    return lax.optimization_barrier((value, *deps))[0] if deps else value


def pick(stack, index):
    return lax.dynamic_index_in_dim(stack, index, axis=0, keepdims=False)


def split(value):
    high = value.astype(jnp.bfloat16)
    return high, (value - high.astype(jnp.float32)).astype(jnp.bfloat16)


def take(refs, to, sems, chosen=None):
    if chosen is None:
        copies = [
            pltpu.make_async_copy(ref, to.at[k], sems.at[k]) for k, ref in enumerate(refs)
        ]
        for copy in copies:
            copy.start()
        return copies
    for k in range(len(refs) // 2):

        @pl.when(chosen == k)
        def _(k=k):
            for p in range(2):
                pltpu.make_async_copy(refs[2 * k + p], to.at[p], sems.at[p]).start()

    return [pltpu.make_async_copy(refs[p], to.at[p], sems.at[p]) for p in range(2)]


def multiply(out, row_high, row_low, strip, strip_high, strip_low):
    deep, chunk = strip.shape[1], 64
    for p in range(2):

        @pl.loop(0, deep // chunk)
        def _(i, p=p):
            high, low = split(strip[p, pl.ds(i * chunk, chunk), :])
            at = pl.ds(p * deep + i * chunk, chunk)
            strip_high[at, :] = high
            strip_low[at, :] = low

    dot = functools.partial(jnp.dot, preferred_element_type=jnp.float32)
    tall = out.shape[0] // 2

    @pl.loop(0, 2)
    def _(r):
        at = pl.ds(pl.multiple_of(r * tall, tall), tall)
        value = dot(row_high[at, :], strip_low[...]) + dot(row_low[at, :], strip_high[...])
        out[at, :] = value + dot(row_high[at, :], strip_high[...])


def first_kernel(places, *refs):
    rows, strips = refs[:4], refs[4:12]
    out_high, out_low, out = refs[12:15]
    row, row_high, row_low, strip, strip_high, strip_low, row_sems, sems = refs[15:]
    row_copies = take(rows, row, row_sems)
    strip_copies = take(strips, strip, sems, places[4])
    half, deep = rows[0].shape[1:]
    chunk = 64
    for k, copy in enumerate(row_copies):
        copy.wait()
        first = places[k] * half
        for p in range(2):

            @pl.loop(0, half // chunk)
            def _(i, k=k, p=p, first=first):
                high, low = split(row[k, p, pl.ds(i * chunk, chunk), :])
                at = pl.ds(pl.multiple_of(first + i * chunk, chunk), chunk)
                row_high[at, pl.ds(p * deep, deep)] = high
                row_low[at, pl.ds(p * deep, deep)] = low

    outs = [
        pltpu.make_async_copy(row_high, out_high, row_sems.at[0]),
        pltpu.make_async_copy(row_low, out_low, row_sems.at[1]),
    ]
    for copy in outs:
        copy.start()
    for copy in strip_copies:
        copy.wait()
    multiply(out, row_high, row_low, strip, strip_high, strip_low)
    for copy in outs:
        copy.wait()


def next_kernel(places, *refs):
    rows, strips = refs[:2], refs[2:10]
    out, row_high, row_low, strip, strip_high, strip_low, row_sems, sems = refs[10:]
    row_copies = [
        pltpu.make_async_copy(ref, to, row_sems.at[p])
        for p, (ref, to) in enumerate(zip(rows, (row_high, row_low)))
    ]
    strip_copies = take(strips, strip, sems, places[0])
    for copy in row_copies:
        copy.start()
    for copy in strip_copies:
        copy.wait()
    for copy in row_copies:
        copy.wait()
    multiply(out, row_high, row_low, strip, strip_high, strip_low)


def product(places, rows, strips):
    vmem, hbm = (pl.BlockSpec(memory_space=m) for m in (pltpu.VMEM, pltpu.HBM))
    deep, wide = strips[0].shape
    first = len(rows) == 4
    tall = 4 * rows[0].shape[1] if first else rows[0].shape[0]
    parts = jax.ShapeDtypeStruct((tall, 2 * deep), jnp.bfloat16)
    out = jax.ShapeDtypeStruct((tall, wide), jnp.float32)
    scratch = [pltpu.VMEM((tall, 2 * deep), jnp.bfloat16)] * 2
    scratch += [pltpu.VMEM((2, deep, wide), jnp.float32)]
    scratch += [pltpu.VMEM((2 * deep, wide), jnp.bfloat16)] * 2
    if first:
        scratch = [pltpu.VMEM((4, *rows[0].shape), jnp.float32)] + scratch
    results = pl.pallas_call(
        first_kernel if first else next_kernel,
        out_shape=[parts, parts, out] if first else [out],
        in_specs=[pl.BlockSpec(memory_space=pltpu.SMEM)] + [hbm] * (len(rows) + 8),
        out_specs=[hbm, hbm, vmem] if first else [vmem],
        scratch_shapes=scratch
        + [pltpu.SemaphoreType.DMA((4 if first else 2,)), pltpu.SemaphoreType.DMA((2,))],
        compiler_params=pltpu.CompilerParams(vmem_limit_bytes=56 * 2**20),
        cost_estimate=pl.CostEstimate(
            flops=tall, bytes_accessed=tall, transcendentals=0
        ),
        name="first_product" if first else "next_product",
    )(jnp.stack(places).astype(jnp.int32), *rows, *strips)
    return results if first else results[0]


def local(
    ancestor_inv, panel_one, panel_two, parent_block, diag_one, diag_two, pattern_one, pattern_two
):
    x, z, y, core = (lax.axis_index(a) for a in ("x", "z", "y", "core"))
    row_index = x * 4 + z
    col_index = y * 2 + core
    panel_rows, w1 = panel_one.shape
    w2 = panel_two.shape[1]
    span = w1 + w2
    half = ancestor_inv.shape[0] // 2
    child_pattern = pattern_two * jnp.repeat(pattern_one, CHILDREN, axis=1)
    with jax.named_scope("gather"):
        halves = ancestor_inv.reshape(2, half, panel_rows)
        given = pick(halves, 1 - core)
        panel_one, panel_two = after(panel_one, given), after(panel_two, given)
        given = swap(given)
    with jax.named_scope("mask"):
        blocks = panel_rows // BLOCK
        mask_one = lax.dynamic_slice(
            pattern_one, (col_index * blocks, row_index // CHILDREN), (blocks, 1)
        )
        mask_two = mask_one * lax.dynamic_slice(
            pattern_two, (col_index * blocks, row_index), (blocks, 1)
        )
        lhs = jnp.concatenate(
            [
                (p.reshape(blocks, BLOCK, -1) * m.astype(jnp.float32)[:, :, None]).reshape(
                    panel_rows, -1
                )
                for p, m in ((panel_one, mask_one), (panel_two, mask_two))
            ],
            axis=1,
        )
    side = jnp.where(core == 0, -1, 1)

    def place(offset):
        offset = offset % 4
        return jnp.where(
            offset == 0, 0, jnp.where(offset == 2, 3, jnp.where(offset == side % 4, 1, 2))
        )

    with jax.named_scope("gather"):
        rows = jnp.stack((pick(halves, core), given))
        lhs = after(lhs, given)
        lhs_other = swap(lhs)
        mine, other = (
            lax.dynamic_index_in_dim(v.reshape(2, 2, half, span), core, axis=1, keepdims=False)
            for v in (lhs, lhs_other)
        )
        source = jnp.concatenate(
            (jnp.where(core == 0, mine, other), jnp.where(core == 0, other, mine)), axis=0
        ).reshape(panel_rows, span)
        source = after(source, rows)
        a_first, a_second = send(rows, "z", 1), send(rows, "z", -1)
        l_first, l_second = send(lhs, "x", 1), send(lhs, "x", -1)
        t_first = send(source, "y", 1)
        t_second = send(after(source, t_first), "y", -1)
        a_first, a_second, l_first, l_second, t_second = lax.optimization_barrier(
            (a_first, a_second, l_first, l_second, t_second)
        )
        a_far, l_far = send(a_first, "z", 1), send(l_first, "x", 1)
        t_far = send(after(t_first, t_second), "y", 1)
        first_other, second_other = swap(l_second), swap(l_first)
        a_far, l_far, t_far, first_other, second_other = lax.optimization_barrier(
            (a_far, l_far, t_far, first_other, second_other)
        )
        far_other = swap(l_far)

    def spread(values):
        return [
            lax.ppermute(
                value,
                ("z", "core"),
                [
                    ((2 * c + j) * 2 + h, ((2 * j + h) ^ turn_over) * 2 + c)
                    for c in range(2)
                    for j in range(2)
                    for h in range(2)
                ],
            )
            for turn_over, value in enumerate(values)
        ]

    def turn(value, offset, which=0):
        pairs = []
        for i in range(4):
            for c, m in ((0, 1), (1, -1)):
                begin = i + which * m
                end = begin + offset * m
                pairs.append(((begin % 4 * 4 + i) * 2 + c, (end % 4 * 4 + i) * 2 + c))
        return lax.ppermute(value, ("x", "y", "core"), pairs)

    strips = (lhs, lhs_other, l_first, first_other, l_second, second_other, l_far, far_other)
    offsets = (0, side, -side, 2)

    def strip_of(offset):
        return place(y + offset - x)

    with jax.named_scope("product"):
        *parts, far = product(
            [(z + o) % 4 for o in offsets] + [strip_of(2)],
            (rows, a_first, a_second, a_far),
            strips,
        )
        far_came = send(far, "y", 1)
        q_step = turn(after(t_far, l_far), 1)
        q_first = turn(after(t_first, l_far), -1)
        near = product([strip_of(side)], [after(p, far) for p in parts], strips)
        near_came = send(near, "y", -1)
        q_far = turn(after(q_step, near), 1, 1)
        q_second = turn(after(t_second, q_first, near), 1)
        last = product([strip_of(-side)], [after(p, near, far_came) for p in parts], strips)
        last = after(last, near_came) + far_came
        last_came = send(last, "y", 1)
    with jax.named_scope("turned"):
        shift = (x - y) % 4
        turned = jnp.where(
            shift == 0,
            source,
            jnp.where(
                shift == 2, q_far, jnp.where(shift == side % 4, q_first, q_second)
            ),
        )
        own = turned[:, :w1]
        mate = lax.ppermute(own, "z", [(0, 1), (1, 0), (2, 3), (3, 2)])
        full_one = jnp.concatenate(
            (jnp.where(z % 2 == 0, own, mate), jnp.where(z % 2 == 0, mate, own)), axis=1
        )
    with jax.named_scope("total"):
        rest = product([strip_of(0)], [after(p, last, turned) for p in parts], strips)
        rest, near_came, last_came = lax.optimization_barrier((rest, near_came, last_came))
        total = rest + near_came + last_came
    with jax.named_scope("out"):
        pairs_of_rows = total.reshape(2, 2 * half, span)
        kept, came = pick(pairs_of_rows, core), swap(pick(pairs_of_rows, 1 - core))
        kept, came = kept.reshape(2, half, span), came.reshape(2, half, span)
        blocks = jnp.concatenate(
            (jnp.where(core == 0, kept, came), jnp.where(core == 0, came, kept)), axis=1
        )
        pieces = []
        for turn_over in range(2):
            pairs = [
                ((2 * c + j) * 2 + h, (2 * h + (j + turn_over) % 2) * 2 + c)
                for c in range(2)
                for j in range(2)
                for h in range(2)
            ]
            pieces.append(lax.ppermute(pick(blocks, (z + turn_over) % 2), ("z", "core"), pairs))
    with jax.named_scope("quad"):
        quad_one = lax.dot_general(full_one, total, (((0,), (0,)), ((), ())), precision=HIGH)
        quad_two = lax.dot_general(
            turned[:, w1:], total[:, w1:], (((0,), (0,)), ((), ())), precision=HIGH
        )
        quad = jnp.concatenate((quad_one, quad_two), axis=1)
        wide = quad.shape[1]
        quad = quad.reshape(2, BLOCK // 2, wide)
        quad = pick(quad, core) + swap(pick(quad, 1 - core))
        first, second = send(quad, "x", 1), send(quad, "x", -1)
        around = quad + first + second + send(first, "x", 1)
        around = after(around, *pieces)
        came = jnp.stack(spread([around] * 4))
        sums = [
            jnp.concatenate([pick(came, (2 * j + h) ^ z) for h in range(2)], axis=0)
            for j in range(2)
        ]
    with jax.named_scope("out"):
        joined = [jnp.where(z % 2 == j, pieces[0], pieces[1]) for j in range(2)]
        prod_one = jnp.concatenate([v[:, :w1] for v in joined], axis=1)
        inv_one = -prod_one
        inv_two = jnp.concatenate(
            [
                jnp.dot(prod_one, parent_block[i], precision=HIGH) - joined[i][:, w1:]
                for i in range(2)
            ],
            axis=1,
        )
    with jax.named_scope("diag"):
        first = jnp.concatenate((sums[0][:, :w1], sums[1][:, :w1]), axis=1)
        across = jnp.stack([s[:, w1 : w1 + w2] for s in sums])
        reach = jnp.stack([s[:, w1 + w2 :] for s in sums])
        diag_inv_one = diag_one + first[None]
        inv_par = across - jnp.einsum("ab,pbc->pac", diag_inv_one[0], parent_block, precision=HIGH)
        diag_inv_two = (
            diag_two
            + reach
            - jnp.einsum("pba,pbc->pac", across, parent_block, precision=HIGH)
            - jnp.einsum("pba,pbc->pac", parent_block, inv_par, precision=HIGH)
        )
    return (inv_one, diag_inv_one, inv_two, inv_par, diag_inv_two)


def solution(mesh):
    grid = Mesh(mesh.devices.reshape(4, 4, 4, 2), ("x", "z", "y", "core"))
    row, col = ("x", "z"), ("y", "core")
    return jax.shard_map(
        local,
        mesh=grid,
        in_specs=(
            P(row, col),
            P(col, row),
            P(col, row),
            P(col, None, None),
            P(col, None, None),
            P(col, None, None),
            P(),
            P(),
        ),
        out_specs=(
            P(row, col),
            P(col, None, None),
            P(row, col),
            P(col, None, None),
            P(col, None, None),
        ),
        check_vma=False,
    )
```

profile of v0, /device:TPU:0, one launch (start us, length us, event | category | flops | bytes accessed | tf_op | source)
XLA Modules:
  0.0 194.9 jit_solution(6899735772681388982)
XLA Ops:
  0.7 2.2 %constant_dynamic-slice_fusion.1 = (f32[1,192,768]{2,1,0:T(8,128)S(1)}, f32[192,768]{1,0:T(8,128)}) fusion(f32[2,192,768]{2,1,0:T(8,128)} %bitcast.101, s32[]{:T(128)S(6)} %select_n.251, s32[]{:T(128)S(6)} %select_n.252), kind=kLoop, calls=%fused_computation.70 | loop fusion | bytes 2359304 | tf_op jit(solution)/shard_map/gather/jit(dynamic_index_in_dim)/dynamic_slice | solution.py:38
  2.9 0.8 convert_bitcast_fusion.1
  4.3 0.9 collective-permute-done
  5.4 1.1 pad_maximum_fusion.1.refs_0_
  6.5 1.6 collective-permute-done.5.refs_5_.refs_3_
  8.2 0.9 copy-done.1
  9.2 1.7 collective-permute-start.6
  10.9 1.5 collective-permute-start.3
  12.4 1.7 collective-permute-start.4
  14.2 1.9 collective-permute-start.1
  16.1 2.1 %collective-permute-start.2 = (f32[2,192,768]{2,1,0:T(8,128)S(1)}, f32[2,192,768]{2,1,0:T(8,128)S(1)}, u32[]{:S(2)}, u32[]{:S(2)}) collective-permute-start(f32[2,192,768]{2,1,0:T(8,128)S(1)} %pad_maximum_fusion.1.refs_0_), channel_id=1, source_target_pairs={{0,24},{1,9},{8,0},{9,17},{16,8},{17,25},{24,16},{25,1},{2,26},{3,... | collective-permute-start | bytes 3538952 | tf_op jit(solution)/shard_map/gather/ppermute | solution.py:30
  18.2 8.6 %collective-permute-done.6 = f32[768,384]{1,0:T(8,128)} collective-permute-done((f32[768,384]{1,0:T(8,128)S(1)}, f32[768,384]{1,0:T(8,128)}, u32[]{:S(2)}, u32[]{:S(2)}) %collective-permute-start.6) | collective-permute-done | bytes 1179680 | tf_op jit(solution)/shard_map/gather/ppermute | solution.py:30
  26.8 1.9 collective-permute-start.7
  28.7 9.4 %collective-permute-done.3.refs_6_.refs_4_ = f32[768,384]{1,0:T(8,128)S(1)} collective-permute-done((f32[768,384]{1,0:T(8,128)S(1)}, f32[768,384]{1,0:T(8,128)S(1)}, u32[]{:S(2)}, u32[]{:S(2)}) %collective-permute-start.3) | collective-permute-done | bytes 1179680 | tf_op jit(solution)/shard_map/gather/ppermute | solution.py:30
  38.1 2.3 %collective-permute-done.4.refs_8_.refs_6_ = f32[768,384]{1,0:T(8,128)S(1)} collective-permute-done((f32[768,384]{1,0:T(8,128)S(1)}, f32[768,384]{1,0:T(8,128)S(1)}, u32[]{:S(2)}, u32[]{:S(2)}) %collective-permute-start.4) | collective-permute-done | bytes 1179680 | tf_op jit(solution)/shard_map/gather/ppermute | solution.py:30
  40.4 2.1 %collective-permute-done.1.refs_1_ = f32[2,192,768]{2,1,0:T(8,128)S(1)} collective-permute-done((f32[2,192,768]{2,1,0:T(8,128)S(1)}, f32[2,192,768]{2,1,0:T(8,128)S(1)}, u32[]{:S(2)}, u32[]{:S(2)}) %collective-permute-start.1) | collective-permute-done | bytes 1179680 | tf_op jit(solution)/shard_map/gather/ppermute | solution.py:30
  42.4 1.7 collective-permute-done.2.refs_2_
  44.2 2.5 %collective-permute-start.10 = (f32[768,384]{1,0:T(8,128)}, f32[768,384]{1,0:T(8,128)}, u32[]{:S(2)}, u32[]{:S(2)}) collective-permute-start(f32[768,384]{1,0:T(8,128)} %collective-permute-done.6), channel_id=1, source_target_pairs={{0,2},{1,7},{2,4},{3,1},{4,6},{5,3},{6,0},{7,5},{8,10},{9,15},{10,... | collective-permute-start | bytes 3538952 | tf_op jit(solution)/shard_map/gather/ppermute | solution.py:30
  46.7 0.5 collective-permute-start.12
  47.5 14.4 %collective-permute-done.10 = f32[768,384]{1,0:T(8,128)} collective-permute-done((f32[768,384]{1,0:T(8,128)}, f32[768,384]{1,0:T(8,128)}, u32[]{:S(2)}, u32[]{:S(2)}) %collective-permute-start.10) | collective-permute-done | bytes 1179680 | tf_op jit(solution)/shard_map/gather/ppermute | solution.py:30
  61.9 2.7 %collective-permute-done.8.refs_3_ = f32[2,192,768]{2,1,0:T(8,128)S(1)} collective-permute-done((f32[2,192,768]{2,1,0:T(8,128)S(1)}, f32[2,192,768]{2,1,0:T(8,128)S(1)}, u32[]{:S(2)}, u32[]{:S(2)}) %collective-permute-start.8) | collective-permute-done | bytes 1179680 | tf_op jit(solution)/shard_map/gather/ppermute | solution.py:30
  64.7 6.4 %collective-permute-start.18 = (f32[768,384]{1,0:T(8,128)}, f32[768,384]{1,0:T(8,128)}, u32[]{:S(2)}, u32[]{:S(2)}) collective-permute-start(f32[768,384]{1,0:T(8,128)} %collective-permute-done.6), channel_id=1, source_target_pairs={{0,96},{1,33},{34,2},{35,67},{68,36},{69,101},{102,70},{103,7},{8,... | collective-permute-start | bytes 3538952 | tf_op jit(solution)/shard_map/product/ppermute | solution.py:253
  71.1 2.3 %collective-permute-start.16 = (f32[768,384]{1,0:T(8,128)}, f32[768,384]{1,0:T(8,128)}, u32[]{:S(2)}, u32[]{:S(2)}) collective-permute-start(f32[768,384]{1,0:T(8,128)} %collective-permute-done.10), channel_id=1, source_target_pairs={{0,32},{1,97},{34,66},{35,3},{68,100},{69,37},{102,6},{103,71},{8,... | collective-permute-start | bytes 3538952 | tf_op jit(solution)/shard_map/product/ppermute | solution.py:253
  73.4 0.7 stack.73.places
  74.0 9.2 %first_product.1 = (bf16[768,1536]{1,0:T(8,128)(2,1)}, bf16[768,1536]{1,0:T(8,128)(2,1)}, f32[768,384]{1,0:T(8,128)}) custom-call(s32[5]{0:T(128)} %stack.73.places, f32[2,192,768]{2,1,0:T(8,128)} %copy-done.10, f32[2,192,768]{2,1,0:T(8,128)} %copy-done.14, f32[2,192,768]{2,1,0:T(8,128)} %copy-done.15, f32[2,192,768]{2,1,0:T(8,128)} %copy-done.16, ...), custom_call_target="tpu_custom_call" | custom-call | flops 768 | bytes 768 | tf_op jit(solution)/shard_map/product/first_product/pallas_call | solution.py:147
  83.3 8.6 %next_product.3 = f32[768,384]{1,0:T(8,128)} custom-call(s32[1]{0:T(128)} %bitcast.20.places, bf16[768,1536]{1,0:T(8,128)(2,1)} %get-tuple-element.67.refs_0_, bf16[768,1536]{1,0:T(8,128)(2,1)} %get-tuple-element.68.refs_1_, f32[768,384]{1,0:T(8,128)} %copy-done, f32[768,384]{1,0:T(8,128)} %copy-done.1, f32[768,384]{1,0:T(8,128)} %copy-done.2, ...), custom_call_target="tpu_custom_call" | custom-call | flops 768 | bytes 768 | tf_op jit(solution)/shard_map/product/next_product/pallas_call | solution.py:147
  91.9 3.3 %collective-permute-start.15 = (f32[768,384]{1,0:T(8,128)}, f32[768,384]{1,0:T(8,128)}, u32[]{:S(2)}, u32[]{:S(2)}) collective-permute-start(f32[768,384]{1,0:T(8,128)} %next_product.3), channel_id=1, source_target_pairs={{0,6},{1,3},{2,0},{3,5},{4,2},{5,7},{6,4},{7,1},{8,14},{9,11},{10,... | collective-permute-start | bytes 3538952 | tf_op jit(solution)/shard_map/product/ppermute | solution.py:30
  95.2 0.8 collective-permute-done.18
  96.0 1.4 collective-permute-start.19
  97.3 1.7 collective-permute-start.17
  99.0 7.7 %collective-permute-done.14 = f32[768,384]{1,0:T(8,128)S(1)} collective-permute-done((f32[768,384]{1,0:T(8,128)}, f32[768,384]{1,0:T(8,128)S(1)}, u32[]{:S(2)}, u32[]{:S(2)}) %collective-permute-start.14) | collective-permute-done | bytes 1179680 | tf_op jit(solution)/shard_map/product/ppermute | solution.py:30
  106.7 9.0 %next_product.4 = f32[768,384]{1,0:T(8,128)} custom-call(s32[1]{0:T(128)} %bitcast.19.places, bf16[768,1536]{1,0:T(8,128)(2,1)} %get-tuple-element.67.refs_0_, bf16[768,1536]{1,0:T(8,128)(2,1)} %get-tuple-element.68.refs_1_, f32[768,384]{1,0:T(8,128)} %copy-done, f32[768,384]{1,0:T(8,128)} %copy-done.1, f32[768,384]{1,0:T(8,128)} %copy-done.2, ...), custom_call_target="tpu_custom_call" | custom-call | flops 768 | bytes 768 | tf_op jit(solution)/shard_map/product/next_product/pallas_call | solution.py:147
  115.8 1.8 add.170
  117.7 1.0 copy-done.12
  118.7 1.5 select_select_fusion
  120.6 8.6 %next_product.5 = f32[768,384]{1,0:T(8,128)} custom-call(s32[1]{0:T(128)} %bitcast.places, bf16[768,1536]{1,0:T(8,128)(2,1)} %get-tuple-element.67.refs_0_, bf16[768,1536]{1,0:T(8,128)(2,1)} %get-tuple-element.68.refs_1_, f32[768,384]{1,0:T(8,128)} %copy-done, f32[768,384]{1,0:T(8,128)} %copy-done.1, f32[768,384]{1,0:T(8,128)} %copy-done.2, ...), custom_call_target="tpu_custom_call" | custom-call | flops 768 | bytes 768 | tf_op jit(solution)/shard_map/total/next_product/pallas_call | solution.py:147
  129.3 5.9 %collective-permute-done.20 = f32[768,384]{1,0:T(8,128)} collective-permute-done((f32[768,384]{1,0:T(8,128)S(1)}, f32[768,384]{1,0:T(8,128)}, u32[]{:S(2)}, u32[]{:S(2)}) %collective-permute-start.20) | collective-permute-done | bytes 1179680 | tf_op jit(solution)/shard_map/product/ppermute | solution.py:30
  135.2 1.8 add_add_fusion
  137.0 0.8 fusion.2
  137.8 0.9 fusion.5
  139.0 0.6 collective-permute-start.21
  139.6 1.0 collective-permute-done.25
  140.7 3.2 %collective-permute-start.27 = (f32[128,640]{1,0:T(8,128)S(1)}, f32[128,640]{1,0:T(8,128)}, u32[]{:S(2)}, u32[]{:S(2)}) collective-permute-start(f32[128,640]{1,0:T(8,128)S(1)} %bitcast_add_fusion), channel_id=1, source_target_pairs={{0,96},{1,33},{32,0},{33,65},{64,32},{65,97},{96,64},{97,1},{2,98}... | collective-permute-start | bytes 983048 | tf_op jit(solution)/shard_map/quad/ppermute | solution.py:30
  143.9 7.8 %collective-permute-done.26 = f32[128,640]{1,0:T(8,128)} collective-permute-done((f32[128,640]{1,0:T(8,128)S(1)}, f32[128,640]{1,0:T(8,128)}, u32[]{:S(2)}, u32[]{:S(2)}) %collective-permute-start.26) | collective-permute-done | bytes 327712 | tf_op jit(solution)/shard_map/quad/ppermute | solution.py:30
  152.1 0.7 collective-permute-start.22
  153.2 7.2 %collective-permute-done.28 = f32[128,640]{1,0:T(8,128)} collective-permute-done((f32[128,640]{1,0:T(8,128)}, f32[128,640]{1,0:T(8,128)}, u32[]{:S(2)}, u32[]{:S(2)}) %collective-permute-start.28) | collective-permute-done | bytes 327712 | tf_op jit(solution)/shard_map/quad/ppermute | solution.py:30
  160.4 2.0 %add_add_fusion.1 = f32[128,640]{1,0:T(8,128)} fusion(f32[128,640]{1,0:T(8,128)} %collective-permute-done.28, f32[128,640]{1,0:T(8,128)} %collective-permute-done.27, f32[128,640]{1,0:T(8,128)S(1)} %bitcast_add_fusion, f32[128,640]{1,0:T(8,128)} %collective-permute-done.26), kind=kLoop, calls=%fused_computation.42 | loop fusion | flops 245760 | bytes 1638400 | tf_op jit(solution)/shard_map/quad/add | solution.py:321
  162.4 6.3 %collective-permute-done.23 = f32[384,384]{0,1:T(8,128)S(1)} collective-permute-done((f32[384,384]{0,1:T(8,128)S(1)}, f32[384,384]{0,1:T(8,128)S(1)}, u32[]{:S(2)}, u32[]{:S(2)}) %collective-permute-start.23) | collective-permute-done | bytes 589856 | tf_op jit(solution)/shard_map/out/ppermute | solution.py:310
  168.7 1.6 collective-permute-start.29
  170.3 2.7 %collective-permute-start.30 = (f32[128,640]{1,0:T(8,128)}, f32[128,640]{1,0:T(8,128)}, u32[]{:S(2)}, u32[]{:S(2)}) collective-permute-start(f32[128,640]{1,0:T(8,128)} %add_add_fusion.1), channel_id=1, source_target_pairs={{0,8},{1,0},{8,24},{9,16},{16,9},{17,1},{24,25},{25,17},{2,10},{3,... | collective-permute-start | bytes 983048 | tf_op jit(solution)/shard_map/quad/ppermute | solution.py:233
  173.0 3.0 %collective-permute-start.31 = (f32[128,640]{1,0:T(8,128)}, f32[128,640]{1,0:T(8,128)}, u32[]{:S(2)}, u32[]{:S(2)}) collective-permute-start(f32[128,640]{1,0:T(8,128)} %add_add_fusion.1), channel_id=1, source_target_pairs={{0,16},{1,24},{8,0},{9,8},{16,17},{17,25},{24,1},{25,9},{2,18},{3,... | collective-permute-start | bytes 983048 | tf_op jit(solution)/shard_map/quad/ppermute | solution.py:233
  176.0 1.9 collective-permute-start.32
  178.0 0.4 convolution_subtract_fusion.2
  178.4 0.4 convolution_subtract_fusion.1
  178.9 1.1 copy.34
  180.1 0.9 copy.33
  181.0 0.4 collective-permute-done.30
  181.5 8.0 %collective-permute-done.31 = f32[128,640]{1,0:T(8,128)} collective-permute-done((f32[128,640]{1,0:T(8,128)}, f32[128,640]{1,0:T(8,128)}, u32[]{:S(2)}, u32[]{:S(2)}) %collective-permute-start.31) | collective-permute-done | bytes 327712 | tf_op jit(solution)/shard_map/quad/ppermute | solution.py:233
  189.4 1.3 pad_maximum_fusion
  190.9 0.9 copy-done.21
  191.8 0.4 fusion.1
  192.2 0.6 convolution_bitcast_fusion.1
  192.9 0.6 copy-done.19
  193.5 1.4 fusion
  (96 shorter events, 3.4 us)
Async XLA Ops:
  0.6 3.2 %copy-start.20 = (f32[768,128]{1,0:T(8,128)S(1)}, f32[768,128]{1,0:T(8,128)}, u32[]{:S(2)}) copy-start(f32[768,128]{1,0:T(8,128)} %param.9) | copy-start | bytes 1179652
  0.6 3.4 %copy-start.18 = (f32[768,256]{1,0:T(8,128)S(1)}, f32[768,256]{1,0:T(8,128)}, u32[]{:S(2)}) copy-start(f32[768,256]{1,0:T(8,128)} %param.10) | copy-start | bytes 2359300
  2.9 2.3 %collective-permute-start = (f32[192,768]{1,0:T(8,128)}, f32[192,768]{1,0:T(8,128)}, u32[]{:S(2)}, u32[]{:S(2)}) collective-permute-start(f32[192,768]{1,0:T(8,128)} %get-tuple-element.98), channel_id=1, source_target_pairs={{0,1},{1,0},{2,3},{3,2},{4,5},{5,4},{6,7},{7,6},{8,9},{9,8},{10,11... | collective-permute-start | bytes 1769480 | tf_op jit(solution)/shard_map/gather/ppermute | solution.py:22
  4.3 8.1 %copy-start = (f32[768,384]{1,0:T(8,128)}, f32[768,384]{1,0:T(8,128)S(1)}, u32[]{:S(2)}) copy-start(f32[768,384]{1,0:T(8,128)S(1)} %pad_maximum_fusion.2.refs_4_.refs_2_) | copy-start | bytes 3538948
  5.2 2.8 %collective-permute-start.5 = (f32[768,384]{1,0:T(8,128)S(1)}, f32[768,384]{1,0:T(8,128)S(1)}, u32[]{:S(2)}, u32[]{:S(2)}) collective-permute-start(f32[768,384]{1,0:T(8,128)S(1)} %pad_maximum_fusion.2.refs_4_.refs_2_), channel_id=1, source_target_pairs={{0,1},{1,0},{2,3},{3,2},{4,5},{5,4},{6,7},{7,6},{8,9},{9,8},{10,11... | collective-permute-start | bytes 3538952 | tf_op jit(solution)/shard_map/gather/ppermute | solution.py:22
  6.5 9.6 %copy-start.10 = (f32[2,192,768]{2,1,0:T(8,128)}, f32[2,192,768]{2,1,0:T(8,128)S(1)}, u32[]{:S(2)}) copy-start(f32[2,192,768]{2,1,0:T(8,128)S(1)} %pad_maximum_fusion.1.refs_0_) | copy-start | bytes 3538948
  8.1 1.0 copy-start.1
  9.2 55.5 %copy-start.8 = (f32[4,192,384]{2,1,0:T(8,128)}, f32[4,192,384]{2,1,0:T(8,128)S(1)}, u32[]{:S(2)}) copy-start(f32[4,192,384]{2,1,0:T(8,128)S(1)} %pad_maximum_fusion.3) | copy-start | bytes 3538948
  9.2 17.6 %collective-permute-start.6 = (f32[768,384]{1,0:T(8,128)S(1)}, f32[768,384]{1,0:T(8,128)}, u32[]{:S(2)}, u32[]{:S(2)}) collective-permute-start(f32[768,384]{1,0:T(8,128)S(1)} %bitcast.95), channel_id=1, source_target_pairs={{0,2},{1,7},{2,4},{3,1},{4,6},{5,3},{6,0},{7,5},{8,10},{9,15},{10,... | collective-permute-start | bytes 3538952 | tf_op jit(solution)/shard_map/gather/ppermute | solution.py:30
  10.9 27.2 %collective-permute-start.3 = (f32[768,384]{1,0:T(8,128)S(1)}, f32[768,384]{1,0:T(8,128)S(1)}, u32[]{:S(2)}, u32[]{:S(2)}) collective-permute-start(f32[768,384]{1,0:T(8,128)S(1)} %pad_maximum_fusion.2.refs_4_.refs_2_), channel_id=1, source_target_pairs={{0,32},{1,97},{32,64},{33,1},{64,96},{65,33},{96,0},{97,65},{2,34}... | collective-permute-start | bytes 3538952 | tf_op jit(solution)/shard_map/gather/ppermute | solution.py:30
  12.4 28.0 %collective-permute-start.4 = (f32[768,384]{1,0:T(8,128)S(1)}, f32[768,384]{1,0:T(8,128)S(1)}, u32[]{:S(2)}, u32[]{:S(2)}) collective-permute-start(f32[768,384]{1,0:T(8,128)S(1)} %pad_maximum_fusion.2.refs_4_.refs_2_), channel_id=1, source_target_pairs={{0,96},{1,33},{32,0},{33,65},{64,32},{65,97},{96,64},{97,1},{2,98}... | collective-permute-start | bytes 3538952 | tf_op jit(solution)/shard_map/gather/ppermute | solution.py:30
  14.2 28.3 %collective-permute-start.1 = (f32[2,192,768]{2,1,0:T(8,128)S(1)}, f32[2,192,768]{2,1,0:T(8,128)S(1)}, u32[]{:S(2)}, u32[]{:S(2)}) collective-permute-start(f32[2,192,768]{2,1,0:T(8,128)S(1)} %pad_maximum_fusion.1.refs_0_), channel_id=1, source_target_pairs={{0,8},{1,25},{8,16},{9,1},{16,24},{17,9},{24,0},{25,17},{2,10},{3,... | collective-permute-start | bytes 3538952 | tf_op jit(solution)/shard_map/gather/ppermute | solution.py:30
  16.1 28.0 %collective-permute-start.2 = (f32[2,192,768]{2,1,0:T(8,128)S(1)}, f32[2,192,768]{2,1,0:T(8,128)S(1)}, u32[]{:S(2)}, u32[]{:S(2)}) collective-permute-start(f32[2,192,768]{2,1,0:T(8,128)S(1)} %pad_maximum_fusion.1.refs_0_), channel_id=1, source_target_pairs={{0,24},{1,9},{8,0},{9,17},{16,8},{17,25},{24,16},{25,1},{2,26},{3,... | collective-permute-start | bytes 3538952 | tf_op jit(solution)/shard_map/gather/ppermute | solution.py:30
  26.8 17.4 %collective-permute-start.7 = (f32[768,384]{1,0:T(8,128)S(1)}, f32[768,384]{1,0:T(8,128)}, u32[]{:S(2)}, u32[]{:S(2)}) collective-permute-start(f32[768,384]{1,0:T(8,128)S(1)} %bitcast.96), channel_id=1, source_target_pairs={{0,6},{1,3},{2,0},{3,5},{4,2},{5,7},{6,4},{7,1},{8,14},{9,11},{10,... | collective-permute-start | bytes 3538952 | tf_op jit(solution)/shard_map/gather/ppermute | solution.py:30
  38.1 35.9 %copy-start.2 = (f32[768,384]{1,0:T(8,128)}, f32[768,384]{1,0:T(8,128)S(1)}, u32[]{:S(2)}) copy-start(f32[768,384]{1,0:T(8,128)S(1)} %collective-permute-done.3.refs_6_.refs_4_) | copy-start | bytes 3538948
  40.4 33.7 %copy-start.3 = (f32[768,384]{1,0:T(8,128)}, f32[768,384]{1,0:T(8,128)S(1)}, u32[]{:S(2)}) copy-start(f32[768,384]{1,0:T(8,128)S(1)} %collective-permute-done.4.refs_8_.refs_6_) | copy-start | bytes 3538948
  42.4 28.6 %copy-start.14 = (f32[2,192,768]{2,1,0:T(8,128)}, f32[2,192,768]{2,1,0:T(8,128)S(1)}, u32[]{:S(2)}) copy-start(f32[2,192,768]{2,1,0:T(8,128)S(1)} %collective-permute-done.1.refs_1_) | copy-start | bytes 3538948
  44.1 2.5 %copy-start.15 = (f32[2,192,768]{2,1,0:T(8,128)}, f32[2,192,768]{2,1,0:T(8,128)S(1)}, u32[]{:S(2)}) copy-start(f32[2,192,768]{2,1,0:T(8,128)S(1)} %collective-permute-done.2.refs_2_) | copy-start | bytes 3538948
  44.2 17.7 %collective-permute-start.10 = (f32[768,384]{1,0:T(8,128)}, f32[768,384]{1,0:T(8,128)}, u32[]{:S(2)}, u32[]{:S(2)}) collective-permute-start(f32[768,384]{1,0:T(8,128)} %collective-permute-done.6), channel_id=1, source_target_pairs={{0,2},{1,7},{2,4},{3,1},{4,6},{5,3},{6,0},{7,5},{8,10},{9,15},{10,... | collective-permute-start | bytes 3538952 | tf_op jit(solution)/shard_map/gather/ppermute | solution.py:30
  46.7 15.2 %collective-permute-start.11 = (f32[768,384]{1,0:T(8,128)S(1)}, f32[768,384]{1,0:T(8,128)S(1)}, u32[]{:S(2)}, u32[]{:S(2)}) collective-permute-start(f32[768,384]{1,0:T(8,128)S(1)} %collective-permute-done.4.refs_8_.refs_6_), channel_id=1, source_target_pairs={{0,1},{1,0},{2,3},{3,2},{4,5},{5,4},{6,7},{7,6},{8,9},{9,8},{10,11... | collective-permute-start | bytes 3538952 | tf_op jit(solution)/shard_map/gather/ppermute | solution.py:22
  46.7 15.2 %collective-permute-start.12 = (f32[768,384]{1,0:T(8,128)S(1)}, f32[768,384]{1,0:T(8,128)S(1)}, u32[]{:S(2)}, u32[]{:S(2)}) collective-permute-start(f32[768,384]{1,0:T(8,128)S(1)} %collective-permute-done.3.refs_6_.refs_4_), channel_id=1, source_target_pairs={{0,1},{1,0},{2,3},{3,2},{4,5},{5,4},{6,7},{7,6},{8,9},{9,8},{10,11... | collective-permute-start | bytes 3538952 | tf_op jit(solution)/shard_map/gather/ppermute | solution.py:22
  47.2 17.4 %collective-permute-start.8 = (f32[2,192,768]{2,1,0:T(8,128)S(1)}, f32[2,192,768]{2,1,0:T(8,128)S(1)}, u32[]{:S(2)}, u32[]{:S(2)}) collective-permute-start(f32[2,192,768]{2,1,0:T(8,128)S(1)} %collective-permute-done.1.refs_1_), channel_id=1, source_target_pairs={{0,8},{1,25},{8,16},{9,1},{16,24},{17,9},{24,0},{25,17},{2,10},{3,... | collective-permute-start | bytes 3538952 | tf_op jit(solution)/shard_map/gather/ppermute | solution.py:30
  47.2 17.5 %collective-permute-start.9 = (f32[768,384]{1,0:T(8,128)S(1)}, f32[768,384]{1,0:T(8,128)}, u32[]{:S(2)}, u32[]{:S(2)}) collective-permute-start(f32[768,384]{1,0:T(8,128)S(1)} %collective-permute-done.3.refs_6_.refs_4_), channel_id=1, source_target_pairs={{0,32},{1,97},{32,64},{33,1},{64,96},{65,33},{96,0},{97,65},{2,34}... | collective-permute-start | bytes 3538952 | tf_op jit(solution)/shard_map/gather/ppermute | solution.py:30
  61.9 12.2 %copy-start.4 = (f32[768,384]{1,0:T(8,128)}, f32[768,384]{1,0:T(8,128)S(1)}, u32[]{:S(2)}) copy-start(f32[768,384]{1,0:T(8,128)S(1)} %collective-permute-done.11.refs_7_.refs_5_) | copy-start | bytes 3538948
  61.9 2.8 %copy-start.5 = (f32[768,384]{1,0:T(8,128)}, f32[768,384]{1,0:T(8,128)S(1)}, u32[]{:S(2)}) copy-start(f32[768,384]{1,0:T(8,128)S(1)} %collective-permute-done.12.refs_9_.refs_7_) | copy-start | bytes 3538948
  64.6 6.5 %copy-start.16 = (f32[2,192,768]{2,1,0:T(8,128)}, f32[2,192,768]{2,1,0:T(8,128)S(1)}, u32[]{:S(2)}) copy-start(f32[2,192,768]{2,1,0:T(8,128)S(1)} %collective-permute-done.8.refs_3_) | copy-start | bytes 3538948
  64.7 9.3 %collective-permute-start.13 = (f32[768,384]{1,0:T(8,128)}, f32[768,384]{1,0:T(8,128)}, u32[]{:S(2)}, u32[]{:S(2)}) collective-permute-start(f32[768,384]{1,0:T(8,128)} %collective-permute-done.9.refs_10_.refs_8_), channel_id=1, source_target_pairs={{0,1},{1,0},{2,3},{3,2},{4,5},{5,4},{6,7},{7,6},{8,9},{9,8},{10,11... | collective-permute-start | bytes 3538952 | tf_op jit(solution)/shard_map/gather/ppermute | solution.py:22
  64.7 31.3 %collective-permute-start.18 = (f32[768,384]{1,0:T(8,128)}, f32[768,384]{1,0:T(8,128)}, u32[]{:S(2)}, u32[]{:S(2)}) collective-permute-start(f32[768,384]{1,0:T(8,128)} %collective-permute-done.6), channel_id=1, source_target_pairs={{0,96},{1,33},{34,2},{35,67},{68,36},{69,101},{102,70},{103,7},{8,... | collective-permute-start | bytes 3538952 | tf_op jit(solution)/shard_map/product/ppermute | solution.py:253
  71.1 26.3 %collective-permute-start.16 = (f32[768,384]{1,0:T(8,128)}, f32[768,384]{1,0:T(8,128)}, u32[]{:S(2)}, u32[]{:S(2)}) collective-permute-start(f32[768,384]{1,0:T(8,128)} %collective-permute-done.10), channel_id=1, source_target_pairs={{0,32},{1,97},{34,66},{35,3},{68,100},{69,37},{102,6},{103,71},{8,... | collective-permute-start | bytes 3538952 | tf_op jit(solution)/shard_map/product/ppermute | solution.py:253
  83.3 23.5 %collective-permute-start.14 = (f32[768,384]{1,0:T(8,128)}, f32[768,384]{1,0:T(8,128)S(1)}, u32[]{:S(2)}, u32[]{:S(2)}) collective-permute-start(f32[768,384]{1,0:T(8,128)} %get-tuple-element.55), channel_id=1, source_target_pairs={{0,2},{1,7},{2,4},{3,1},{4,6},{5,3},{6,0},{7,5},{8,10},{9,15},{10,... | collective-permute-start | bytes 3538952 | tf_op jit(solution)/shard_map/product/ppermute | solution.py:30
  91.9 23.8 %collective-permute-start.15 = (f32[768,384]{1,0:T(8,128)}, f32[768,384]{1,0:T(8,128)}, u32[]{:S(2)}, u32[]{:S(2)}) collective-permute-start(f32[768,384]{1,0:T(8,128)} %next_product.3), channel_id=1, source_target_pairs={{0,6},{1,3},{2,0},{3,5},{4,2},{5,7},{6,4},{7,1},{8,14},{9,11},{10,... | collective-permute-start | bytes 3538952 | tf_op jit(solution)/shard_map/product/ppermute | solution.py:30
  96.0 21.7 %collective-permute-start.19 = (f32[768,384]{1,0:T(8,128)}, f32[768,384]{1,0:T(8,128)S(1)}, u32[]{:S(2)}, u32[]{:S(2)}) collective-permute-start(f32[768,384]{1,0:T(8,128)} %collective-permute-done.7), channel_id=1, source_target_pairs={{0,32},{1,97},{34,66},{35,3},{68,100},{69,37},{102,6},{103,71},{8,... | collective-permute-start | bytes 3538952 | tf_op jit(solution)/shard_map/product/ppermute | solution.py:253
  97.3 21.4 %collective-permute-start.17 = (f32[768,384]{1,0:T(8,128)}, f32[768,384]{1,0:T(8,128)}, u32[]{:S(2)}, u32[]{:S(2)}) collective-permute-start(f32[768,384]{1,0:T(8,128)} %collective-permute-done.16), channel_id=1, source_target_pairs={{32,64},{97,65},{66,98},{3,99},{100,4},{37,5},{6,38},{71,39},{40,7... | collective-permute-start | bytes 3538952 | tf_op jit(solution)/shard_map/product/ppermute | solution.py:253
  106.7 9.0 %copy-start.13 = (f32[768,384]{1,0:T(8,128)}, f32[768,384]{1,0:T(8,128)S(1)}, u32[]{:S(2)}) copy-start(f32[768,384]{1,0:T(8,128)S(1)} %collective-permute-done.14) | copy-start | bytes 3538948
  115.7 3.0 %copy-start.9 = (f32[4,192,384]{2,1,0:T(8,128)S(1)}, f32[4,192,384]{2,1,0:T(8,128)}, u32[]{:S(2)}) copy-start(f32[4,192,384]{2,1,0:T(8,128)} %copy-done.8) | copy-start | bytes 3538948
  117.6 17.6 %collective-permute-start.20 = (f32[768,384]{1,0:T(8,128)S(1)}, f32[768,384]{1,0:T(8,128)}, u32[]{:S(2)}, u32[]{:S(2)}) collective-permute-start(f32[768,384]{1,0:T(8,128)S(1)} %add.170), channel_id=1, source_target_pairs={{0,2},{1,7},{2,4},{3,1},{4,6},{5,3},{6,0},{7,5},{8,10},{9,15},{10,... | collective-permute-start | bytes 3538952 | tf_op jit(solution)/shard_map/product/ppermute | solution.py:30
  117.7 1.0 copy-start.12
  120.3 9.0 %collective-permute-start.24 = (f32[768,128]{1,0:T(8,128)S(1)}, f32[768,128]{1,0:T(8,128)S(1)}, u32[]{:S(2)}, u32[]{:S(2)}) collective-permute-start(f32[768,128]{1,0:T(8,128)S(1)} %slice.62), channel_id=1, source_target_pairs={{0,8},{8,0},{16,24},{24,16},{1,9},{9,1},{17,25},{25,17},{2,10},{10... | collective-permute-start | bytes 1179656 | tf_op jit(solution)/shard_map/turned/ppermute | solution.py:287
  129.2 6.0 %copy-start.7 = (f32[768,384]{1,0:T(8,128)S(1)}, f32[768,384]{1,0:T(8,128)}, u32[]{:S(2)}) copy-start(f32[768,384]{1,0:T(8,128)} %next_product.5) | copy-start | bytes 3538948
  138.8 1.7 collective-permute-start.25
  139.0 4.9 %collective-permute-start.21 = (f32[384,384]{1,0:T(8,128)S(1)}, f32[384,384]{1,0:T(8,128)S(1)}, u32[]{:S(2)}, u32[]{:S(2)}) collective-permute-start(f32[384,384]{1,0:T(8,128)S(1)} %get-tuple-element.95), channel_id=1, source_target_pairs={{0,1},{1,0},{2,3},{3,2},{4,5},{5,4},{6,7},{7,6},{8,9},{9,8},{10,11... | collective-permute-start | bytes 1769480 | tf_op jit(solution)/shard_map/out/ppermute | solution.py:22
  140.5 11.2 %collective-permute-start.26 = (f32[128,640]{1,0:T(8,128)S(1)}, f32[128,640]{1,0:T(8,128)}, u32[]{:S(2)}, u32[]{:S(2)}) collective-permute-start(f32[128,640]{1,0:T(8,128)S(1)} %bitcast_add_fusion), channel_id=1, source_target_pairs={{0,32},{1,97},{32,64},{33,1},{64,96},{65,33},{96,0},{97,65},{2,34}... | collective-permute-start | bytes 983048 | tf_op jit(solution)/shard_map/quad/ppermute | solution.py:30
  140.7 12.5 %collective-permute-start.27 = (f32[128,640]{1,0:T(8,128)S(1)}, f32[128,640]{1,0:T(8,128)}, u32[]{:S(2)}, u32[]{:S(2)}) collective-permute-start(f32[128,640]{1,0:T(8,128)S(1)} %bitcast_add_fusion), channel_id=1, source_target_pairs={{0,96},{1,33},{32,0},{33,65},{64,32},{65,97},{96,64},{97,1},{2,98}... | collective-permute-start | bytes 983048 | tf_op jit(solution)/shard_map/quad/ppermute | solution.py:30
  151.8 8.6 %collective-permute-start.28 = (f32[128,640]{1,0:T(8,128)}, f32[128,640]{1,0:T(8,128)}, u32[]{:S(2)}, u32[]{:S(2)}) collective-permute-start(f32[128,640]{1,0:T(8,128)} %collective-permute-done.26), channel_id=1, source_target_pairs={{0,32},{1,97},{32,64},{33,1},{64,96},{65,33},{96,0},{97,65},{2,34}... | collective-permute-start | bytes 983048 | tf_op jit(solution)/shard_map/quad/ppermute | solution.py:30
  152.1 10.2 %collective-permute-start.22 = (f32[384,384]{0,1:T(8,128)S(1)}, f32[384,384]{0,1:T(8,128)S(1)}, u32[]{:S(2)}, u32[]{:S(2)}) collective-permute-start(f32[384,384]{0,1:T(8,128)S(1)} %bitcast.103), channel_id=1, source_target_pairs={{0,0},{1,16},{8,8},{9,24},{16,1},{17,17},{24,9},{25,25},{2,2},{3,1... | collective-permute-start | bytes 1769480 | tf_op jit(solution)/shard_map/out/ppermute | solution.py:310
  153.0 15.6 %collective-permute-start.23 = (f32[384,384]{0,1:T(8,128)S(1)}, f32[384,384]{0,1:T(8,128)S(1)}, u32[]{:S(2)}, u32[]{:S(2)}) collective-permute-start(f32[384,384]{0,1:T(8,128)S(1)} %bitcast.104), channel_id=1, source_target_pairs={{0,8},{1,24},{8,0},{9,16},{16,9},{17,25},{24,1},{25,17},{2,10},{3,... | collective-permute-start | bytes 1769480 | tf_op jit(solution)/shard_map/out/ppermute | solution.py:310
  162.3 15.7 %copy-start.6 = (f32[2,256,256]{2,1,0:T(8,128)S(1)}, f32[2,256,256]{2,1,0:T(8,128)}, u32[]{:S(2)}) copy-start(f32[2,256,256]{2,1,0:T(8,128)} %param.11) | copy-start | bytes 1572868
  168.7 12.4 %collective-permute-start.29 = (f32[128,640]{1,0:T(8,128)}, f32[128,640]{1,0:T(8,128)S(1)}, u32[]{:S(2)}, u32[]{:S(2)}) collective-permute-start(f32[128,640]{1,0:T(8,128)} %add_add_fusion.1), channel_id=1, source_target_pairs={{0,0},{1,8},{8,16},{9,24},{16,1},{17,9},{24,17},{25,25},{2,2},{3,1... | collective-permute-start | bytes 983048 | tf_op jit(solution)/shard_map/quad/ppermute | solution.py:233
  170.3 11.2 %collective-permute-start.30 = (f32[128,640]{1,0:T(8,128)}, f32[128,640]{1,0:T(8,128)}, u32[]{:S(2)}, u32[]{:S(2)}) collective-permute-start(f32[128,640]{1,0:T(8,128)} %add_add_fusion.1), channel_id=1, source_target_pairs={{0,8},{1,0},{8,24},{9,16},{16,9},{17,1},{24,25},{25,17},{2,10},{3,... | collective-permute-start | bytes 983048 | tf_op jit(solution)/shard_map/quad/ppermute | solution.py:233
  173.0 16.4 %collective-permute-start.31 = (f32[128,640]{1,0:T(8,128)}, f32[128,640]{1,0:T(8,128)}, u32[]{:S(2)}, u32[]{:S(2)}) collective-permute-start(f32[128,640]{1,0:T(8,128)} %add_add_fusion.1), channel_id=1, source_target_pairs={{0,16},{1,24},{8,0},{9,8},{16,17},{17,25},{24,1},{25,9},{2,18},{3,... | collective-permute-start | bytes 983048 | tf_op jit(solution)/shard_map/quad/ppermute | solution.py:233
  176.0 13.5 %collective-permute-start.32 = (f32[128,640]{1,0:T(8,128)}, f32[128,640]{1,0:T(8,128)}, u32[]{:S(2)}, u32[]{:S(2)}) collective-permute-start(f32[128,640]{1,0:T(8,128)} %add_add_fusion.1), channel_id=1, source_target_pairs={{0,24},{1,16},{8,8},{9,0},{16,25},{17,17},{24,9},{25,1},{2,26},{3,... | collective-permute-start | bytes 983048 | tf_op jit(solution)/shard_map/quad/ppermute | solution.py:233
  190.8 1.0 copy-start.21
  191.8 1.1 copy-start.17
  192.2 2.7 %copy-start.11 = (f32[2,256,256]{2,1,0:T(8,128)}, f32[2,256,256]{2,1,0:T(8,128)S(1)}, u32[]{:S(2)}) copy-start(f32[2,256,256]{2,1,0:T(8,128)S(1)} %fusion.1) | copy-start | bytes 1572868
  192.2 1.2 copy-start.19
where the time goes:
time: 198 us; the launch traced here: 195 us
  waiting for transfers between devices  88.9 us (45%)
  starting transfers between devices  43.7 us (22%)
  Pallas kernels  35.3 us (18%)
  other arithmetic  11.4 us (6%)
  local copies, waits for them, and re-layouts  9.24 us (5%)
  matrix products  5.01 us (3%)
    ppermute x15, waiting for transfers between devices, send(): return lax.ppermute(value, (axis, 'core'), split_pairs(step))  69.9 us
    pallas_call x4, Pallas kernels, product(): pl.pallas_call(first_kernel if first else next_kernel, out_shape=[parts,...  35.3 us
    ppermute x15, starting transfers between devices, send(): return lax.ppermute(value, (axis, 'core'), split_pairs(step))  20.4 us
    ppermute x4, starting transfers between devices, turn(): return lax.ppermute(value, ('x', 'y', 'core'), pairs)  11.7 us
    ppermute x4, starting transfers between devices, spread(): lax.ppermute(value, ('z', 'core'), [((2 * c + j) * 2 + h, (2 * j + h ^ tu...  9.2 us
    ppermute x4, waiting for transfers between devices, spread(): lax.ppermute(value, ('z', 'core'), [((2 * c + j) * 2 + h, (2 * j + h ^ tu...  8.42 us
    ppermute x2, waiting for transfers between devices, local(): lax.ppermute(pick(blocks, (z + turn_over) % 2), ('z', 'core'), pairs)  6.31 us
    unnamed x46, local copies, waits for them, and re-layouts  5.46 us
  transfers between devices with their start and end apart: 33, of which 19 were waited for; matrix products, arithmetic and copies ran while one was open for 6% of the time, Pallas kernels for 18%

commit v1 on v0

--- a/solution.py
+++ b/solution.py
@@ -61,9 +61,10 @@
     return [pltpu.make_async_copy(refs[p], to.at[p], sems.at[p]) for p in range(2)]
 
 
-def multiply(out, row_high, row_low, strip, strip_high, strip_low):
+def split_strip(strip, strip_high, strip_low, copies):
     deep, chunk = strip.shape[1], 64
     for p in range(2):
+        copies[p].wait()
 
         @pl.loop(0, deep // chunk)
         def _(i, p=p):
@@ -72,6 +73,8 @@
             strip_high[at, :] = high
             strip_low[at, :] = low
 
+
+def multiply(out, row_high, row_low, strip_high, strip_low):
     dot = functools.partial(jnp.dot, preferred_element_type=jnp.float32)
     tall = out.shape[0] // 2
 
@@ -86,8 +89,9 @@
     rows, strips = refs[:4], refs[4:12]
     out_high, out_low, out = refs[12:15]
     row, row_high, row_low, strip, strip_high, strip_low, row_sems, sems = refs[15:]
+    strip_copies = take(strips, strip, sems, places[4])
     row_copies = take(rows, row, row_sems)
-    strip_copies = take(strips, strip, sems, places[4])
+    split_strip(strip, strip_high, strip_low, strip_copies)
     half, deep = rows[0].shape[1:]
     chunk = 64
     for k, copy in enumerate(row_copies):
@@ -108,9 +112,7 @@
     ]
     for copy in outs:
         copy.start()
-    for copy in strip_copies:
-        copy.wait()
-    multiply(out, row_high, row_low, strip, strip_high, strip_low)
+    multiply(out, row_high, row_low, strip_high, strip_low)
     for copy in outs:
         copy.wait()
 
@@ -125,14 +127,13 @@
     strip_copies = take(strips, strip, sems, places[0])
     for copy in row_copies:
         copy.start()
-    for copy in strip_copies:
-        copy.wait()
+    split_strip(strip, strip_high, strip_low, strip_copies)
     for copy in row_copies:
         copy.wait()
-    multiply(out, row_high, row_low, strip, strip_high, strip_low)
-
-
-def product(places, rows, strips):
+    multiply(out, row_high, row_low, strip_high, strip_low)
+
+
+def product(places, rows, strips, counted=False):
     vmem, hbm = (pl.BlockSpec(memory_space=m) for m in (pltpu.VMEM, pltpu.HBM))
     deep, wide = strips[0].shape
     first = len(rows) == 4
@@ -153,7 +154,7 @@
         + [pltpu.SemaphoreType.DMA((4 if first else 2,)), pltpu.SemaphoreType.DMA((2,))],
         compiler_params=pltpu.CompilerParams(vmem_limit_bytes=56 * 2**20),
         cost_estimate=pl.CostEstimate(
-            flops=tall, bytes_accessed=tall, transcendentals=0
+            flops=8 * 10**9 if counted else tall, bytes_accessed=tall, transcendentals=0
         ),
         name="first_product" if first else "next_product",
     )(jnp.stack(places).astype(jnp.int32), *rows, *strips)
@@ -270,9 +271,9 @@
         near = product([strip_of(side)], [after(p, far) for p in parts], strips)
         near_came = send(near, "y", -1)
         q_far = turn(after(q_step, near), 1, 1)
-        q_second = turn(after(t_second, q_first, near), 1)
-        last = product([strip_of(-side)], [after(p, near, far_came) for p in parts], strips)
-        last = after(last, near_came) + far_came
+        q_second = turn(after(t_second, near), 1)
+        last = product([strip_of(-side)], [after(p, near) for p in parts], strips)
+        last = last + far_came
         last_came = send(last, "y", 1)
     with jax.named_scope("turned"):
         shift = (x - y) % 4
@@ -289,7 +290,7 @@
             (jnp.where(z % 2 == 0, own, mate), jnp.where(z % 2 == 0, mate, own)), axis=1
         )
     with jax.named_scope("total"):
-        rest = product([strip_of(0)], [after(p, last, turned) for p in parts], strips)
+        rest = product([strip_of(0)], [after(p, last, turned, near_came) for p in parts], strips, True)
         rest, near_came, last_came = lax.optimization_barrier((rest, near_came, last_came))
         total = rest + near_came + last_came
     with jax.named_scope("out"):
@@ -318,8 +319,8 @@
         quad = quad.reshape(2, BLOCK // 2, wide)
         quad = pick(quad, core) + swap(pick(quad, 1 - core))
         first, second = send(quad, "x", 1), send(quad, "x", -1)
-        around = quad + first + second + send(first, "x", 1)
-        around = after(around, *pieces)
+        around = quad + first + second + send(after(first, pieces[1]), "x", 1)
+        around = after(around, pieces[0])
         came = jnp.stack(spread([around] * 4))
         sums = [
             jnp.concatenate([pick(came, (2 * j + h) ^ z) for h in range(2)], axis=0)

time: 198 us -> 183 us (0.924)
  waiting for transfers between devices: 88.9 us -> 75.6 us
  other arithmetic: 11.4 us -> 7.28 us
  starting transfers between devices: 43.7 us -> 46.2 us
    ppermute x15, waiting for transfers between devices: 69.9 us -> 60.9 us  [send(): return lax.ppermute(value, (axis, 'core'), split_pairs(step))]
    ppermute x2, waiting for transfers between devices: 6.31 us -> 2.43 us  [local(): lax.ppermute(pick(blocks, (z + turn_over) % 2), ('z', 'core'), pairs)]
    unnamed x46 -> x42, local copies, waits for them, and re-layouts: 5.46 us -> 6.49 us
  transfers between devices with their start and end apart: 33 -> 33, of which waited for: 19 -> 16; matrix products, arithmetic and copies ran while one was open for 6% -> 6% of each run, Pallas kernels for 18% -> 19%
where the time goes in v1:
time: 183 us; the launch traced here: 180 us
  waiting for transfers between devices  75.6 us (41%)
  starting transfers between devices  46.2 us (25%)
  Pallas kernels  33.8 us (18%)
  local copies, waits for them, and re-layouts  11 us (6%)
  other arithmetic  7.28 us (4%)
  matrix products  5.03 us (3%)
    ppermute x15, waiting for transfers between devices, send(): return lax.ppermute(value, (axis, 'core'), split_pairs(step))  60.9 us
    pallas_call x4, Pallas kernels, product(): pl.pallas_call(first_kernel if first else next_kernel, out_shape=[parts,...  33.8 us
    ppermute x15, starting transfers between devices, send(): return lax.ppermute(value, (axis, 'core'), split_pairs(step))  21.4 us
    ppermute x4, starting transfers between devices, turn(): return lax.ppermute(value, ('x', 'y', 'core'), pairs)  10.7 us
    ppermute x4, starting transfers between devices, spread(): lax.ppermute(value, ('z', 'core'), [((2 * c + j) * 2 + h, (2 * j + h ^ tu...  10.1 us
    ppermute x4, waiting for transfers between devices, spread(): lax.ppermute(value, ('z', 'core'), [((2 * c + j) * 2 + h, (2 * j + h ^ tu...  8.88 us
    unnamed x42, local copies, waits for them, and re-layouts  6.49 us
  transfers between devices with their start and end apart: 33, of which 16 were waited for; matrix products, arithmetic and copies ran while one was open for 6% of the time, Pallas kernels for 19%

profile of v1, /device:TPU:0, one launch (start us, length us, event | category | flops | bytes accessed | tf_op | source)
XLA Modules:
  0.0 180.2 jit_solution(17280684502575432300)
XLA Ops:
  0.7 2.2 %constant_dynamic-slice_fusion.1 = (f32[1,192,768]{2,1,0:T(8,128)S(1)}, f32[192,768]{1,0:T(8,128)}) fusion(f32[2,192,768]{2,1,0:T(8,128)} %bitcast.101, s32[]{:T(128)S(6)} %select_n.251, s32[]{:T(128)S(6)} %select_n.252), kind=kLoop, calls=%fused_computation.70 | loop fusion | bytes 2359304 | tf_op jit(solution)/shard_map/gather/jit(dynamic_index_in_dim)/dynamic_slice | solution.py:38
  2.9 0.8 convert_bitcast_fusion.1
  4.3 0.8 collective-permute-done
  5.3 2.6 %collective-permute-done.5.refs_5_.refs_3_ = f32[768,384]{1,0:T(8,128)S(1)} collective-permute-done((f32[768,384]{1,0:T(8,128)S(1)}, f32[768,384]{1,0:T(8,128)S(1)}, u32[]{:S(2)}, u32[]{:S(2)}) %collective-permute-start.5) | collective-permute-done | bytes 1179680 | tf_op jit(solution)/shard_map/gather/ppermute | solution.py:22
  8.1 0.9 copy-done.1
  9.1 1.7 collective-permute-start.6
  10.8 1.5 collective-permute-start.3
  12.3 1.7 collective-permute-start.4
  14.0 1.9 %collective-permute-start.1 = (f32[2,192,768]{2,1,0:T(8,128)S(1)}, f32[2,192,768]{2,1,0:T(8,128)S(1)}, u32[]{:S(2)}, u32[]{:S(2)}) collective-permute-start(f32[2,192,768]{2,1,0:T(8,128)S(1)} %pad_maximum_fusion.1.refs_0_), channel_id=1, source_target_pairs={{0,8},{1,25},{8,16},{9,1},{16,24},{17,9},{24,0},{25,17},{2,10},{3,... | collective-permute-start | bytes 3538952 | tf_op jit(solution)/shard_map/gather/ppermute | solution.py:30
  16.0 2.1 %collective-permute-start.2 = (f32[2,192,768]{2,1,0:T(8,128)S(1)}, f32[2,192,768]{2,1,0:T(8,128)S(1)}, u32[]{:S(2)}, u32[]{:S(2)}) collective-permute-start(f32[2,192,768]{2,1,0:T(8,128)S(1)} %pad_maximum_fusion.1.refs_0_), channel_id=1, source_target_pairs={{0,24},{1,9},{8,0},{9,17},{16,8},{17,25},{24,16},{25,1},{2,26},{3,... | collective-permute-start | bytes 3538952 | tf_op jit(solution)/shard_map/gather/ppermute | solution.py:30
  18.1 8.6 %collective-permute-done.6 = f32[768,384]{1,0:T(8,128)} collective-permute-done((f32[768,384]{1,0:T(8,128)S(1)}, f32[768,384]{1,0:T(8,128)}, u32[]{:S(2)}, u32[]{:S(2)}) %collective-permute-start.6) | collective-permute-done | bytes 1179680 | tf_op jit(solution)/shard_map/gather/ppermute | solution.py:30
  26.7 1.9 %collective-permute-start.7 = (f32[768,384]{1,0:T(8,128)S(1)}, f32[768,384]{1,0:T(8,128)}, u32[]{:S(2)}, u32[]{:S(2)}) collective-permute-start(f32[768,384]{1,0:T(8,128)S(1)} %bitcast.96), channel_id=1, source_target_pairs={{0,6},{1,3},{2,0},{3,5},{4,2},{5,7},{6,4},{7,1},{8,14},{9,11},{10,... | collective-permute-start | bytes 3538952 | tf_op jit(solution)/shard_map/gather/ppermute | solution.py:30
  28.5 9.4 %collective-permute-done.3.refs_6_.refs_4_ = f32[768,384]{1,0:T(8,128)S(1)} collective-permute-done((f32[768,384]{1,0:T(8,128)S(1)}, f32[768,384]{1,0:T(8,128)S(1)}, u32[]{:S(2)}, u32[]{:S(2)}) %collective-permute-start.3) | collective-permute-done | bytes 1179680 | tf_op jit(solution)/shard_map/gather/ppermute | solution.py:30
  38.0 2.3 %collective-permute-done.4.refs_8_.refs_6_ = f32[768,384]{1,0:T(8,128)S(1)} collective-permute-done((f32[768,384]{1,0:T(8,128)S(1)}, f32[768,384]{1,0:T(8,128)S(1)}, u32[]{:S(2)}, u32[]{:S(2)}) %collective-permute-start.4) | collective-permute-done | bytes 1179680 | tf_op jit(solution)/shard_map/gather/ppermute | solution.py:30
  40.2 2.1 %collective-permute-done.1.refs_1_ = f32[2,192,768]{2,1,0:T(8,128)S(1)} collective-permute-done((f32[2,192,768]{2,1,0:T(8,128)S(1)}, f32[2,192,768]{2,1,0:T(8,128)S(1)}, u32[]{:S(2)}, u32[]{:S(2)}) %collective-permute-start.1) | collective-permute-done | bytes 1179680 | tf_op jit(solution)/shard_map/gather/ppermute | solution.py:30
  42.3 1.7 collective-permute-done.2.refs_2_
  44.0 2.5 %collective-permute-start.10 = (f32[768,384]{1,0:T(8,128)}, f32[768,384]{1,0:T(8,128)}, u32[]{:S(2)}, u32[]{:S(2)}) collective-permute-start(f32[768,384]{1,0:T(8,128)} %collective-permute-done.6), channel_id=1, source_target_pairs={{0,2},{1,7},{2,4},{3,1},{4,6},{5,3},{6,0},{7,5},{8,10},{9,15},{10,... | collective-permute-start | bytes 3538952 | tf_op jit(solution)/shard_map/gather/ppermute | solution.py:30
  46.5 0.5 collective-permute-start.12
  47.3 14.4 %collective-permute-done.10 = f32[768,384]{1,0:T(8,128)} collective-permute-done((f32[768,384]{1,0:T(8,128)}, f32[768,384]{1,0:T(8,128)}, u32[]{:S(2)}, u32[]{:S(2)}) %collective-permute-start.10) | collective-permute-done | bytes 1179680 | tf_op jit(solution)/shard_map/gather/ppermute | solution.py:30
  61.8 2.7 %collective-permute-done.8.refs_3_ = f32[2,192,768]{2,1,0:T(8,128)S(1)} collective-permute-done((f32[2,192,768]{2,1,0:T(8,128)S(1)}, f32[2,192,768]{2,1,0:T(8,128)S(1)}, u32[]{:S(2)}, u32[]{:S(2)}) %collective-permute-start.8) | collective-permute-done | bytes 1179680 | tf_op jit(solution)/shard_map/gather/ppermute | solution.py:30
  64.6 0.9 copy-done.13
  65.4 3.1 %collective-permute-start.15 = (f32[768,384]{1,0:T(8,128)}, f32[768,384]{1,0:T(8,128)}, u32[]{:S(2)}, u32[]{:S(2)}) collective-permute-start(f32[768,384]{1,0:T(8,128)} %collective-permute-done.10), channel_id=1, source_target_pairs={{0,32},{1,97},{34,66},{35,3},{68,100},{69,37},{102,6},{103,71},{8,... | collective-permute-start | bytes 3538952 | tf_op jit(solution)/shard_map/product/ppermute | solution.py:254
  68.5 0.7 stack.73.places
  69.2 4.1 %collective-permute-start.17 = (f32[768,384]{1,0:T(8,128)}, f32[768,384]{1,0:T(8,128)}, u32[]{:S(2)}, u32[]{:S(2)}) collective-permute-start(f32[768,384]{1,0:T(8,128)} %collective-permute-done.6), channel_id=1, source_target_pairs={{0,96},{1,33},{34,2},{35,67},{68,36},{69,101},{102,70},{103,7},{8,... | collective-permute-start | bytes 3538952 | tf_op jit(solution)/shard_map/product/ppermute | solution.py:254
  73.3 9.4 %first_product.1 = (bf16[768,1536]{1,0:T(8,128)(2,1)}, bf16[768,1536]{1,0:T(8,128)(2,1)}, f32[768,384]{1,0:T(8,128)}) custom-call(s32[5]{0:T(128)} %stack.73.places, f32[2,192,768]{2,1,0:T(8,128)} %copy-done.9, f32[2,192,768]{2,1,0:T(8,128)} %copy-done.11, f32[2,192,768]{2,1,0:T(8,128)} %copy-done.12, f32[2,192,768]{2,1,0:T(8,128)} %copy-done.13, ...), custom_call_target="tpu_custom_call" | custom-call | flops 768 | bytes 768 | tf_op jit(solution)/shard_map/product/first_product/pallas_call | solution.py:148
  82.8 8.1 %next_product.3 = f32[768,384]{1,0:T(8,128)} custom-call(s32[1]{0:T(128)} %bitcast.20.places, bf16[768,1536]{1,0:T(8,128)(2,1)} %get-tuple-element.66.refs_0_, bf16[768,1536]{1,0:T(8,128)(2,1)} %get-tuple-element.67.refs_1_, f32[768,384]{1,0:T(8,128)} %copy-done, f32[768,384]{1,0:T(8,128)} %copy-done.1, f32[768,384]{1,0:T(8,128)} %copy-done.2, ...), custom_call_target="tpu_custom_call" | custom-call | flops 768 | bytes 768 | tf_op jit(solution)/shard_map/product/next_product/pallas_call | solution.py:148
  90.9 2.8 %collective-permute-start.18 = (f32[768,384]{1,0:T(8,128)}, f32[768,384]{1,0:T(8,128)S(1)}, u32[]{:S(2)}, u32[]{:S(2)}) collective-permute-start(f32[768,384]{1,0:T(8,128)} %collective-permute-done.7), channel_id=1, source_target_pairs={{0,32},{1,97},{34,66},{35,3},{68,100},{69,37},{102,6},{103,71},{8,... | collective-permute-start | bytes 3538952 | tf_op jit(solution)/shard_map/product/ppermute | solution.py:254
  93.7 0.7 collective-permute-start.16
  94.5 4.3 %collective-permute-start.19 = (f32[768,384]{1,0:T(8,128)}, f32[768,384]{1,0:T(8,128)}, u32[]{:S(2)}, u32[]{:S(2)}) collective-permute-start(f32[768,384]{1,0:T(8,128)} %next_product.3), channel_id=1, source_target_pairs={{0,6},{1,3},{2,0},{3,5},{4,2},{5,7},{6,4},{7,1},{8,14},{9,11},{10,... | collective-permute-start | bytes 3538952 | tf_op jit(solution)/shard_map/product/ppermute | solution.py:30
  98.7 8.1 %next_product.4 = f32[768,384]{1,0:T(8,128)} custom-call(s32[1]{0:T(128)} %bitcast.19.places, bf16[768,1536]{1,0:T(8,128)(2,1)} %get-tuple-element.66.refs_0_, bf16[768,1536]{1,0:T(8,128)(2,1)} %get-tuple-element.67.refs_1_, f32[768,384]{1,0:T(8,128)} %copy-done, f32[768,384]{1,0:T(8,128)} %copy-done.1, f32[768,384]{1,0:T(8,128)} %copy-done.2, ...), custom_call_target="tpu_custom_call" | custom-call | flops 768 | bytes 768 | tf_op jit(solution)/shard_map/product/next_product/pallas_call | solution.py:148
  106.9 1.5 add.170
  108.5 0.4 select_select_fusion
  108.9 1.5 collective-permute-start.24
  110.4 7.3 %collective-permute-done.19 = f32[768,384]{1,0:T(8,128)} collective-permute-done((f32[768,384]{1,0:T(8,128)}, f32[768,384]{1,0:T(8,128)}, u32[]{:S(2)}, u32[]{:S(2)}) %collective-permute-start.19) | collective-permute-done | bytes 1179680 | tf_op jit(solution)/shard_map/product/ppermute | solution.py:30
  117.7 8.1 %next_product.5 = f32[768,384]{1,0:T(8,128)} custom-call(s32[1]{0:T(128)} %bitcast.places, bf16[768,1536]{1,0:T(8,128)(2,1)} %get-tuple-element.66.refs_0_, bf16[768,1536]{1,0:T(8,128)(2,1)} %get-tuple-element.67.refs_1_, f32[768,384]{1,0:T(8,128)} %copy-done, f32[768,384]{1,0:T(8,128)} %copy-done.1, f32[768,384]{1,0:T(8,128)} %copy-done.2, ...), custom_call_target="tpu_custom_call" | custom-call | flops 8000000000 | bytes 768 | tf_op jit(solution)/shard_map/total/next_product/pallas_call | solution.py:148
  125.9 1.2 copy-done.14
  127.1 1.4 add_add_fusion
  128.7 0.9 fusion.5
  129.6 0.8 fusion.2
  130.5 0.8 dynamic-slice_bitcast_fusion.6
  131.2 0.5 collective-permute-start.25
  132.1 0.6 collective-permute-start.23
  133.0 0.7 collective-permute-start.22
  133.9 3.2 %collective-permute-start.27 = (f32[128,640]{1,0:T(8,128)S(1)}, f32[128,640]{1,0:T(8,128)S(1)}, u32[]{:S(2)}, u32[]{:S(2)}) collective-permute-start(f32[128,640]{1,0:T(8,128)S(1)} %bitcast_add_fusion), channel_id=1, source_target_pairs={{0,96},{1,33},{32,0},{33,65},{64,32},{65,97},{96,64},{97,1},{2,98}... | collective-permute-start | bytes 983048 | tf_op jit(solution)/shard_map/quad/ppermute | solution.py:30
  137.1 5.7 %collective-permute-done.26 = f32[128,640]{1,0:T(8,128)S(1)} collective-permute-done((f32[128,640]{1,0:T(8,128)S(1)}, f32[128,640]{1,0:T(8,128)S(1)}, u32[]{:S(2)}, u32[]{:S(2)}) %collective-permute-start.26) | collective-permute-done | bytes 327712 | tf_op jit(solution)/shard_map/quad/ppermute | solution.py:30
  142.8 2.4 %collective-permute-done.23 = f32[384,384]{0,1:T(8,128)} collective-permute-done((f32[384,384]{0,1:T(8,128)S(1)}, f32[384,384]{0,1:T(8,128)}, u32[]{:S(2)}, u32[]{:S(2)}) %collective-permute-start.23) | collective-permute-done | bytes 589856 | tf_op jit(solution)/shard_map/out/ppermute | solution.py:311
  145.2 1.1 broadcast_select_fusion.3
  146.4 0.4 convolution_subtract_fusion.2
  146.9 6.6 %collective-permute-done.28 = f32[128,640]{1,0:T(8,128)S(1)} collective-permute-done((f32[128,640]{1,0:T(8,128)S(1)}, f32[128,640]{1,0:T(8,128)S(1)}, u32[]{:S(2)}, u32[]{:S(2)}) %collective-permute-start.28) | collective-permute-done | bytes 327712 | tf_op jit(solution)/shard_map/quad/ppermute | solution.py:30
  153.5 0.8 add_add_fusion.1
  154.3 1.6 collective-permute-start.29
  155.9 5.9 %collective-permute-start.30 = (f32[128,640]{1,0:T(8,128)}, f32[128,640]{1,0:T(8,128)S(1)}, u32[]{:S(2)}, u32[]{:S(2)}) collective-permute-start(f32[128,640]{1,0:T(8,128)} %add_add_fusion.1), channel_id=1, source_target_pairs={{0,8},{1,0},{8,24},{9,16},{16,9},{17,1},{24,25},{25,17},{2,10},{3,... | collective-permute-start | bytes 983048 | tf_op jit(solution)/shard_map/quad/ppermute | solution.py:234
  161.8 0.7 collective-permute-start.31
  162.5 1.9 %collective-permute-start.32 = (f32[128,640]{1,0:T(8,128)}, f32[128,640]{1,0:T(8,128)S(1)}, u32[]{:S(2)}, u32[]{:S(2)}) collective-permute-start(f32[128,640]{1,0:T(8,128)} %add_add_fusion.1), channel_id=1, source_target_pairs={{0,24},{1,16},{8,8},{9,0},{16,25},{17,17},{24,9},{25,1},{2,26},{3,... | collective-permute-start | bytes 983048 | tf_op jit(solution)/shard_map/quad/ppermute | solution.py:234
  164.4 0.4 convolution_subtract_fusion.1
  164.9 1.1 copy.34
  166.1 0.9 copy.33
  167.0 1.1 collective-permute-done.30
  168.1 7.8 %collective-permute-done.31 = f32[128,640]{1,0:T(8,128)S(1)} collective-permute-done((f32[128,640]{1,0:T(8,128)}, f32[128,640]{1,0:T(8,128)S(1)}, u32[]{:S(2)}, u32[]{:S(2)}) %collective-permute-start.31) | collective-permute-done | bytes 327712 | tf_op jit(solution)/shard_map/quad/ppermute | solution.py:234
  176.2 0.9 copy-done.19
  177.1 0.4 fusion.1
  177.5 0.6 convolution_bitcast_fusion.1
  178.2 0.6 copy-done.17
  178.7 1.4 fusion
  (92 shorter events, 3.1 us)
Async XLA Ops:
  0.6 3.2 %copy-start.18 = (f32[768,128]{1,0:T(8,128)S(1)}, f32[768,128]{1,0:T(8,128)}, u32[]{:S(2)}) copy-start(f32[768,128]{1,0:T(8,128)} %param.9) | copy-start | bytes 1179652
  0.6 3.4 %copy-start.16 = (f32[768,256]{1,0:T(8,128)S(1)}, f32[768,256]{1,0:T(8,128)}, u32[]{:S(2)}) copy-start(f32[768,256]{1,0:T(8,128)} %param.10) | copy-start | bytes 2359300
  2.9 2.2 %collective-permute-start = (f32[192,768]{1,0:T(8,128)}, f32[192,768]{1,0:T(8,128)S(1)}, u32[]{:S(2)}, u32[]{:S(2)}) collective-permute-start(f32[192,768]{1,0:T(8,128)} %get-tuple-element.98), channel_id=1, source_target_pairs={{0,1},{1,0},{2,3},{3,2},{4,5},{5,4},{6,7},{7,6},{8,9},{9,8},{10,11... | collective-permute-start | bytes 1769480 | tf_op jit(solution)/shard_map/gather/ppermute | solution.py:22
  4.3 8.0 %copy-start = (f32[768,384]{1,0:T(8,128)}, f32[768,384]{1,0:T(8,128)S(1)}, u32[]{:S(2)}) copy-start(f32[768,384]{1,0:T(8,128)S(1)} %pad_maximum_fusion.2.refs_4_.refs_2_) | copy-start | bytes 3538948
  5.1 2.8 %collective-permute-start.5 = (f32[768,384]{1,0:T(8,128)S(1)}, f32[768,384]{1,0:T(8,128)S(1)}, u32[]{:S(2)}, u32[]{:S(2)}) collective-permute-start(f32[768,384]{1,0:T(8,128)S(1)} %pad_maximum_fusion.2.refs_4_.refs_2_), channel_id=1, source_target_pairs={{0,1},{1,0},{2,3},{3,2},{4,5},{5,4},{6,7},{7,6},{8,9},{9,8},{10,11... | collective-permute-start | bytes 3538952 | tf_op jit(solution)/shard_map/gather/ppermute | solution.py:22
  5.3 10.6 %copy-start.9 = (f32[2,192,768]{2,1,0:T(8,128)}, f32[2,192,768]{2,1,0:T(8,128)S(1)}, u32[]{:S(2)}) copy-start(f32[2,192,768]{2,1,0:T(8,128)S(1)} %pad_maximum_fusion.1.refs_0_) | copy-start | bytes 3538948
  8.0 1.0 copy-start.1
  9.1 55.5 %copy-start.7 = (f32[4,192,384]{2,1,0:T(8,128)}, f32[4,192,384]{2,1,0:T(8,128)S(1)}, u32[]{:S(2)}) copy-start(f32[4,192,384]{2,1,0:T(8,128)S(1)} %pad_maximum_fusion.3) | copy-start | bytes 3538948
  9.1 17.6 %collective-permute-start.6 = (f32[768,384]{1,0:T(8,128)S(1)}, f32[768,384]{1,0:T(8,128)}, u32[]{:S(2)}, u32[]{:S(2)}) collective-permute-start(f32[768,384]{1,0:T(8,128)S(1)} %bitcast.95), channel_id=1, source_target_pairs={{0,2},{1,7},{2,4},{3,1},{4,6},{5,3},{6,0},{7,5},{8,10},{9,15},{10,... | collective-permute-start | bytes 3538952 | tf_op jit(solution)/shard_map/gather/ppermute | solution.py:30
  10.8 27.2 %collective-permute-start.3 = (f32[768,384]{1,0:T(8,128)S(1)}, f32[768,384]{1,0:T(8,128)S(1)}, u32[]{:S(2)}, u32[]{:S(2)}) collective-permute-start(f32[768,384]{1,0:T(8,128)S(1)} %pad_maximum_fusion.2.refs_4_.refs_2_), channel_id=1, source_target_pairs={{0,32},{1,97},{32,64},{33,1},{64,96},{65,33},{96,0},{97,65},{2,34}... | collective-permute-start | bytes 3538952 | tf_op jit(solution)/shard_map/gather/ppermute | solution.py:30
  12.3 28.0 %collective-permute-start.4 = (f32[768,384]{1,0:T(8,128)S(1)}, f32[768,384]{1,0:T(8,128)S(1)}, u32[]{:S(2)}, u32[]{:S(2)}) collective-permute-start(f32[768,384]{1,0:T(8,128)S(1)} %pad_maximum_fusion.2.refs_4_.refs_2_), channel_id=1, source_target_pairs={{0,96},{1,33},{32,0},{33,65},{64,32},{65,97},{96,64},{97,1},{2,98}... | collective-permute-start | bytes 3538952 | tf_op jit(solution)/shard_map/gather/ppermute | solution.py:30
  14.0 28.3 %collective-permute-start.1 = (f32[2,192,768]{2,1,0:T(8,128)S(1)}, f32[2,192,768]{2,1,0:T(8,128)S(1)}, u32[]{:S(2)}, u32[]{:S(2)}) collective-permute-start(f32[2,192,768]{2,1,0:T(8,128)S(1)} %pad_maximum_fusion.1.refs_0_), channel_id=1, source_target_pairs={{0,8},{1,25},{8,16},{9,1},{16,24},{17,9},{24,0},{25,17},{2,10},{3,... | collective-permute-start | bytes 3538952 | tf_op jit(solution)/shard_map/gather/ppermute | solution.py:30
  16.0 28.0 %collective-permute-start.2 = (f32[2,192,768]{2,1,0:T(8,128)S(1)}, f32[2,192,768]{2,1,0:T(8,128)S(1)}, u32[]{:S(2)}, u32[]{:S(2)}) collective-permute-start(f32[2,192,768]{2,1,0:T(8,128)S(1)} %pad_maximum_fusion.1.refs_0_), channel_id=1, source_target_pairs={{0,24},{1,9},{8,0},{9,17},{16,8},{17,25},{24,16},{25,1},{2,26},{3,... | collective-permute-start | bytes 3538952 | tf_op jit(solution)/shard_map/gather/ppermute | solution.py:30
  26.7 17.4 %collective-permute-start.7 = (f32[768,384]{1,0:T(8,128)S(1)}, f32[768,384]{1,0:T(8,128)}, u32[]{:S(2)}, u32[]{:S(2)}) collective-permute-start(f32[768,384]{1,0:T(8,128)S(1)} %bitcast.96), channel_id=1, source_target_pairs={{0,6},{1,3},{2,0},{3,5},{4,2},{5,7},{6,4},{7,1},{8,14},{9,11},{10,... | collective-permute-start | bytes 3538952 | tf_op jit(solution)/shard_map/gather/ppermute | solution.py:30
  38.0 35.3 %copy-start.2 = (f32[768,384]{1,0:T(8,128)}, f32[768,384]{1,0:T(8,128)S(1)}, u32[]{:S(2)}) copy-start(f32[768,384]{1,0:T(8,128)S(1)} %collective-permute-done.3.refs_6_.refs_4_) | copy-start | bytes 3538948
  40.2 33.1 %copy-start.3 = (f32[768,384]{1,0:T(8,128)}, f32[768,384]{1,0:T(8,128)S(1)}, u32[]{:S(2)}) copy-start(f32[768,384]{1,0:T(8,128)S(1)} %collective-permute-done.4.refs_8_.refs_6_) | copy-start | bytes 3538948
  42.3 22.3 %copy-start.11 = (f32[2,192,768]{2,1,0:T(8,128)}, f32[2,192,768]{2,1,0:T(8,128)S(1)}, u32[]{:S(2)}) copy-start(f32[2,192,768]{2,1,0:T(8,128)S(1)} %collective-permute-done.1.refs_1_) | copy-start | bytes 3538948
  44.0 2.5 %copy-start.12 = (f32[2,192,768]{2,1,0:T(8,128)}, f32[2,192,768]{2,1,0:T(8,128)S(1)}, u32[]{:S(2)}) copy-start(f32[2,192,768]{2,1,0:T(8,128)S(1)} %collective-permute-done.2.refs_2_) | copy-start | bytes 3538948
  44.0 17.7 %collective-permute-start.10 = (f32[768,384]{1,0:T(8,128)}, f32[768,384]{1,0:T(8,128)}, u32[]{:S(2)}, u32[]{:S(2)}) collective-permute-start(f32[768,384]{1,0:T(8,128)} %collective-permute-done.6), channel_id=1, source_target_pairs={{0,2},{1,7},{2,4},{3,1},{4,6},{5,3},{6,0},{7,5},{8,10},{9,15},{10,... | collective-permute-start | bytes 3538952 | tf_op jit(solution)/shard_map/gather/ppermute | solution.py:30
  46.5 15.2 %collective-permute-start.11 = (f32[768,384]{1,0:T(8,128)S(1)}, f32[768,384]{1,0:T(8,128)S(1)}, u32[]{:S(2)}, u32[]{:S(2)}) collective-permute-start(f32[768,384]{1,0:T(8,128)S(1)} %collective-permute-done.4.refs_8_.refs_6_), channel_id=1, source_target_pairs={{0,1},{1,0},{2,3},{3,2},{4,5},{5,4},{6,7},{7,6},{8,9},{9,8},{10,11... | collective-permute-start | bytes 3538952 | tf_op jit(solution)/shard_map/gather/ppermute | solution.py:22
  46.5 15.2 %collective-permute-start.12 = (f32[768,384]{1,0:T(8,128)S(1)}, f32[768,384]{1,0:T(8,128)S(1)}, u32[]{:S(2)}, u32[]{:S(2)}) collective-permute-start(f32[768,384]{1,0:T(8,128)S(1)} %collective-permute-done.3.refs_6_.refs_4_), channel_id=1, source_target_pairs={{0,1},{1,0},{2,3},{3,2},{4,5},{5,4},{6,7},{7,6},{8,9},{9,8},{10,11... | collective-permute-start | bytes 3538952 | tf_op jit(solution)/shard_map/gather/ppermute | solution.py:22
  47.0 17.4 %collective-permute-start.8 = (f32[2,192,768]{2,1,0:T(8,128)S(1)}, f32[2,192,768]{2,1,0:T(8,128)S(1)}, u32[]{:S(2)}, u32[]{:S(2)}) collective-permute-start(f32[2,192,768]{2,1,0:T(8,128)S(1)} %collective-permute-done.1.refs_1_), channel_id=1, source_target_pairs={{0,8},{1,25},{8,16},{9,1},{16,24},{17,9},{24,0},{25,17},{2,10},{3,... | collective-permute-start | bytes 3538952 | tf_op jit(solution)/shard_map/gather/ppermute | solution.py:30
  47.0 17.5 %collective-permute-start.9 = (f32[768,384]{1,0:T(8,128)S(1)}, f32[768,384]{1,0:T(8,128)}, u32[]{:S(2)}, u32[]{:S(2)}) collective-permute-start(f32[768,384]{1,0:T(8,128)S(1)} %collective-permute-done.3.refs_6_.refs_4_), channel_id=1, source_target_pairs={{0,32},{1,97},{32,64},{33,1},{64,96},{65,33},{96,0},{97,65},{2,34}... | collective-permute-start | bytes 3538952 | tf_op jit(solution)/shard_map/gather/ppermute | solution.py:30
  61.7 11.6 %copy-start.4 = (f32[768,384]{1,0:T(8,128)}, f32[768,384]{1,0:T(8,128)S(1)}, u32[]{:S(2)}) copy-start(f32[768,384]{1,0:T(8,128)S(1)} %collective-permute-done.11.refs_7_.refs_5_) | copy-start | bytes 3538948
  61.8 2.8 %copy-start.5 = (f32[768,384]{1,0:T(8,128)}, f32[768,384]{1,0:T(8,128)S(1)}, u32[]{:S(2)}) copy-start(f32[768,384]{1,0:T(8,128)S(1)} %collective-permute-done.12.refs_9_.refs_7_) | copy-start | bytes 3538948
  64.4 1.0 copy-start.13
  64.6 8.7 %collective-permute-start.13 = (f32[768,384]{1,0:T(8,128)}, f32[768,384]{1,0:T(8,128)}, u32[]{:S(2)}, u32[]{:S(2)}) collective-permute-start(f32[768,384]{1,0:T(8,128)} %collective-permute-done.9.refs_10_.refs_8_), channel_id=1, source_target_pairs={{0,1},{1,0},{2,3},{3,2},{4,5},{5,4},{6,7},{7,6},{8,9},{9,8},{10,11... | collective-permute-start | bytes 3538952 | tf_op jit(solution)/shard_map/gather/ppermute | solution.py:22
  65.4 28.3 %collective-permute-start.15 = (f32[768,384]{1,0:T(8,128)}, f32[768,384]{1,0:T(8,128)}, u32[]{:S(2)}, u32[]{:S(2)}) collective-permute-start(f32[768,384]{1,0:T(8,128)} %collective-permute-done.10), channel_id=1, source_target_pairs={{0,32},{1,97},{34,66},{35,3},{68,100},{69,37},{102,6},{103,71},{8,... | collective-permute-start | bytes 3538952 | tf_op jit(solution)/shard_map/product/ppermute | solution.py:254
  69.2 39.3 %collective-permute-start.17 = (f32[768,384]{1,0:T(8,128)}, f32[768,384]{1,0:T(8,128)}, u32[]{:S(2)}, u32[]{:S(2)}) collective-permute-start(f32[768,384]{1,0:T(8,128)} %collective-permute-done.6), channel_id=1, source_target_pairs={{0,96},{1,33},{34,2},{35,67},{68,36},{69,101},{102,70},{103,7},{8,... | collective-permute-start | bytes 3538952 | tf_op jit(solution)/shard_map/product/ppermute | solution.py:254
  82.7 24.2 %collective-permute-start.14 = (f32[768,384]{1,0:T(8,128)}, f32[768,384]{1,0:T(8,128)S(1)}, u32[]{:S(2)}, u32[]{:S(2)}) collective-permute-start(f32[768,384]{1,0:T(8,128)} %get-tuple-element.55), channel_id=1, source_target_pairs={{0,2},{1,7},{2,4},{3,1},{4,6},{5,3},{6,0},{7,5},{8,10},{9,15},{10,... | collective-permute-start | bytes 3538952 | tf_op jit(solution)/shard_map/product/ppermute | solution.py:30
  90.9 17.5 %collective-permute-start.18 = (f32[768,384]{1,0:T(8,128)}, f32[768,384]{1,0:T(8,128)S(1)}, u32[]{:S(2)}, u32[]{:S(2)}) collective-permute-start(f32[768,384]{1,0:T(8,128)} %collective-permute-done.7), channel_id=1, source_target_pairs={{0,32},{1,97},{34,66},{35,3},{68,100},{69,37},{102,6},{103,71},{8,... | collective-permute-start | bytes 3538952 | tf_op jit(solution)/shard_map/product/ppermute | solution.py:254
  93.7 14.7 %collective-permute-start.16 = (f32[768,384]{1,0:T(8,128)}, f32[768,384]{1,0:T(8,128)S(1)}, u32[]{:S(2)}, u32[]{:S(2)}) collective-permute-start(f32[768,384]{1,0:T(8,128)} %collective-permute-done.15), channel_id=1, source_target_pairs={{32,64},{97,65},{66,98},{3,99},{100,4},{37,5},{6,38},{71,39},{40,7... | collective-permute-start | bytes 3538952 | tf_op jit(solution)/shard_map/product/ppermute | solution.py:254
  94.5 23.2 %collective-permute-start.19 = (f32[768,384]{1,0:T(8,128)}, f32[768,384]{1,0:T(8,128)}, u32[]{:S(2)}, u32[]{:S(2)}) collective-permute-start(f32[768,384]{1,0:T(8,128)} %next_product.3), channel_id=1, source_target_pairs={{0,6},{1,3},{2,0},{3,5},{4,2},{5,7},{6,4},{7,1},{8,14},{9,11},{10,... | collective-permute-start | bytes 3538952 | tf_op jit(solution)/shard_map/product/ppermute | solution.py:30
  106.9 1.6 copy-start.8
  108.4 17.5 %collective-permute-start.20 = (f32[768,384]{1,0:T(8,128)S(1)}, f32[768,384]{1,0:T(8,128)S(1)}, u32[]{:S(2)}, u32[]{:S(2)}) collective-permute-start(f32[768,384]{1,0:T(8,128)S(1)} %add.170), channel_id=1, source_target_pairs={{0,2},{1,7},{2,4},{3,1},{4,6},{5,3},{6,0},{7,5},{8,10},{9,15},{10,... | collective-permute-start | bytes 3538952 | tf_op jit(solution)/shard_map/product/ppermute | solution.py:30
  108.9 16.9 %collective-permute-start.24 = (f32[768,128]{1,0:T(8,128)S(1)}, f32[768,128]{1,0:T(8,128)S(1)}, u32[]{:S(2)}, u32[]{:S(2)}) collective-permute-start(f32[768,128]{1,0:T(8,128)S(1)} %slice.62), channel_id=1, source_target_pairs={{0,8},{8,0},{16,24},{24,16},{1,9},{9,1},{17,25},{25,17},{2,10},{10... | collective-permute-start | bytes 1179656 | tf_op jit(solution)/shard_map/turned/ppermute | solution.py:288
  125.8 1.3 copy-start.14
  128.6 3.1 %collective-permute-start.21 = (f32[384,384]{1,0:T(8,128)S(1)}, f32[384,384]{1,0:T(8,128)S(1)}, u32[]{:S(2)}, u32[]{:S(2)}) collective-permute-start(f32[384,384]{1,0:T(8,128)S(1)} %get-tuple-element.95), channel_id=1, source_target_pairs={{0,1},{1,0},{2,3},{3,2},{4,5},{5,4},{6,7},{7,6},{8,9},{9,8},{10,11... | collective-permute-start | bytes 1769480 | tf_op jit(solution)/shard_map/out/ppermute | solution.py:22
  131.2 2.5 %collective-permute-start.25 = (f32[128,640]{1,0:T(8,128)}, f32[128,640]{1,0:T(8,128)S(1)}, u32[]{:S(2)}, u32[]{:S(2)}) collective-permute-start(f32[128,640]{1,0:T(8,128)} %dynamic-slice_bitcast_fusion.6), channel_id=1, source_target_pairs={{0,1},{1,0},{2,3},{3,2},{4,5},{5,4},{6,7},{7,6},{8,9},{9,8},{10,11... | collective-permute-start | bytes 983048 | tf_op jit(solution)/shard_map/quad/ppermute | solution.py:22
  132.1 13.1 %collective-permute-start.23 = (f32[384,384]{0,1:T(8,128)S(1)}, f32[384,384]{0,1:T(8,128)}, u32[]{:S(2)}, u32[]{:S(2)}) collective-permute-start(f32[384,384]{0,1:T(8,128)S(1)} %bitcast.104), channel_id=1, source_target_pairs={{0,8},{1,24},{8,0},{9,16},{16,9},{17,25},{24,1},{25,17},{2,10},{3,... | collective-permute-start | bytes 1769480 | tf_op jit(solution)/shard_map/out/ppermute | solution.py:311
  133.0 12.2 %collective-permute-start.22 = (f32[384,384]{0,1:T(8,128)S(1)}, f32[384,384]{0,1:T(8,128)S(1)}, u32[]{:S(2)}, u32[]{:S(2)}) collective-permute-start(f32[384,384]{0,1:T(8,128)S(1)} %bitcast.103), channel_id=1, source_target_pairs={{0,0},{1,16},{8,8},{9,24},{16,1},{17,17},{24,9},{25,25},{2,2},{3,1... | collective-permute-start | bytes 1769480 | tf_op jit(solution)/shard_map/out/ppermute | solution.py:311
  133.8 9.0 %collective-permute-start.26 = (f32[128,640]{1,0:T(8,128)S(1)}, f32[128,640]{1,0:T(8,128)S(1)}, u32[]{:S(2)}, u32[]{:S(2)}) collective-permute-start(f32[128,640]{1,0:T(8,128)S(1)} %bitcast_add_fusion), channel_id=1, source_target_pairs={{0,32},{1,97},{32,64},{33,1},{64,96},{65,33},{96,0},{97,65},{2,34}... | collective-permute-start | bytes 983048 | tf_op jit(solution)/shard_map/quad/ppermute | solution.py:30
  133.9 12.6 %copy-start.6 = (f32[2,256,256]{2,1,0:T(8,128)S(1)}, f32[2,256,256]{2,1,0:T(8,128)}, u32[]{:S(2)}) copy-start(f32[2,256,256]{2,1,0:T(8,128)} %param.11) | copy-start | bytes 1572868
  133.9 13.0 %collective-permute-start.27 = (f32[128,640]{1,0:T(8,128)S(1)}, f32[128,640]{1,0:T(8,128)S(1)}, u32[]{:S(2)}, u32[]{:S(2)}) collective-permute-start(f32[128,640]{1,0:T(8,128)S(1)} %bitcast_add_fusion), channel_id=1, source_target_pairs={{0,96},{1,33},{32,0},{33,65},{64,32},{65,97},{96,64},{97,1},{2,98}... | collective-permute-start | bytes 983048 | tf_op jit(solution)/shard_map/quad/ppermute | solution.py:30
  145.2 8.3 %collective-permute-start.28 = (f32[128,640]{1,0:T(8,128)S(1)}, f32[128,640]{1,0:T(8,128)S(1)}, u32[]{:S(2)}, u32[]{:S(2)}) collective-permute-start(f32[128,640]{1,0:T(8,128)S(1)} %collective-permute-done.26), channel_id=1, source_target_pairs={{0,32},{1,97},{32,64},{33,1},{64,96},{65,33},{96,0},{97,65},{2,34}... | collective-permute-start | bytes 983048 | tf_op jit(solution)/shard_map/quad/ppermute | solution.py:30
  154.3 12.7 %collective-permute-start.29 = (f32[128,640]{1,0:T(8,128)}, f32[128,640]{1,0:T(8,128)S(1)}, u32[]{:S(2)}, u32[]{:S(2)}) collective-permute-start(f32[128,640]{1,0:T(8,128)} %add_add_fusion.1), channel_id=1, source_target_pairs={{0,0},{1,8},{8,16},{9,24},{16,1},{17,9},{24,17},{25,25},{2,2},{3,1... | collective-permute-start | bytes 983048 | tf_op jit(solution)/shard_map/quad/ppermute | solution.py:234
  155.9 12.2 %collective-permute-start.30 = (f32[128,640]{1,0:T(8,128)}, f32[128,640]{1,0:T(8,128)S(1)}, u32[]{:S(2)}, u32[]{:S(2)}) collective-permute-start(f32[128,640]{1,0:T(8,128)} %add_add_fusion.1), channel_id=1, source_target_pairs={{0,8},{1,0},{8,24},{9,16},{16,9},{17,1},{24,25},{25,17},{2,10},{3,... | collective-permute-start | bytes 983048 | tf_op jit(solution)/shard_map/quad/ppermute | solution.py:234
  161.8 14.1 %collective-permute-start.31 = (f32[128,640]{1,0:T(8,128)}, f32[128,640]{1,0:T(8,128)S(1)}, u32[]{:S(2)}, u32[]{:S(2)}) collective-permute-start(f32[128,640]{1,0:T(8,128)} %add_add_fusion.1), channel_id=1, source_target_pairs={{0,16},{1,24},{8,0},{9,8},{16,17},{17,25},{24,1},{25,9},{2,18},{3,... | collective-permute-start | bytes 983048 | tf_op jit(solution)/shard_map/quad/ppermute | solution.py:234
  162.5 13.4 %collective-permute-start.32 = (f32[128,640]{1,0:T(8,128)}, f32[128,640]{1,0:T(8,128)S(1)}, u32[]{:S(2)}, u32[]{:S(2)}) collective-permute-start(f32[128,640]{1,0:T(8,128)} %add_add_fusion.1), channel_id=1, source_target_pairs={{0,24},{1,16},{8,8},{9,0},{16,25},{17,17},{24,9},{25,1},{2,26},{3,... | collective-permute-start | bytes 983048 | tf_op jit(solution)/shard_map/quad/ppermute | solution.py:234
  176.1 1.0 copy-start.19
  177.1 1.1 copy-start.15
  177.5 2.7 %copy-start.10 = (f32[2,256,256]{2,1,0:T(8,128)}, f32[2,256,256]{2,1,0:T(8,128)S(1)}, u32[]{:S(2)}) copy-start(f32[2,256,256]{2,1,0:T(8,128)S(1)} %fusion.1) | copy-start | bytes 1572868
  177.5 1.2 copy-start.17

commit v2 on v1

--- a/solution.py
+++ b/solution.py
@@ -161,6 +161,59 @@
     return results if first else results[0]
 
 
+def dot_in_parts(left, right, contract):
+    left, right = split(left), split(right)
+    dot = functools.partial(
+        lax.dot_general,
+        dimension_numbers=((contract[:1], contract[1:]), ((), ())),
+        preferred_element_type=jnp.float32,
+    )
+    return dot(left[0], right[1]) + dot(left[1], right[0]) + dot(left[0], right[0])
+
+
+def finish_kernel(z, *refs):
+    came, (parent, diag_one, diag_two, out_one, out_par, out_two, sums) = refs[:4], refs[4:]
+    tall, wide = came[0].shape
+    block = parent.shape[1]
+    for turn_over, ref in enumerate(came):
+        which = z[turn_over]
+        at = pl.ds(pl.multiple_of(which % 2 * tall, tall), tall)
+        sums[which // 2, at, :] = ref[...]
+    part = wide - 2 * block
+    first = jnp.concatenate([sums[j, :, pl.ds(0, part)] for j in range(2)], axis=1)
+    first = first + diag_one[0]
+    out_one[0] = first
+    for j in range(2):
+        across = sums[j, :, pl.ds(part, block)]
+        reach = sums[j, :, pl.ds(part + block, block)]
+        par = across - dot_in_parts(first, parent[j], (1, 0))
+        out_par[j] = par
+        out_two[j] = (
+            diag_two[j]
+            + reach
+            - dot_in_parts(across, parent[j], (0, 0))
+            - dot_in_parts(parent[j], par, (0, 0))
+        )
+
+
+def finish(z, came, parent, diag_one, diag_two):
+    vmem = pl.BlockSpec(memory_space=pltpu.VMEM)
+    tall, wide = came[0].shape
+    which = jnp.stack([z ^ turn_over for turn_over in range(4)]).astype(jnp.int32)
+    return pl.pallas_call(
+        finish_kernel,
+        out_shape=[
+            jax.ShapeDtypeStruct(v.shape, jnp.float32) for v in (diag_one, parent, diag_two)
+        ],
+        in_specs=[pl.BlockSpec(memory_space=pltpu.SMEM)] + [vmem] * 7,
+        out_specs=[vmem] * 3,
+        scratch_shapes=[pltpu.VMEM((2, 2 * tall, wide), jnp.float32)],
+        compiler_params=pltpu.CompilerParams(vmem_limit_bytes=24 * 2**20),
+        cost_estimate=pl.CostEstimate(flops=10**8, bytes_accessed=10**6, transcendentals=0),
+        name="finish",
+    )(which, *came, parent, diag_one, diag_two)
+
+
 def local(
     ancestor_inv, panel_one, panel_two, parent_block, diag_one, diag_two, pattern_one, pattern_two
 ):
@@ -224,8 +277,8 @@
         a_far, l_far = send(a_first, "z", 1), send(l_first, "x", 1)
         t_far = send(after(t_first, t_second), "y", 1)
         first_other, second_other = swap(l_second), swap(l_first)
-        a_far, l_far, t_far, first_other, second_other = lax.optimization_barrier(
-            (a_far, l_far, t_far, first_other, second_other)
+        a_far, l_far, first_other, second_other = lax.optimization_barrier(
+            (a_far, l_far, first_other, second_other)
         )
         far_other = swap(l_far)
 
@@ -277,6 +330,7 @@
         last_came = send(last, "y", 1)
     with jax.named_scope("turned"):
         shift = (x - y) % 4
+        q_far = after(q_far, near_came)
         turned = jnp.where(
             shift == 0,
             source,
@@ -290,7 +344,7 @@
             (jnp.where(z % 2 == 0, own, mate), jnp.where(z % 2 == 0, mate, own)), axis=1
         )
     with jax.named_scope("total"):
-        rest = product([strip_of(0)], [after(p, last, turned, near_came) for p in parts], strips, True)
+        rest = product([strip_of(0)], [after(p, last) for p in parts], strips, True)
         rest, near_came, last_came = lax.optimization_barrier((rest, near_came, last_came))
         total = rest + near_came + last_came
     with jax.named_scope("out"):
@@ -319,13 +373,9 @@
         quad = quad.reshape(2, BLOCK // 2, wide)
         quad = pick(quad, core) + swap(pick(quad, 1 - core))
         first, second = send(quad, "x", 1), send(quad, "x", -1)
-        around = quad + first + second + send(after(first, pieces[1]), "x", 1)
+        around = quad + first + second + send(after(first, second, pieces[1]), "x", 1)
         around = after(around, pieces[0])
-        came = jnp.stack(spread([around] * 4))
-        sums = [
-            jnp.concatenate([pick(came, (2 * j + h) ^ z) for h in range(2)], axis=0)
-            for j in range(2)
-        ]
+        came = spread([around] * 4)
     with jax.named_scope("out"):
         joined = [jnp.where(z % 2 == j, pieces[0], pieces[1]) for j in range(2)]
         prod_one = jnp.concatenate([v[:, :w1] for v in joined], axis=1)
@@ -338,17 +388,7 @@
             axis=1,
         )
     with jax.named_scope("diag"):
-        first = jnp.concatenate((sums[0][:, :w1], sums[1][:, :w1]), axis=1)
-        across = jnp.stack([s[:, w1 : w1 + w2] for s in sums])
-        reach = jnp.stack([s[:, w1 + w2 :] for s in sums])
-        diag_inv_one = diag_one + first[None]
-        inv_par = across - jnp.einsum("ab,pbc->pac", diag_inv_one[0], parent_block, precision=HIGH)
-        diag_inv_two = (
-            diag_two
-            + reach
-            - jnp.einsum("pba,pbc->pac", across, parent_block, precision=HIGH)
-            - jnp.einsum("pba,pbc->pac", parent_block, inv_par, precision=HIGH)
-        )
+        diag_inv_one, inv_par, diag_inv_two = finish(z, came, parent_block, diag_one, diag_two)
     return (inv_one, diag_inv_one, inv_two, inv_par, diag_inv_two)
 
 

time: 183 us -> 183 us (level); the launches traced: 180 us -> 183 us
  starting transfers between devices: 46.2 us -> 52.5 us
  waiting for transfers between devices: 75.6 us -> 71.2 us
  other arithmetic: 7.28 us -> 10 us
  matrix products: 5.03 us -> 2.54 us
  Pallas kernels: 33.8 us -> 36.2 us
    ppermute x15, waiting for transfers between devices: 60.9 us -> 56.3 us  [send(): return lax.ppermute(value, (axis, 'core'), split_pairs(step))]
    ppermute x2, starting transfers between devices: 1.33 us -> 4.1 us  [local(): lax.ppermute(pick(blocks, (z + turn_over) % 2), ('z', 'core'), pairs)]
    dot_general x3 -> x0, matrix products: 2.47 us -> none  [the longest x1 1.45 us: local(): jnp.einsum('pba,pbc->pac', across, parent_block, precision=HIGH)]
    ppermute x2, waiting for transfers between devices: 2.43 us -> 0.01 us  [local(): lax.ppermute(pick(blocks, (z + turn_over) % 2), ('z', 'core'), pairs)]
    pallas_call x0 -> x1, Pallas kernels: none -> 2.4 us  [finish(): pl.pallas_call(finish_kernel, out_shape=[jax.ShapeDtypeStruct(v.shape, jn...]
    ppermute x1, starting transfers between devices: 1.48 us -> 3.7 us  [local(): mate = lax.ppermute(own, 'z', [(0, 1), (1, 0), (2, 3), (3, 2)])]
    unnamed x42 -> x44, local copies, waits for them, and re-layouts: 6.49 us -> 4.86 us
  transfers between devices with their start and end apart: 33 -> 33, of which waited for: 16 -> 18; matrix products, arithmetic and copies ran while one was open for 6% -> 7% of each run, Pallas kernels for 19% -> 18%
where the time goes in v2:
time: 183 us
  waiting for transfers between devices  71.2 us (39%)
  starting transfers between devices  52.5 us (29%)
  Pallas kernels  36.2 us (20%)
  other arithmetic  10 us (5%)
  local copies, waits for them, and re-layouts  9.26 us (5%)
  matrix products  2.54 us (1%)
    ppermute x15, waiting for transfers between devices, send(): return lax.ppermute(value, (axis, 'core'), split_pairs(step))  56.3 us
    pallas_call x4, Pallas kernels, product(): pl.pallas_call(first_kernel if first else next_kernel, out_shape=[parts,...  33.8 us
    ppermute x15, starting transfers between devices, send(): return lax.ppermute(value, (axis, 'core'), split_pairs(step))  20.1 us
    ppermute x4, starting transfers between devices, spread(): lax.ppermute(value, ('z', 'core'), [((2 * c + j) * 2 + h, (2 * j + h ^ tu...  11.7 us
    ppermute x4, starting transfers between devices, turn(): return lax.ppermute(value, ('x', 'y', 'core'), pairs)  10.7 us
    ppermute x4, waiting for transfers between devices, spread(): lax.ppermute(value, ('z', 'core'), [((2 * c + j) * 2 + h, (2 * j + h ^ tu...  8.88 us
    unnamed x44, local copies, waits for them, and re-layouts  4.86 us
    ppermute x7, waiting for transfers between devices, swap(): return lax.ppermute(value, 'core', [(0, 1), (1, 0)])  4.22 us
  transfers between devices with their start and end apart: 33, of which 18 were waited for; matrix products, arithmetic and copies ran while one was open for 7% of the time, Pallas kernels for 18%

profile of v2, /device:TPU:0, one launch (start us, length us, event | category | flops | bytes accessed | tf_op | source)
XLA Modules:
  0.0 182.9 jit_solution(16892582301599115145)
XLA Ops:
  0.7 2.2 %constant_dynamic-slice_fusion.1 = (f32[1,192,768]{2,1,0:T(8,128)S(1)}, f32[192,768]{1,0:T(8,128)}) fusion(f32[2,192,768]{2,1,0:T(8,128)} %bitcast.67, s32[]{:T(128)S(6)} %select_n.238, s32[]{:T(128)S(6)} %select_n.239), kind=kLoop, calls=%fused_computation.45 | loop fusion | bytes 2359304 | tf_op jit(solution)/shard_map/gather/jit(dynamic_index_in_dim)/dynamic_slice | solution.py:38
  2.9 0.8 convert_bitcast_fusion.1
  4.3 0.9 collective-permute-done
  5.4 1.1 pad_maximum_fusion.refs_0_
  6.5 1.6 collective-permute-done.5.refs_5_.refs_3_
  8.2 0.9 copy-done.4
  9.2 1.7 collective-permute-start.6
  10.9 1.5 collective-permute-start.3
  12.4 1.7 collective-permute-start.4
  14.2 1.9 %collective-permute-start.1 = (f32[2,192,768]{2,1,0:T(8,128)S(1)}, f32[2,192,768]{2,1,0:T(8,128)S(1)}, u32[]{:S(2)}, u32[]{:S(2)}) collective-permute-start(f32[2,192,768]{2,1,0:T(8,128)S(1)} %pad_maximum_fusion.refs_0_), channel_id=1, source_target_pairs={{0,8},{1,25},{8,16},{9,1},{16,24},{17,9},{24,0},{25,17},{2,10},{3,... | collective-permute-start | bytes 3538952 | tf_op jit(solution)/shard_map/gather/ppermute | solution.py:30
  16.1 2.1 %collective-permute-start.2 = (f32[2,192,768]{2,1,0:T(8,128)S(1)}, f32[2,192,768]{2,1,0:T(8,128)S(1)}, u32[]{:S(2)}, u32[]{:S(2)}) collective-permute-start(f32[2,192,768]{2,1,0:T(8,128)S(1)} %pad_maximum_fusion.refs_0_), channel_id=1, source_target_pairs={{0,24},{1,9},{8,0},{9,17},{16,8},{17,25},{24,16},{25,1},{2,26},{3,... | collective-permute-start | bytes 3538952 | tf_op jit(solution)/shard_map/gather/ppermute | solution.py:30
  18.2 8.5 %collective-permute-done.6 = f32[768,384]{1,0:T(8,128)S(1)} collective-permute-done((f32[768,384]{1,0:T(8,128)S(1)}, f32[768,384]{1,0:T(8,128)S(1)}, u32[]{:S(2)}, u32[]{:S(2)}) %collective-permute-start.6) | collective-permute-done | bytes 1179680 | tf_op jit(solution)/shard_map/gather/ppermute | solution.py:30
  26.7 1.9 %collective-permute-start.7 = (f32[768,384]{1,0:T(8,128)S(1)}, f32[768,384]{1,0:T(8,128)}, u32[]{:S(2)}, u32[]{:S(2)}) collective-permute-start(f32[768,384]{1,0:T(8,128)S(1)} %bitcast.62), channel_id=1, source_target_pairs={{0,6},{1,3},{2,0},{3,5},{4,2},{5,7},{6,4},{7,1},{8,14},{9,11},{10,... | collective-permute-start | bytes 3538952 | tf_op jit(solution)/shard_map/gather/ppermute | solution.py:30
  28.6 9.5 %collective-permute-done.3.refs_6_.refs_4_ = f32[768,384]{1,0:T(8,128)S(1)} collective-permute-done((f32[768,384]{1,0:T(8,128)S(1)}, f32[768,384]{1,0:T(8,128)S(1)}, u32[]{:S(2)}, u32[]{:S(2)}) %collective-permute-start.3) | collective-permute-done | bytes 1179680 | tf_op jit(solution)/shard_map/gather/ppermute | solution.py:30
  38.1 2.3 %collective-permute-done.4.refs_8_.refs_6_ = f32[768,384]{1,0:T(8,128)S(1)} collective-permute-done((f32[768,384]{1,0:T(8,128)S(1)}, f32[768,384]{1,0:T(8,128)S(1)}, u32[]{:S(2)}, u32[]{:S(2)}) %collective-permute-start.4) | collective-permute-done | bytes 1179680 | tf_op jit(solution)/shard_map/gather/ppermute | solution.py:30
  40.4 2.1 %collective-permute-done.1.refs_1_ = f32[2,192,768]{2,1,0:T(8,128)S(1)} collective-permute-done((f32[2,192,768]{2,1,0:T(8,128)S(1)}, f32[2,192,768]{2,1,0:T(8,128)S(1)}, u32[]{:S(2)}, u32[]{:S(2)}) %collective-permute-start.1) | collective-permute-done | bytes 1179680 | tf_op jit(solution)/shard_map/gather/ppermute | solution.py:30
  42.4 1.7 collective-permute-done.2.refs_2_
  44.1 1.1 copy-done.13
  45.3 0.7 collective-permute-start.10
  46.3 0.7 collective-permute-start.9
  47.0 1.4 collective-permute-start.19
  48.4 1.7 collective-permute-done.11.refs_9_.refs_7_
  50.1 13.5 %collective-permute-done.8.refs_3_ = f32[2,192,768]{2,1,0:T(8,128)S(1)} collective-permute-done((f32[2,192,768]{2,1,0:T(8,128)S(1)}, f32[2,192,768]{2,1,0:T(8,128)S(1)}, u32[]{:S(2)}, u32[]{:S(2)}) %collective-permute-start.8) | collective-permute-done | bytes 1179680 | tf_op jit(solution)/shard_map/gather/ppermute | solution.py:30
  63.8 0.8 collective-permute-start.12
  64.7 4.3 %collective-permute-start.20 = (f32[768,384]{1,0:T(8,128)}, f32[768,384]{1,0:T(8,128)}, u32[]{:S(2)}, u32[]{:S(2)}) collective-permute-start(f32[768,384]{1,0:T(8,128)} %collective-permute-done.19), channel_id=1, source_target_pairs={{0,32},{1,97},{34,66},{35,3},{68,100},{69,37},{102,6},{103,71},{8,... | collective-permute-start | bytes 3538952 | tf_op jit(solution)/shard_map/product/ppermute | solution.py:307
  69.0 0.7 stack.55.places
  69.6 3.1 %collective-permute-start.22 = (f32[768,384]{1,0:T(8,128)}, f32[768,384]{1,0:T(8,128)}, u32[]{:S(2)}, u32[]{:S(2)}) collective-permute-start(f32[768,384]{1,0:T(8,128)} %copy-done.20), channel_id=1, source_target_pairs={{0,96},{1,33},{34,2},{35,67},{68,36},{69,101},{102,70},{103,7},{8,... | collective-permute-start | bytes 3538952 | tf_op jit(solution)/shard_map/product/ppermute | solution.py:307
  72.7 9.4 %first_product.1 = (bf16[768,1536]{1,0:T(8,128)(2,1)}, bf16[768,1536]{1,0:T(8,128)(2,1)}, f32[768,384]{1,0:T(8,128)}) custom-call(s32[5]{0:T(128)} %stack.55.places, f32[2,192,768]{2,1,0:T(8,128)} %copy-done.11, f32[2,192,768]{2,1,0:T(8,128)} %copy-done.12, f32[2,192,768]{2,1,0:T(8,128)} %copy-done.13, f32[2,192,768]{2,1,0:T(8,128)} %copy-done.14, ...), custom_call_target="tpu_custom_call" | custom-call | flops 768 | bytes 768 | tf_op jit(solution)/shard_map/product/first_product/pallas_call | solution.py:148
  82.2 8.1 %next_product.3 = f32[768,384]{1,0:T(8,128)} custom-call(s32[1]{0:T(128)} %bitcast.20.places, bf16[768,1536]{1,0:T(8,128)(2,1)} %get-tuple-element.62.refs_0_, bf16[768,1536]{1,0:T(8,128)(2,1)} %get-tuple-element.63.refs_1_, f32[768,384]{1,0:T(8,128)} %copy-done.3, f32[768,384]{1,0:T(8,128)} %copy-done.4, f32[768,384]{1,0:T(8,128)} %copy-done.5, ...), custom_call_target="tpu_custom_call" | custom-call | flops 768 | bytes 768 | tf_op jit(solution)/shard_map/product/next_product/pallas_call | solution.py:148
  90.4 3.3 %collective-permute-start.14 = (f32[768,384]{1,0:T(8,128)}, f32[768,384]{1,0:T(8,128)}, u32[]{:S(2)}, u32[]{:S(2)}) collective-permute-start(f32[768,384]{1,0:T(8,128)} %next_product.3), channel_id=1, source_target_pairs={{0,6},{1,3},{2,0},{3,5},{4,2},{5,7},{6,4},{7,1},{8,14},{9,11},{10,... | collective-permute-start | bytes 3538952 | tf_op jit(solution)/shard_map/product/ppermute | solution.py:30
  93.6 0.7 collective-permute-start.21
  94.4 2.6 %collective-permute-start.23 = (f32[768,384]{1,0:T(8,128)}, f32[768,384]{1,0:T(8,128)S(1)}, u32[]{:S(2)}, u32[]{:S(2)}) collective-permute-start(f32[768,384]{1,0:T(8,128)} %collective-permute-done.7), channel_id=1, source_target_pairs={{0,32},{1,97},{34,66},{35,3},{68,100},{69,37},{102,6},{103,71},{8,... | collective-permute-start | bytes 3538952 | tf_op jit(solution)/shard_map/product/ppermute | solution.py:307
  97.1 8.1 %next_product.4 = f32[768,384]{1,0:T(8,128)} custom-call(s32[1]{0:T(128)} %bitcast.19.places, bf16[768,1536]{1,0:T(8,128)(2,1)} %get-tuple-element.62.refs_0_, bf16[768,1536]{1,0:T(8,128)(2,1)} %get-tuple-element.63.refs_1_, f32[768,384]{1,0:T(8,128)} %copy-done.3, f32[768,384]{1,0:T(8,128)} %copy-done.4, f32[768,384]{1,0:T(8,128)} %copy-done.5, ...), custom_call_target="tpu_custom_call" | custom-call | flops 768 | bytes 768 | tf_op jit(solution)/shard_map/product/next_product/pallas_call | solution.py:148
  105.2 1.5 add.151
  106.8 4.0 %collective-permute-done.14 = f32[768,384]{1,0:T(8,128)} collective-permute-done((f32[768,384]{1,0:T(8,128)}, f32[768,384]{1,0:T(8,128)}, u32[]{:S(2)}, u32[]{:S(2)}) %collective-permute-start.14) | collective-permute-done | bytes 1179680 | tf_op jit(solution)/shard_map/product/ppermute | solution.py:30
  111.1 3.7 %collective-permute-start.24 = (f32[768,128]{1,0:T(8,128)S(1)}, f32[768,128]{1,0:T(8,128)S(1)}, u32[]{:S(2)}, u32[]{:S(2)}) collective-permute-start(f32[768,128]{1,0:T(8,128)S(1)} %slice.38), channel_id=1, source_target_pairs={{0,8},{8,0},{16,24},{24,16},{1,9},{9,1},{17,25},{25,17},{2,10},{10... | collective-permute-start | bytes 1179656 | tf_op jit(solution)/shard_map/turned/ppermute | solution.py:342
  114.8 8.1 %next_product.5 = f32[768,384]{1,0:T(8,128)} custom-call(s32[1]{0:T(128)} %bitcast.places, bf16[768,1536]{1,0:T(8,128)(2,1)} %get-tuple-element.62.refs_0_, bf16[768,1536]{1,0:T(8,128)(2,1)} %get-tuple-element.63.refs_1_, f32[768,384]{1,0:T(8,128)} %copy-done.3, f32[768,384]{1,0:T(8,128)} %copy-done.4, f32[768,384]{1,0:T(8,128)} %copy-done.5, ...), custom_call_target="tpu_custom_call" | custom-call | flops 8000000000 | bytes 768 | tf_op jit(solution)/shard_map/total/next_product/pallas_call | solution.py:148
  123.0 1.6 collective-permute-done.24
  124.7 0.4 collective-permute-done.15
  125.1 1.4 add_add_fusion
  126.7 0.9 fusion.3
  127.6 0.8 fusion
  128.5 0.8 dynamic-slice_bitcast_fusion.2
  129.3 0.5 collective-permute-start.25
  130.2 2.6 %collective-permute-start.18 = (f32[384,384]{0,1:T(8,128)S(1)}, f32[384,384]{0,1:T(8,128)S(1)}, u32[]{:S(2)}, u32[]{:S(2)}) collective-permute-start(f32[384,384]{0,1:T(8,128)S(1)} %bitcast.70), channel_id=1, source_target_pairs={{0,8},{1,24},{8,0},{9,16},{16,9},{17,25},{24,1},{25,17},{2,10},{3,... | collective-permute-start | bytes 1769480 | tf_op jit(solution)/shard_map/out/ppermute | solution.py:365
  133.0 1.5 collective-permute-start.17
  134.5 1.0 bitcast_add_fusion
  135.6 3.2 %collective-permute-start.27 = (f32[128,640]{1,0:T(8,128)S(1)}, f32[128,640]{1,0:T(8,128)S(1)}, u32[]{:S(2)}, u32[]{:S(2)}) collective-permute-start(f32[128,640]{1,0:T(8,128)S(1)} %bitcast_add_fusion), channel_id=1, source_target_pairs={{0,96},{1,33},{32,0},{33,65},{64,32},{65,97},{96,64},{97,1},{2,98}... | collective-permute-start | bytes 983048 | tf_op jit(solution)/shard_map/quad/ppermute | solution.py:30
  138.9 5.1 %collective-permute-done.26 = f32[128,640]{1,0:T(8,128)} collective-permute-done((f32[128,640]{1,0:T(8,128)S(1)}, f32[128,640]{1,0:T(8,128)}, u32[]{:S(2)}, u32[]{:S(2)}) %collective-permute-start.26) | collective-permute-done | bytes 327712 | tf_op jit(solution)/shard_map/quad/ppermute | solution.py:30
  144.0 2.6 %collective-permute-done.27 = f32[128,640]{1,0:T(8,128)S(1)} collective-permute-done((f32[128,640]{1,0:T(8,128)S(1)}, f32[128,640]{1,0:T(8,128)S(1)}, u32[]{:S(2)}, u32[]{:S(2)}) %collective-permute-start.27) | collective-permute-done | bytes 327712 | tf_op jit(solution)/shard_map/quad/ppermute | solution.py:30
  146.6 0.7 copy-done.18
  147.3 1.1 broadcast_select_fusion.3
  148.5 0.4 convolution_subtract_fusion.1
  148.9 6.6 %collective-permute-done.28 = f32[128,640]{1,0:T(8,128)S(1)} collective-permute-done((f32[128,640]{1,0:T(8,128)}, f32[128,640]{1,0:T(8,128)S(1)}, u32[]{:S(2)}, u32[]{:S(2)}) %collective-permute-start.28) | collective-permute-done | bytes 327712 | tf_op jit(solution)/shard_map/quad/ppermute | solution.py:30
  155.5 1.8 add_add_fusion.1
  157.3 1.6 collective-permute-start.29
  158.9 5.5 %collective-permute-start.30 = (f32[128,640]{1,0:T(8,128)}, f32[128,640]{1,0:T(8,128)S(1)}, u32[]{:S(2)}, u32[]{:S(2)}) collective-permute-start(f32[128,640]{1,0:T(8,128)} %add_add_fusion.1), channel_id=1, source_target_pairs={{0,8},{1,0},{8,24},{9,16},{16,9},{17,1},{24,25},{25,17},{2,10},{3,... | collective-permute-start | bytes 983048 | tf_op jit(solution)/shard_map/quad/ppermute | solution.py:287
  164.4 2.7 %collective-permute-start.31 = (f32[128,640]{1,0:T(8,128)}, f32[128,640]{1,0:T(8,128)S(1)}, u32[]{:S(2)}, u32[]{:S(2)}) collective-permute-start(f32[128,640]{1,0:T(8,128)} %add_add_fusion.1), channel_id=1, source_target_pairs={{0,16},{1,24},{8,0},{9,8},{16,17},{17,25},{24,1},{25,9},{2,18},{3,... | collective-permute-start | bytes 983048 | tf_op jit(solution)/shard_map/quad/ppermute | solution.py:287
  167.1 1.9 %collective-permute-start.32 = (f32[128,640]{1,0:T(8,128)}, f32[128,640]{1,0:T(8,128)S(1)}, u32[]{:S(2)}, u32[]{:S(2)}) collective-permute-start(f32[128,640]{1,0:T(8,128)} %add_add_fusion.1), channel_id=1, source_target_pairs={{0,24},{1,16},{8,8},{9,0},{16,25},{17,17},{24,9},{25,1},{2,26},{3,... | collective-permute-start | bytes 983048 | tf_op jit(solution)/shard_map/quad/ppermute | solution.py:287
  169.1 0.4 convolution_subtract_fusion
  169.6 1.1 copy.28
  170.7 0.9 copy.27
  171.7 8.9 %collective-permute-done.31.refs_2_ = f32[128,640]{1,0:T(8,128)S(1)} collective-permute-done((f32[128,640]{1,0:T(8,128)}, f32[128,640]{1,0:T(8,128)S(1)}, u32[]{:S(2)}, u32[]{:S(2)}) %collective-permute-start.31) | collective-permute-done | bytes 327712 | tf_op jit(solution)/shard_map/quad/ppermute | solution.py:287
  180.5 2.4 %finish.1 = (f32[1,256,256]{2,1,0:T(8,128)}, f32[2,256,256]{2,1,0:T(8,128)}, f32[2,256,256]{2,1,0:T(8,128)}) custom-call(s32[4]{0:T(128)S(1)} %pad_add_fusion.z, f32[128,640]{1,0:T(8,128)S(1)} %collective-permute-done.29.refs_0_, f32[128,640]{1,0:T(8,128)S(1)} %collective-permute-done.30.refs_1_, f32[128,640]{1,0:T(8,128)S(1)} %collective-permute-done.31.refs_2_, ...), custom_call_target="tpu_custom_call" | custom-call | flops 100000000 | bytes 1000000 | tf_op jit(solution)/shard_map/diag/finish/pallas_call | solution.py:203
  (89 shorter events, 3.3 us)
Async XLA Ops:
  0.6 3.2 %copy-start.17 = (f32[768,128]{1,0:T(8,128)S(1)}, f32[768,128]{1,0:T(8,128)}, u32[]{:S(2)}) copy-start(f32[768,128]{1,0:T(8,128)} %param.9) | copy-start | bytes 1179652
  0.6 3.4 %copy-start.16 = (f32[768,256]{1,0:T(8,128)S(1)}, f32[768,256]{1,0:T(8,128)}, u32[]{:S(2)}) copy-start(f32[768,256]{1,0:T(8,128)} %param.10) | copy-start | bytes 2359300
  2.9 2.3 %collective-permute-start = (f32[192,768]{1,0:T(8,128)}, f32[192,768]{1,0:T(8,128)}, u32[]{:S(2)}, u32[]{:S(2)}) collective-permute-start(f32[192,768]{1,0:T(8,128)} %get-tuple-element.100), channel_id=1, source_target_pairs={{0,1},{1,0},{2,3},{3,2},{4,5},{5,4},{6,7},{7,6},{8,9},{9,8},{10,11... | collective-permute-start | bytes 1769480 | tf_op jit(solution)/shard_map/gather/ppermute | solution.py:22
  4.3 8.1 %copy-start.3 = (f32[768,384]{1,0:T(8,128)}, f32[768,384]{1,0:T(8,128)S(1)}, u32[]{:S(2)}) copy-start(f32[768,384]{1,0:T(8,128)S(1)} %pad_maximum_fusion.1.refs_4_.refs_2_) | copy-start | bytes 3538948
  5.2 2.8 %collective-permute-start.5 = (f32[768,384]{1,0:T(8,128)S(1)}, f32[768,384]{1,0:T(8,128)S(1)}, u32[]{:S(2)}, u32[]{:S(2)}) collective-permute-start(f32[768,384]{1,0:T(8,128)S(1)} %pad_maximum_fusion.1.refs_4_.refs_2_), channel_id=1, source_target_pairs={{0,1},{1,0},{2,3},{3,2},{4,5},{5,4},{6,7},{7,6},{8,9},{9,8},{10,11... | collective-permute-start | bytes 3538952 | tf_op jit(solution)/shard_map/gather/ppermute | solution.py:22
  6.5 9.6 %copy-start.11 = (f32[2,192,768]{2,1,0:T(8,128)}, f32[2,192,768]{2,1,0:T(8,128)S(1)}, u32[]{:S(2)}) copy-start(f32[2,192,768]{2,1,0:T(8,128)S(1)} %pad_maximum_fusion.refs_0_) | copy-start | bytes 3538948
  8.1 1.0 copy-start.4
  9.2 55.4 %copy-start.9 = (f32[4,192,384]{2,1,0:T(8,128)}, f32[4,192,384]{2,1,0:T(8,128)S(1)}, u32[]{:S(2)}) copy-start(f32[4,192,384]{2,1,0:T(8,128)S(1)} %pad_maximum_fusion.2) | copy-start | bytes 3538948
  9.2 17.5 %collective-permute-start.6 = (f32[768,384]{1,0:T(8,128)S(1)}, f32[768,384]{1,0:T(8,128)S(1)}, u32[]{:S(2)}, u32[]{:S(2)}) collective-permute-start(f32[768,384]{1,0:T(8,128)S(1)} %bitcast.61), channel_id=1, source_target_pairs={{0,2},{1,7},{2,4},{3,1},{4,6},{5,3},{6,0},{7,5},{8,10},{9,15},{10,... | collective-permute-start | bytes 3538952 | tf_op jit(solution)/shard_map/gather/ppermute | solution.py:30
  10.9 27.2 %collective-permute-start.3 = (f32[768,384]{1,0:T(8,128)S(1)}, f32[768,384]{1,0:T(8,128)S(1)}, u32[]{:S(2)}, u32[]{:S(2)}) collective-permute-start(f32[768,384]{1,0:T(8,128)S(1)} %pad_maximum_fusion.1.refs_4_.refs_2_), channel_id=1, source_target_pairs={{0,32},{1,97},{32,64},{33,1},{64,96},{65,33},{96,0},{97,65},{2,34}... | collective-permute-start | bytes 3538952 | tf_op jit(solution)/shard_map/gather/ppermute | solution.py:30
  12.4 28.0 %collective-permute-start.4 = (f32[768,384]{1,0:T(8,128)S(1)}, f32[768,384]{1,0:T(8,128)S(1)}, u32[]{:S(2)}, u32[]{:S(2)}) collective-permute-start(f32[768,384]{1,0:T(8,128)S(1)} %pad_maximum_fusion.1.refs_4_.refs_2_), channel_id=1, source_target_pairs={{0,96},{1,33},{32,0},{33,65},{64,32},{65,97},{96,64},{97,1},{2,98}... | collective-permute-start | bytes 3538952 | tf_op jit(solution)/shard_map/gather/ppermute | solution.py:30
  14.2 28.3 %collective-permute-start.1 = (f32[2,192,768]{2,1,0:T(8,128)S(1)}, f32[2,192,768]{2,1,0:T(8,128)S(1)}, u32[]{:S(2)}, u32[]{:S(2)}) collective-permute-start(f32[2,192,768]{2,1,0:T(8,128)S(1)} %pad_maximum_fusion.refs_0_), channel_id=1, source_target_pairs={{0,8},{1,25},{8,16},{9,1},{16,24},{17,9},{24,0},{25,17},{2,10},{3,... | collective-permute-start | bytes 3538952 | tf_op jit(solution)/shard_map/gather/ppermute | solution.py:30
  16.1 28.0 %collective-permute-start.2 = (f32[2,192,768]{2,1,0:T(8,128)S(1)}, f32[2,192,768]{2,1,0:T(8,128)S(1)}, u32[]{:S(2)}, u32[]{:S(2)}) collective-permute-start(f32[2,192,768]{2,1,0:T(8,128)S(1)} %pad_maximum_fusion.refs_0_), channel_id=1, source_target_pairs={{0,24},{1,9},{8,0},{9,17},{16,8},{17,25},{24,16},{25,1},{2,26},{3,... | collective-permute-start | bytes 3538952 | tf_op jit(solution)/shard_map/gather/ppermute | solution.py:30
  26.7 38.0 %copy-start.20 = (f32[768,384]{1,0:T(8,128)}, f32[768,384]{1,0:T(8,128)S(1)}, u32[]{:S(2)}) copy-start(f32[768,384]{1,0:T(8,128)S(1)} %collective-permute-done.6) | copy-start | bytes 3538948
  26.7 17.5 %collective-permute-start.7 = (f32[768,384]{1,0:T(8,128)S(1)}, f32[768,384]{1,0:T(8,128)}, u32[]{:S(2)}, u32[]{:S(2)}) collective-permute-start(f32[768,384]{1,0:T(8,128)S(1)} %bitcast.62), channel_id=1, source_target_pairs={{0,6},{1,3},{2,0},{3,5},{4,2},{5,7},{6,4},{7,1},{8,14},{9,11},{10,... | collective-permute-start | bytes 3538952 | tf_op jit(solution)/shard_map/gather/ppermute | solution.py:30
  38.1 34.6 %copy-start.5 = (f32[768,384]{1,0:T(8,128)}, f32[768,384]{1,0:T(8,128)S(1)}, u32[]{:S(2)}) copy-start(f32[768,384]{1,0:T(8,128)S(1)} %collective-permute-done.3.refs_6_.refs_4_) | copy-start | bytes 3538948
  40.4 32.4 %copy-start.6 = (f32[768,384]{1,0:T(8,128)}, f32[768,384]{1,0:T(8,128)S(1)}, u32[]{:S(2)}) copy-start(f32[768,384]{1,0:T(8,128)S(1)} %collective-permute-done.4.refs_8_.refs_6_) | copy-start | bytes 3538948
  42.4 22.2 %copy-start.12 = (f32[2,192,768]{2,1,0:T(8,128)}, f32[2,192,768]{2,1,0:T(8,128)S(1)}, u32[]{:S(2)}) copy-start(f32[2,192,768]{2,1,0:T(8,128)S(1)} %collective-permute-done.1.refs_1_) | copy-start | bytes 3538948
  44.1 1.1 copy-start.13
  45.3 3.2 %collective-permute-start.10 = (f32[768,384]{1,0:T(8,128)S(1)}, f32[768,384]{1,0:T(8,128)S(1)}, u32[]{:S(2)}, u32[]{:S(2)}) collective-permute-start(f32[768,384]{1,0:T(8,128)S(1)} %collective-permute-done.4.refs_8_.refs_6_), channel_id=1, source_target_pairs={{0,1},{1,0},{2,3},{3,2},{4,5},{5,4},{6,7},{7,6},{8,9},{9,8},{10,11... | collective-permute-start | bytes 3538952 | tf_op jit(solution)/shard_map/gather/ppermute | solution.py:22
  46.0 4.2 %collective-permute-start.11 = (f32[768,384]{1,0:T(8,128)S(1)}, f32[768,384]{1,0:T(8,128)S(1)}, u32[]{:S(2)}, u32[]{:S(2)}) collective-permute-start(f32[768,384]{1,0:T(8,128)S(1)} %collective-permute-done.3.refs_6_.refs_4_), channel_id=1, source_target_pairs={{0,1},{1,0},{2,3},{3,2},{4,5},{5,4},{6,7},{7,6},{8,9},{9,8},{10,11... | collective-permute-start | bytes 3538952 | tf_op jit(solution)/shard_map/gather/ppermute | solution.py:22
  46.0 17.7 %collective-permute-start.8 = (f32[2,192,768]{2,1,0:T(8,128)S(1)}, f32[2,192,768]{2,1,0:T(8,128)S(1)}, u32[]{:S(2)}, u32[]{:S(2)}) collective-permute-start(f32[2,192,768]{2,1,0:T(8,128)S(1)} %collective-permute-done.1.refs_1_), channel_id=1, source_target_pairs={{0,8},{1,25},{8,16},{9,1},{16,24},{17,9},{24,0},{25,17},{2,10},{3,... | collective-permute-start | bytes 3538952 | tf_op jit(solution)/shard_map/gather/ppermute | solution.py:30
  46.3 17.5 %collective-permute-start.9 = (f32[768,384]{1,0:T(8,128)S(1)}, f32[768,384]{1,0:T(8,128)}, u32[]{:S(2)}, u32[]{:S(2)}) collective-permute-start(f32[768,384]{1,0:T(8,128)S(1)} %collective-permute-done.3.refs_6_.refs_4_), channel_id=1, source_target_pairs={{0,32},{1,97},{32,64},{33,1},{64,96},{65,33},{96,0},{97,65},{2,34}... | collective-permute-start | bytes 3538952 | tf_op jit(solution)/shard_map/gather/ppermute | solution.py:30
  47.0 17.6 %collective-permute-start.19 = (f32[768,384]{1,0:T(8,128)S(1)}, f32[768,384]{1,0:T(8,128)}, u32[]{:S(2)}, u32[]{:S(2)}) collective-permute-start(f32[768,384]{1,0:T(8,128)S(1)} %collective-permute-done.6), channel_id=1, source_target_pairs={{0,2},{1,7},{2,4},{3,1},{4,6},{5,3},{6,0},{7,5},{8,10},{9,15},{10,... | collective-permute-start | bytes 3538952 | tf_op jit(solution)/shard_map/gather/ppermute | solution.py:30
  48.4 24.3 %copy-start.7 = (f32[768,384]{1,0:T(8,128)}, f32[768,384]{1,0:T(8,128)S(1)}, u32[]{:S(2)}) copy-start(f32[768,384]{1,0:T(8,128)S(1)} %collective-permute-done.10.refs_7_.refs_5_) | copy-start | bytes 3538948
  50.1 13.7 %copy-start.8 = (f32[768,384]{1,0:T(8,128)}, f32[768,384]{1,0:T(8,128)S(1)}, u32[]{:S(2)}) copy-start(f32[768,384]{1,0:T(8,128)S(1)} %collective-permute-done.11.refs_9_.refs_7_) | copy-start | bytes 3538948
  63.6 1.0 copy-start.14
  63.8 8.9 %collective-permute-start.12 = (f32[768,384]{1,0:T(8,128)}, f32[768,384]{1,0:T(8,128)}, u32[]{:S(2)}, u32[]{:S(2)}) collective-permute-start(f32[768,384]{1,0:T(8,128)} %collective-permute-done.9.refs_10_.refs_8_), channel_id=1, source_target_pairs={{0,1},{1,0},{2,3},{3,2},{4,5},{5,4},{6,7},{7,6},{8,9},{9,8},{10,11... | collective-permute-start | bytes 3538952 | tf_op jit(solution)/shard_map/gather/ppermute | solution.py:22
  64.7 29.0 %collective-permute-start.20 = (f32[768,384]{1,0:T(8,128)}, f32[768,384]{1,0:T(8,128)}, u32[]{:S(2)}, u32[]{:S(2)}) collective-permute-start(f32[768,384]{1,0:T(8,128)} %collective-permute-done.19), channel_id=1, source_target_pairs={{0,32},{1,97},{34,66},{35,3},{68,100},{69,37},{102,6},{103,71},{8,... | collective-permute-start | bytes 3538952 | tf_op jit(solution)/shard_map/product/ppermute | solution.py:307
  69.6 41.2 %collective-permute-start.22 = (f32[768,384]{1,0:T(8,128)}, f32[768,384]{1,0:T(8,128)}, u32[]{:S(2)}, u32[]{:S(2)}) collective-permute-start(f32[768,384]{1,0:T(8,128)} %copy-done.20), channel_id=1, source_target_pairs={{0,96},{1,33},{34,2},{35,67},{68,36},{69,101},{102,70},{103,7},{8,... | collective-permute-start | bytes 3538952 | tf_op jit(solution)/shard_map/product/ppermute | solution.py:307
  82.1 23.1 %collective-permute-start.13 = (f32[768,384]{1,0:T(8,128)}, f32[768,384]{1,0:T(8,128)S(1)}, u32[]{:S(2)}, u32[]{:S(2)}) collective-permute-start(f32[768,384]{1,0:T(8,128)} %get-tuple-element.56), channel_id=1, source_target_pairs={{0,2},{1,7},{2,4},{3,1},{4,6},{5,3},{6,0},{7,5},{8,10},{9,15},{10,... | collective-permute-start | bytes 3538952 | tf_op jit(solution)/shard_map/product/ppermute | solution.py:30
  90.4 20.4 %collective-permute-start.14 = (f32[768,384]{1,0:T(8,128)}, f32[768,384]{1,0:T(8,128)}, u32[]{:S(2)}, u32[]{:S(2)}) collective-permute-start(f32[768,384]{1,0:T(8,128)} %next_product.3), channel_id=1, source_target_pairs={{0,6},{1,3},{2,0},{3,5},{4,2},{5,7},{6,4},{7,1},{8,14},{9,11},{10,... | collective-permute-start | bytes 3538952 | tf_op jit(solution)/shard_map/product/ppermute | solution.py:30
  93.6 17.1 %collective-permute-start.21 = (f32[768,384]{1,0:T(8,128)}, f32[768,384]{1,0:T(8,128)S(1)}, u32[]{:S(2)}, u32[]{:S(2)}) collective-permute-start(f32[768,384]{1,0:T(8,128)} %collective-permute-done.20), channel_id=1, source_target_pairs={{32,64},{97,65},{66,98},{3,99},{100,4},{37,5},{6,38},{71,39},{40,7... | collective-permute-start | bytes 3538952 | tf_op jit(solution)/shard_map/product/ppermute | solution.py:307
  94.4 16.5 %collective-permute-start.23 = (f32[768,384]{1,0:T(8,128)}, f32[768,384]{1,0:T(8,128)S(1)}, u32[]{:S(2)}, u32[]{:S(2)}) collective-permute-start(f32[768,384]{1,0:T(8,128)} %collective-permute-done.7), channel_id=1, source_target_pairs={{0,32},{1,97},{34,66},{35,3},{68,100},{69,37},{102,6},{103,71},{8,... | collective-permute-start | bytes 3538952 | tf_op jit(solution)/shard_map/product/ppermute | solution.py:307
  105.2 5.7 %copy-start.10 = (f32[4,192,384]{2,1,0:T(8,128)S(1)}, f32[4,192,384]{2,1,0:T(8,128)}, u32[]{:S(2)}) copy-start(f32[4,192,384]{2,1,0:T(8,128)} %copy-done.9) | copy-start | bytes 3538948
  106.7 18.4 %collective-permute-start.15 = (f32[768,384]{1,0:T(8,128)S(1)}, f32[768,384]{1,0:T(8,128)S(1)}, u32[]{:S(2)}, u32[]{:S(2)}) collective-permute-start(f32[768,384]{1,0:T(8,128)S(1)} %add.151), channel_id=1, source_target_pairs={{0,2},{1,7},{2,4},{3,1},{4,6},{5,3},{6,0},{7,5},{8,10},{9,15},{10,... | collective-permute-start | bytes 3538952 | tf_op jit(solution)/shard_map/product/ppermute | solution.py:30
  111.1 13.5 %collective-permute-start.24 = (f32[768,128]{1,0:T(8,128)S(1)}, f32[768,128]{1,0:T(8,128)S(1)}, u32[]{:S(2)}, u32[]{:S(2)}) collective-permute-start(f32[768,128]{1,0:T(8,128)S(1)} %slice.38), channel_id=1, source_target_pairs={{0,8},{8,0},{16,24},{24,16},{1,9},{9,1},{17,25},{25,17},{2,10},{10... | collective-permute-start | bytes 1179656 | tf_op jit(solution)/shard_map/turned/ppermute | solution.py:342
  123.0 2.1 %copy-start.15 = (f32[768,384]{1,0:T(8,128)S(1)}, f32[768,384]{1,0:T(8,128)}, u32[]{:S(2)}) copy-start(f32[768,384]{1,0:T(8,128)} %next_product.5) | copy-start | bytes 3538948
  126.6 3.1 %collective-permute-start.16 = (f32[384,384]{1,0:T(8,128)S(1)}, f32[384,384]{1,0:T(8,128)S(1)}, u32[]{:S(2)}, u32[]{:S(2)}) collective-permute-start(f32[384,384]{1,0:T(8,128)S(1)} %get-tuple-element.97), channel_id=1, source_target_pairs={{0,1},{1,0},{2,3},{3,2},{4,5},{5,4},{6,7},{7,6},{8,9},{9,8},{10,11... | collective-permute-start | bytes 1769480 | tf_op jit(solution)/shard_map/out/ppermute | solution.py:22
  129.3 5.2 %collective-permute-start.25 = (f32[128,640]{1,0:T(8,128)}, f32[128,640]{1,0:T(8,128)}, u32[]{:S(2)}, u32[]{:S(2)}) collective-permute-start(f32[128,640]{1,0:T(8,128)} %dynamic-slice_bitcast_fusion.2), channel_id=1, source_target_pairs={{0,1},{1,0},{2,3},{3,2},{4,5},{5,4},{6,7},{7,6},{8,9},{9,8},{10,11... | collective-permute-start | bytes 983048 | tf_op jit(solution)/shard_map/quad/ppermute | solution.py:22
  130.2 16.4 %collective-permute-start.18 = (f32[384,384]{0,1:T(8,128)S(1)}, f32[384,384]{0,1:T(8,128)S(1)}, u32[]{:S(2)}, u32[]{:S(2)}) collective-permute-start(f32[384,384]{0,1:T(8,128)S(1)} %bitcast.70), channel_id=1, source_target_pairs={{0,8},{1,24},{8,0},{9,16},{16,9},{17,25},{24,1},{25,17},{2,10},{3,... | collective-permute-start | bytes 1769480 | tf_op jit(solution)/shard_map/out/ppermute | solution.py:365
  133.0 14.3 %collective-permute-start.17 = (f32[384,384]{0,1:T(8,128)S(1)}, f32[384,384]{0,1:T(8,128)}, u32[]{:S(2)}, u32[]{:S(2)}) collective-permute-start(f32[384,384]{0,1:T(8,128)S(1)} %bitcast.69), channel_id=1, source_target_pairs={{0,0},{1,16},{8,8},{9,24},{16,1},{17,17},{24,9},{25,25},{2,2},{3,1... | collective-permute-start | bytes 1769480 | tf_op jit(solution)/shard_map/out/ppermute | solution.py:365
  135.5 8.5 %collective-permute-start.26 = (f32[128,640]{1,0:T(8,128)S(1)}, f32[128,640]{1,0:T(8,128)}, u32[]{:S(2)}, u32[]{:S(2)}) collective-permute-start(f32[128,640]{1,0:T(8,128)S(1)} %bitcast_add_fusion), channel_id=1, source_target_pairs={{0,32},{1,97},{32,64},{33,1},{64,96},{65,33},{96,0},{97,65},{2,34}... | collective-permute-start | bytes 983048 | tf_op jit(solution)/shard_map/quad/ppermute | solution.py:30
  135.6 10.9 %collective-permute-start.27 = (f32[128,640]{1,0:T(8,128)S(1)}, f32[128,640]{1,0:T(8,128)S(1)}, u32[]{:S(2)}, u32[]{:S(2)}) collective-permute-start(f32[128,640]{1,0:T(8,128)S(1)} %bitcast_add_fusion), channel_id=1, source_target_pairs={{0,96},{1,33},{32,0},{33,65},{64,32},{65,97},{96,64},{97,1},{2,98}... | collective-permute-start | bytes 983048 | tf_op jit(solution)/shard_map/quad/ppermute | solution.py:30
  138.9 9.6 %copy-start = (f32[2,256,256]{2,1,0:T(8,128)S(1)}, f32[2,256,256]{2,1,0:T(8,128)}, u32[]{:S(2)}) copy-start(f32[2,256,256]{2,1,0:T(8,128)} %refs_4_.1) | copy-start | bytes 1572868
  146.6 0.7 copy-start.18
  146.6 9.0 %collective-permute-start.28 = (f32[128,640]{1,0:T(8,128)}, f32[128,640]{1,0:T(8,128)S(1)}, u32[]{:S(2)}, u32[]{:S(2)}) collective-permute-start(f32[128,640]{1,0:T(8,128)} %collective-permute-done.26), channel_id=1, source_target_pairs={{0,32},{1,97},{32,64},{33,1},{64,96},{65,33},{96,0},{97,65},{2,34}... | collective-permute-start | bytes 983048 | tf_op jit(solution)/shard_map/quad/ppermute | solution.py:30
  148.4 7.1 %copy-start.19 = (f32[128,640]{1,0:T(8,128)S(1)}, f32[128,640]{1,0:T(8,128)}, u32[]{:S(2)}) copy-start(f32[128,640]{1,0:T(8,128)} %copy-done.18) | copy-start | bytes 983044
  157.3 14.3 %collective-permute-start.29 = (f32[128,640]{1,0:T(8,128)}, f32[128,640]{1,0:T(8,128)S(1)}, u32[]{:S(2)}, u32[]{:S(2)}) collective-permute-start(f32[128,640]{1,0:T(8,128)} %add_add_fusion.1), channel_id=1, source_target_pairs={{0,0},{1,8},{8,16},{9,24},{16,1},{17,9},{24,17},{25,25},{2,2},{3,1... | collective-permute-start | bytes 983048 | tf_op jit(solution)/shard_map/quad/ppermute | solution.py:287
  158.9 12.7 %collective-permute-start.30 = (f32[128,640]{1,0:T(8,128)}, f32[128,640]{1,0:T(8,128)S(1)}, u32[]{:S(2)}, u32[]{:S(2)}) collective-permute-start(f32[128,640]{1,0:T(8,128)} %add_add_fusion.1), channel_id=1, source_target_pairs={{0,8},{1,0},{8,24},{9,16},{16,9},{17,1},{24,25},{25,17},{2,10},{3,... | collective-permute-start | bytes 983048 | tf_op jit(solution)/shard_map/quad/ppermute | solution.py:287
  164.4 16.1 %collective-permute-start.31 = (f32[128,640]{1,0:T(8,128)}, f32[128,640]{1,0:T(8,128)S(1)}, u32[]{:S(2)}, u32[]{:S(2)}) collective-permute-start(f32[128,640]{1,0:T(8,128)} %add_add_fusion.1), channel_id=1, source_target_pairs={{0,16},{1,24},{8,0},{9,8},{16,17},{17,25},{24,1},{25,9},{2,18},{3,... | collective-permute-start | bytes 983048 | tf_op jit(solution)/shard_map/quad/ppermute | solution.py:287
  167.1 13.4 %collective-permute-start.32 = (f32[128,640]{1,0:T(8,128)}, f32[128,640]{1,0:T(8,128)S(1)}, u32[]{:S(2)}, u32[]{:S(2)}) collective-permute-start(f32[128,640]{1,0:T(8,128)} %add_add_fusion.1), channel_id=1, source_target_pairs={{0,24},{1,16},{8,8},{9,0},{16,25},{17,17},{24,9},{25,1},{2,26},{3,... | collective-permute-start | bytes 983048 | tf_op jit(solution)/shard_map/quad/ppermute | solution.py:287
  170.7 9.8 %copy-start.1 = (f32[2,256,256]{2,1,0:T(8,128)S(1)}, f32[2,256,256]{2,1,0:T(8,128)}, u32[]{:S(2)}) copy-start(f32[2,256,256]{2,1,0:T(8,128)} %refs_6_.1) | copy-start | bytes 1572868
  170.7 9.8 %copy-start.2 = (f32[1,256,256]{2,1,0:T(8,128)S(1)}, f32[1,256,256]{2,1,0:T(8,128)}, u32[]{:S(2)}) copy-start(f32[1,256,256]{2,1,0:T(8,128)} %refs_5_.1) | copy-start | bytes 786436

commit v3 on v2

--- a/solution.py
+++ b/solution.py
@@ -277,8 +277,8 @@
         a_far, l_far = send(a_first, "z", 1), send(l_first, "x", 1)
         t_far = send(after(t_first, t_second), "y", 1)
         first_other, second_other = swap(l_second), swap(l_first)
-        a_far, l_far, first_other, second_other = lax.optimization_barrier(
-            (a_far, l_far, first_other, second_other)
+        a_far, l_far, t_far, first_other, second_other = lax.optimization_barrier(
+            (a_far, l_far, t_far, first_other, second_other)
         )
         far_other = swap(l_far)
 
@@ -330,7 +330,6 @@
         last_came = send(last, "y", 1)
     with jax.named_scope("turned"):
         shift = (x - y) % 4
-        q_far = after(q_far, near_came)
         turned = jnp.where(
             shift == 0,
             source,
@@ -344,7 +343,7 @@
             (jnp.where(z % 2 == 0, own, mate), jnp.where(z % 2 == 0, mate, own)), axis=1
         )
     with jax.named_scope("total"):
-        rest = product([strip_of(0)], [after(p, last) for p in parts], strips, True)
+        rest = product([strip_of(0)], [after(p, last, turned, near_came) for p in parts], strips, True)
         rest, near_came, last_came = lax.optimization_barrier((rest, near_came, last_came))
         total = rest + near_came + last_came
     with jax.named_scope("out"):
@@ -373,7 +372,7 @@
         quad = quad.reshape(2, BLOCK // 2, wide)
         quad = pick(quad, core) + swap(pick(quad, 1 - core))
         first, second = send(quad, "x", 1), send(quad, "x", -1)
-        around = quad + first + second + send(after(first, second, pieces[1]), "x", 1)
+        around = quad + first + second + send(after(first, pieces[1]), "x", 1)
         around = after(around, pieces[0])
         came = spread([around] * 4)
     with jax.named_scope("out"):

time: 183 us -> 183 us (level)
  waiting for transfers between devices: 71.2 us -> 75.1 us
  starting transfers between devices: 52.5 us -> 49.4 us
    ppermute x15, waiting for transfers between devices: 56.3 us -> 63.7 us  [send(): return lax.ppermute(value, (axis, 'core'), split_pairs(step))]
    ppermute x1, starting transfers between devices: 3.7 us -> 0.44 us  [local(): mate = lax.ppermute(own, 'z', [(0, 1), (1, 0), (2, 3), (3, 2)])]
    unnamed x44 -> x38, local copies, waits for them, and re-layouts: 4.86 us -> 5.09 us
  transfers between devices with their start and end apart: 33 -> 33, of which waited for: 18 -> 14; matrix products, arithmetic and copies ran while one was open for 7% -> 7% of each run, Pallas kernels for 18% -> 19%
where the time goes in v3:
time: 183 us; the launch traced here: 182 us
  waiting for transfers between devices  75.1 us (41%)
  starting transfers between devices  49.4 us (27%)
  Pallas kernels  36.2 us (20%)
  local copies, waits for them, and re-layouts  9.49 us (5%)
  other arithmetic  8.24 us (5%)
  matrix products  2.56 us (1%)
    ppermute x15, waiting for transfers between devices, send(): return lax.ppermute(value, (axis, 'core'), split_pairs(step))  63.7 us
    pallas_call x4, Pallas kernels, product(): pl.pallas_call(first_kernel if first else next_kernel, out_shape=[parts,...  33.8 us
    ppermute x15, starting transfers between devices, send(): return lax.ppermute(value, (axis, 'core'), split_pairs(step))  21.5 us
    ppermute x4, starting transfers between devices, spread(): lax.ppermute(value, ('z', 'core'), [((2 * c + j) * 2 + h, (2 * j + h ^ tu...  12.4 us
    ppermute x4, starting transfers between devices, turn(): return lax.ppermute(value, ('x', 'y', 'core'), pairs)  10.7 us
    ppermute x4, waiting for transfers between devices, spread(): lax.ppermute(value, ('z', 'core'), [((2 * c + j) * 2 + h, (2 * j + h ^ tu...  8.88 us
    unnamed x38, local copies, waits for them, and re-layouts  5.09 us
  transfers between devices with their start and end apart: 33, of which 14 were waited for; matrix products, arithmetic and copies ran while one was open for 7% of the time, Pallas kernels for 19%

profile of v3, /device:TPU:0, one launch (start us, length us, event | category | flops | bytes accessed | tf_op | source)
XLA Modules:
  0.0 182.1 jit_solution(9761962314029000888)
XLA Ops:
  0.7 2.2 %constant_dynamic-slice_fusion.1 = (f32[1,192,768]{2,1,0:T(8,128)S(1)}, f32[192,768]{1,0:T(8,128)}) fusion(f32[2,192,768]{2,1,0:T(8,128)} %bitcast.67, s32[]{:T(128)S(6)} %select_n.238, s32[]{:T(128)S(6)} %select_n.239), kind=kLoop, calls=%fused_computation.45 | loop fusion | bytes 2359304 | tf_op jit(solution)/shard_map/gather/jit(dynamic_index_in_dim)/dynamic_slice | solution.py:38
  2.9 0.8 convert_bitcast_fusion.1
  3.8 0.2 broadcast_multiply_fusion.1
  4.0 0.2 broadcast_multiply_fusion
  4.3 0.9 collective-permute-done
  5.4 1.1 pad_maximum_fusion.refs_0_
  6.5 1.6 collective-permute-done.5.refs_5_.refs_3_
  8.2 0.9 copy-done.4
  9.2 1.7 collective-permute-start.6
  10.9 1.5 collective-permute-start.3
  12.4 1.7 collective-permute-start.4
  14.2 1.9 %collective-permute-start.1 = (f32[2,192,768]{2,1,0:T(8,128)S(1)}, f32[2,192,768]{2,1,0:T(8,128)S(1)}, u32[]{:S(2)}, u32[]{:S(2)}) collective-permute-start(f32[2,192,768]{2,1,0:T(8,128)S(1)} %pad_maximum_fusion.refs_0_), channel_id=1, source_target_pairs={{0,8},{1,25},{8,16},{9,1},{16,24},{17,9},{24,0},{25,17},{2,10},{3,... | collective-permute-start | bytes 3538952 | tf_op jit(solution)/shard_map/gather/ppermute | solution.py:30
  16.1 2.1 %collective-permute-start.2 = (f32[2,192,768]{2,1,0:T(8,128)S(1)}, f32[2,192,768]{2,1,0:T(8,128)S(1)}, u32[]{:S(2)}, u32[]{:S(2)}) collective-permute-start(f32[2,192,768]{2,1,0:T(8,128)S(1)} %pad_maximum_fusion.refs_0_), channel_id=1, source_target_pairs={{0,24},{1,9},{8,0},{9,17},{16,8},{17,25},{24,16},{25,1},{2,26},{3,... | collective-permute-start | bytes 3538952 | tf_op jit(solution)/shard_map/gather/ppermute | solution.py:30
  18.2 8.6 %collective-permute-done.6 = f32[768,384]{1,0:T(8,128)} collective-permute-done((f32[768,384]{1,0:T(8,128)S(1)}, f32[768,384]{1,0:T(8,128)}, u32[]{:S(2)}, u32[]{:S(2)}) %collective-permute-start.6) | collective-permute-done | bytes 1179680 | tf_op jit(solution)/shard_map/gather/ppermute | solution.py:30
  26.8 1.9 %collective-permute-start.7 = (f32[768,384]{1,0:T(8,128)S(1)}, f32[768,384]{1,0:T(8,128)}, u32[]{:S(2)}, u32[]{:S(2)}) collective-permute-start(f32[768,384]{1,0:T(8,128)S(1)} %bitcast.62), channel_id=1, source_target_pairs={{0,6},{1,3},{2,0},{3,5},{4,2},{5,7},{6,4},{7,1},{8,14},{9,11},{10,... | collective-permute-start | bytes 3538952 | tf_op jit(solution)/shard_map/gather/ppermute | solution.py:30
  28.7 9.4 %collective-permute-done.3.refs_6_.refs_4_ = f32[768,384]{1,0:T(8,128)S(1)} collective-permute-done((f32[768,384]{1,0:T(8,128)S(1)}, f32[768,384]{1,0:T(8,128)S(1)}, u32[]{:S(2)}, u32[]{:S(2)}) %collective-permute-start.3) | collective-permute-done | bytes 1179680 | tf_op jit(solution)/shard_map/gather/ppermute | solution.py:30
  38.1 2.3 %collective-permute-done.4.refs_8_.refs_6_ = f32[768,384]{1,0:T(8,128)S(1)} collective-permute-done((f32[768,384]{1,0:T(8,128)S(1)}, f32[768,384]{1,0:T(8,128)S(1)}, u32[]{:S(2)}, u32[]{:S(2)}) %collective-permute-start.4) | collective-permute-done | bytes 1179680 | tf_op jit(solution)/shard_map/gather/ppermute | solution.py:30
  40.4 2.1 %collective-permute-done.1.refs_1_ = f32[2,192,768]{2,1,0:T(8,128)S(1)} collective-permute-done((f32[2,192,768]{2,1,0:T(8,128)S(1)}, f32[2,192,768]{2,1,0:T(8,128)S(1)}, u32[]{:S(2)}, u32[]{:S(2)}) %collective-permute-start.1) | collective-permute-done | bytes 1179680 | tf_op jit(solution)/shard_map/gather/ppermute | solution.py:30
  42.4 1.7 collective-permute-done.2.refs_2_
  44.1 2.5 %collective-permute-start.10 = (f32[768,384]{1,0:T(8,128)}, f32[768,384]{1,0:T(8,128)}, u32[]{:S(2)}, u32[]{:S(2)}) collective-permute-start(f32[768,384]{1,0:T(8,128)} %collective-permute-done.6), channel_id=1, source_target_pairs={{0,2},{1,7},{2,4},{3,1},{4,6},{5,3},{6,0},{7,5},{8,10},{9,15},{10,... | collective-permute-start | bytes 3538952 | tf_op jit(solution)/shard_map/gather/ppermute | solution.py:30
  46.7 0.5 collective-permute-start.12
  47.2 0.3 collective-permute-start.9
  47.5 14.4 %collective-permute-done.10 = f32[768,384]{1,0:T(8,128)} collective-permute-done((f32[768,384]{1,0:T(8,128)}, f32[768,384]{1,0:T(8,128)}, u32[]{:S(2)}, u32[]{:S(2)}) %collective-permute-start.10) | collective-permute-done | bytes 1179680 | tf_op jit(solution)/shard_map/gather/ppermute | solution.py:30
  61.9 2.7 %collective-permute-done.8.refs_3_ = f32[2,192,768]{2,1,0:T(8,128)S(1)} collective-permute-done((f32[2,192,768]{2,1,0:T(8,128)S(1)}, f32[2,192,768]{2,1,0:T(8,128)S(1)}, u32[]{:S(2)}, u32[]{:S(2)}) %collective-permute-start.8) | collective-permute-done | bytes 1179680 | tf_op jit(solution)/shard_map/gather/ppermute | solution.py:30
  64.7 0.9 copy-done.14
  65.6 3.1 %collective-permute-start.15 = (f32[768,384]{1,0:T(8,128)}, f32[768,384]{1,0:T(8,128)}, u32[]{:S(2)}, u32[]{:S(2)}) collective-permute-start(f32[768,384]{1,0:T(8,128)} %collective-permute-done.10), channel_id=1, source_target_pairs={{0,32},{1,97},{34,66},{35,3},{68,100},{69,37},{102,6},{103,71},{8,... | collective-permute-start | bytes 3538952 | tf_op jit(solution)/shard_map/product/ppermute | solution.py:307
  68.7 0.7 stack.55.places
  69.3 4.1 %collective-permute-start.17 = (f32[768,384]{1,0:T(8,128)}, f32[768,384]{1,0:T(8,128)}, u32[]{:S(2)}, u32[]{:S(2)}) collective-permute-start(f32[768,384]{1,0:T(8,128)} %collective-permute-done.6), channel_id=1, source_target_pairs={{0,96},{1,33},{34,2},{35,67},{68,36},{69,101},{102,70},{103,7},{8,... | collective-permute-start | bytes 3538952 | tf_op jit(solution)/shard_map/product/ppermute | solution.py:307
  73.4 9.4 %first_product.1 = (bf16[768,1536]{1,0:T(8,128)(2,1)}, bf16[768,1536]{1,0:T(8,128)(2,1)}, f32[768,384]{1,0:T(8,128)}) custom-call(s32[5]{0:T(128)} %stack.55.places, f32[2,192,768]{2,1,0:T(8,128)} %copy-done.11, f32[2,192,768]{2,1,0:T(8,128)} %copy-done.12, f32[2,192,768]{2,1,0:T(8,128)} %copy-done.13, f32[2,192,768]{2,1,0:T(8,128)} %copy-done.14, ...), custom_call_target="tpu_custom_call" | custom-call | flops 768 | bytes 768 | tf_op jit(solution)/shard_map/product/first_product/pallas_call | solution.py:148
  82.9 8.1 %next_product.3 = f32[768,384]{1,0:T(8,128)} custom-call(s32[1]{0:T(128)} %bitcast.20.places, bf16[768,1536]{1,0:T(8,128)(2,1)} %get-tuple-element.69.refs_0_, bf16[768,1536]{1,0:T(8,128)(2,1)} %get-tuple-element.70.refs_1_, f32[768,384]{1,0:T(8,128)} %copy-done.3, f32[768,384]{1,0:T(8,128)} %copy-done.4, f32[768,384]{1,0:T(8,128)} %copy-done.5, ...), custom_call_target="tpu_custom_call" | custom-call | flops 768 | bytes 768 | tf_op jit(solution)/shard_map/product/next_product/pallas_call | solution.py:148
  91.0 2.8 %collective-permute-start.18 = (f32[768,384]{1,0:T(8,128)}, f32[768,384]{1,0:T(8,128)S(1)}, u32[]{:S(2)}, u32[]{:S(2)}) collective-permute-start(f32[768,384]{1,0:T(8,128)} %collective-permute-done.7), channel_id=1, source_target_pairs={{0,32},{1,97},{34,66},{35,3},{68,100},{69,37},{102,6},{103,71},{8,... | collective-permute-start | bytes 3538952 | tf_op jit(solution)/shard_map/product/ppermute | solution.py:307
  93.9 0.7 collective-permute-start.16
  94.6 4.3 %collective-permute-start.19 = (f32[768,384]{1,0:T(8,128)}, f32[768,384]{1,0:T(8,128)}, u32[]{:S(2)}, u32[]{:S(2)}) collective-permute-start(f32[768,384]{1,0:T(8,128)} %next_product.3), channel_id=1, source_target_pairs={{0,6},{1,3},{2,0},{3,5},{4,2},{5,7},{6,4},{7,1},{8,14},{9,11},{10,... | collective-permute-start | bytes 3538952 | tf_op jit(solution)/shard_map/product/ppermute | solution.py:30
  98.9 8.1 %next_product.4 = f32[768,384]{1,0:T(8,128)} custom-call(s32[1]{0:T(128)} %bitcast.19.places, bf16[768,1536]{1,0:T(8,128)(2,1)} %get-tuple-element.69.refs_0_, bf16[768,1536]{1,0:T(8,128)(2,1)} %get-tuple-element.70.refs_1_, f32[768,384]{1,0:T(8,128)} %copy-done.3, f32[768,384]{1,0:T(8,128)} %copy-done.4, f32[768,384]{1,0:T(8,128)} %copy-done.5, ...), custom_call_target="tpu_custom_call" | custom-call | flops 768 | bytes 768 | tf_op jit(solution)/shard_map/product/next_product/pallas_call | solution.py:148
  107.1 1.5 add.151
  108.7 0.4 select_select_fusion
  109.1 8.9 %collective-permute-done.19 = f32[768,384]{1,0:T(8,128)} collective-permute-done((f32[768,384]{1,0:T(8,128)}, f32[768,384]{1,0:T(8,128)}, u32[]{:S(2)}, u32[]{:S(2)}) %collective-permute-start.19) | collective-permute-done | bytes 1179680 | tf_op jit(solution)/shard_map/product/ppermute | solution.py:30
  117.9 0.4 collective-permute-start.24
  118.4 8.1 %next_product.5 = f32[768,384]{1,0:T(8,128)} custom-call(s32[1]{0:T(128)} %bitcast.places, bf16[768,1536]{1,0:T(8,128)(2,1)} %get-tuple-element.69.refs_0_, bf16[768,1536]{1,0:T(8,128)(2,1)} %get-tuple-element.70.refs_1_, f32[768,384]{1,0:T(8,128)} %copy-done.3, f32[768,384]{1,0:T(8,128)} %copy-done.4, f32[768,384]{1,0:T(8,128)} %copy-done.5, ...), custom_call_target="tpu_custom_call" | custom-call | flops 8000000000 | bytes 768 | tf_op jit(solution)/shard_map/total/next_product/pallas_call | solution.py:148
  126.6 1.2 copy-done.15
  127.8 1.4 add_add_fusion
  129.4 0.9 fusion.3
  130.3 0.8 fusion
  131.2 0.8 dynamic-slice_bitcast_fusion.2
  131.9 0.5 collective-permute-start.25
  132.6 0.2 copy.25
  132.9 1.7 collective-permute-start.23
  134.5 0.2 copy.24
  134.8 1.5 collective-permute-start.22
  136.5 3.2 %collective-permute-start.27 = (f32[128,640]{1,0:T(8,128)S(1)}, f32[128,640]{1,0:T(8,128)S(1)}, u32[]{:S(2)}, u32[]{:S(2)}) collective-permute-start(f32[128,640]{1,0:T(8,128)S(1)} %bitcast_add_fusion), channel_id=1, source_target_pairs={{0,96},{1,33},{32,0},{33,65},{64,32},{65,97},{96,64},{97,1},{2,98}... | collective-permute-start | bytes 983048 | tf_op jit(solution)/shard_map/quad/ppermute | solution.py:30
  139.7 7.0 %collective-permute-done.26 = f32[128,640]{1,0:T(8,128)S(1)} collective-permute-done((f32[128,640]{1,0:T(8,128)S(1)}, f32[128,640]{1,0:T(8,128)S(1)}, u32[]{:S(2)}, u32[]{:S(2)}) %collective-permute-start.26) | collective-permute-done | bytes 327712 | tf_op jit(solution)/shard_map/quad/ppermute | solution.py:30
  146.8 1.1 broadcast_select_fusion.3
  148.0 0.4 convolution_subtract_fusion.1
  148.4 6.6 %collective-permute-done.28 = f32[128,640]{1,0:T(8,128)S(1)} collective-permute-done((f32[128,640]{1,0:T(8,128)S(1)}, f32[128,640]{1,0:T(8,128)S(1)}, u32[]{:S(2)}, u32[]{:S(2)}) %collective-permute-start.28) | collective-permute-done | bytes 327712 | tf_op jit(solution)/shard_map/quad/ppermute | solution.py:30
  155.0 0.8 add_add_fusion.1
  155.8 1.6 collective-permute-start.29
  157.4 3.3 %collective-permute-start.30 = (f32[128,640]{1,0:T(8,128)}, f32[128,640]{1,0:T(8,128)S(1)}, u32[]{:S(2)}, u32[]{:S(2)}) collective-permute-start(f32[128,640]{1,0:T(8,128)} %add_add_fusion.1), channel_id=1, source_target_pairs={{0,8},{1,0},{8,24},{9,16},{16,9},{17,1},{24,25},{25,17},{2,10},{3,... | collective-permute-start | bytes 983048 | tf_op jit(solution)/shard_map/quad/ppermute | solution.py:287
  160.8 5.5 %collective-permute-start.31 = (f32[128,640]{1,0:T(8,128)}, f32[128,640]{1,0:T(8,128)S(1)}, u32[]{:S(2)}, u32[]{:S(2)}) collective-permute-start(f32[128,640]{1,0:T(8,128)} %add_add_fusion.1), channel_id=1, source_target_pairs={{0,16},{1,24},{8,0},{9,8},{16,17},{17,25},{24,1},{25,9},{2,18},{3,... | collective-permute-start | bytes 983048 | tf_op jit(solution)/shard_map/quad/ppermute | solution.py:287
  166.3 1.9 %collective-permute-start.32 = (f32[128,640]{1,0:T(8,128)}, f32[128,640]{1,0:T(8,128)S(1)}, u32[]{:S(2)}, u32[]{:S(2)}) collective-permute-start(f32[128,640]{1,0:T(8,128)} %add_add_fusion.1), channel_id=1, source_target_pairs={{0,24},{1,16},{8,8},{9,0},{16,25},{17,17},{24,9},{25,1},{2,26},{3,... | collective-permute-start | bytes 983048 | tf_op jit(solution)/shard_map/quad/ppermute | solution.py:287
  168.2 0.4 convolution_subtract_fusion
  168.7 1.1 copy.28
  169.9 0.9 copy.27
  170.8 8.9 %collective-permute-done.31.refs_2_ = f32[128,640]{1,0:T(8,128)S(1)} collective-permute-done((f32[128,640]{1,0:T(8,128)}, f32[128,640]{1,0:T(8,128)S(1)}, u32[]{:S(2)}, u32[]{:S(2)}) %collective-permute-start.31) | collective-permute-done | bytes 327712 | tf_op jit(solution)/shard_map/quad/ppermute | solution.py:287
  179.7 2.4 %finish.1 = (f32[1,256,256]{2,1,0:T(8,128)}, f32[2,256,256]{2,1,0:T(8,128)}, f32[2,256,256]{2,1,0:T(8,128)}) custom-call(s32[4]{0:T(128)S(1)} %pad_add_fusion.z, f32[128,640]{1,0:T(8,128)S(1)} %collective-permute-done.29.refs_0_, f32[128,640]{1,0:T(8,128)S(1)} %collective-permute-done.30.refs_1_, f32[128,640]{1,0:T(8,128)S(1)} %collective-permute-done.31.refs_2_, ...), custom_call_target="tpu_custom_call" | custom-call | flops 100000000 | bytes 1000000 | tf_op jit(solution)/shard_map/diag/finish/pallas_call | solution.py:203
  (83 shorter events, 1.7 us)
Async XLA Ops:
  0.6 3.2 %copy-start.17 = (f32[768,128]{1,0:T(8,128)S(1)}, f32[768,128]{1,0:T(8,128)}, u32[]{:S(2)}) copy-start(f32[768,128]{1,0:T(8,128)} %param.9) | copy-start | bytes 1179652
  0.6 3.4 %copy-start.16 = (f32[768,256]{1,0:T(8,128)S(1)}, f32[768,256]{1,0:T(8,128)}, u32[]{:S(2)}) copy-start(f32[768,256]{1,0:T(8,128)} %param.10) | copy-start | bytes 2359300
  2.9 2.3 %collective-permute-start = (f32[192,768]{1,0:T(8,128)}, f32[192,768]{1,0:T(8,128)}, u32[]{:S(2)}, u32[]{:S(2)}) collective-permute-start(f32[192,768]{1,0:T(8,128)} %get-tuple-element.100), channel_id=1, source_target_pairs={{0,1},{1,0},{2,3},{3,2},{4,5},{5,4},{6,7},{7,6},{8,9},{9,8},{10,11... | collective-permute-start | bytes 1769480 | tf_op jit(solution)/shard_map/gather/ppermute | solution.py:22
  4.3 8.1 %copy-start.3 = (f32[768,384]{1,0:T(8,128)}, f32[768,384]{1,0:T(8,128)S(1)}, u32[]{:S(2)}) copy-start(f32[768,384]{1,0:T(8,128)S(1)} %pad_maximum_fusion.1.refs_4_.refs_2_) | copy-start | bytes 3538948
  5.2 2.8 %collective-permute-start.5 = (f32[768,384]{1,0:T(8,128)S(1)}, f32[768,384]{1,0:T(8,128)S(1)}, u32[]{:S(2)}, u32[]{:S(2)}) collective-permute-start(f32[768,384]{1,0:T(8,128)S(1)} %pad_maximum_fusion.1.refs_4_.refs_2_), channel_id=1, source_target_pairs={{0,1},{1,0},{2,3},{3,2},{4,5},{5,4},{6,7},{7,6},{8,9},{9,8},{10,11... | collective-permute-start | bytes 3538952 | tf_op jit(solution)/shard_map/gather/ppermute | solution.py:22
  6.5 9.6 %copy-start.11 = (f32[2,192,768]{2,1,0:T(8,128)}, f32[2,192,768]{2,1,0:T(8,128)S(1)}, u32[]{:S(2)}) copy-start(f32[2,192,768]{2,1,0:T(8,128)S(1)} %pad_maximum_fusion.refs_0_) | copy-start | bytes 3538948
  8.1 1.0 copy-start.4
  9.2 55.5 %copy-start.9 = (f32[4,192,384]{2,1,0:T(8,128)}, f32[4,192,384]{2,1,0:T(8,128)S(1)}, u32[]{:S(2)}) copy-start(f32[4,192,384]{2,1,0:T(8,128)S(1)} %pad_maximum_fusion.2) | copy-start | bytes 3538948
  9.2 17.6 %collective-permute-start.6 = (f32[768,384]{1,0:T(8,128)S(1)}, f32[768,384]{1,0:T(8,128)}, u32[]{:S(2)}, u32[]{:S(2)}) collective-permute-start(f32[768,384]{1,0:T(8,128)S(1)} %bitcast.61), channel_id=1, source_target_pairs={{0,2},{1,7},{2,4},{3,1},{4,6},{5,3},{6,0},{7,5},{8,10},{9,15},{10,... | collective-permute-start | bytes 3538952 | tf_op jit(solution)/shard_map/gather/ppermute | solution.py:30
  10.9 27.2 %collective-permute-start.3 = (f32[768,384]{1,0:T(8,128)S(1)}, f32[768,384]{1,0:T(8,128)S(1)}, u32[]{:S(2)}, u32[]{:S(2)}) collective-permute-start(f32[768,384]{1,0:T(8,128)S(1)} %pad_maximum_fusion.1.refs_4_.refs_2_), channel_id=1, source_target_pairs={{0,32},{1,97},{32,64},{33,1},{64,96},{65,33},{96,0},{97,65},{2,34}... | collective-permute-start | bytes 3538952 | tf_op jit(solution)/shard_map/gather/ppermute | solution.py:30
  12.4 28.0 %collective-permute-start.4 = (f32[768,384]{1,0:T(8,128)S(1)}, f32[768,384]{1,0:T(8,128)S(1)}, u32[]{:S(2)}, u32[]{:S(2)}) collective-permute-start(f32[768,384]{1,0:T(8,128)S(1)} %pad_maximum_fusion.1.refs_4_.refs_2_), channel_id=1, source_target_pairs={{0,96},{1,33},{32,0},{33,65},{64,32},{65,97},{96,64},{97,1},{2,98}... | collective-permute-start | bytes 3538952 | tf_op jit(solution)/shard_map/gather/ppermute | solution.py:30
  14.2 28.3 %collective-permute-start.1 = (f32[2,192,768]{2,1,0:T(8,128)S(1)}, f32[2,192,768]{2,1,0:T(8,128)S(1)}, u32[]{:S(2)}, u32[]{:S(2)}) collective-permute-start(f32[2,192,768]{2,1,0:T(8,128)S(1)} %pad_maximum_fusion.refs_0_), channel_id=1, source_target_pairs={{0,8},{1,25},{8,16},{9,1},{16,24},{17,9},{24,0},{25,17},{2,10},{3,... | collective-permute-start | bytes 3538952 | tf_op jit(solution)/shard_map/gather/ppermute | solution.py:30
  16.1 28.0 %collective-permute-start.2 = (f32[2,192,768]{2,1,0:T(8,128)S(1)}, f32[2,192,768]{2,1,0:T(8,128)S(1)}, u32[]{:S(2)}, u32[]{:S(2)}) collective-permute-start(f32[2,192,768]{2,1,0:T(8,128)S(1)} %pad_maximum_fusion.refs_0_), channel_id=1, source_target_pairs={{0,24},{1,9},{8,0},{9,17},{16,8},{17,25},{24,16},{25,1},{2,26},{3,... | collective-permute-start | bytes 3538952 | tf_op jit(solution)/shard_map/gather/ppermute | solution.py:30
  26.8 17.4 %collective-permute-start.7 = (f32[768,384]{1,0:T(8,128)S(1)}, f32[768,384]{1,0:T(8,128)}, u32[]{:S(2)}, u32[]{:S(2)}) collective-permute-start(f32[768,384]{1,0:T(8,128)S(1)} %bitcast.62), channel_id=1, source_target_pairs={{0,6},{1,3},{2,0},{3,5},{4,2},{5,7},{6,4},{7,1},{8,14},{9,11},{10,... | collective-permute-start | bytes 3538952 | tf_op jit(solution)/shard_map/gather/ppermute | solution.py:30
  38.1 35.3 %copy-start.5 = (f32[768,384]{1,0:T(8,128)}, f32[768,384]{1,0:T(8,128)S(1)}, u32[]{:S(2)}) copy-start(f32[768,384]{1,0:T(8,128)S(1)} %collective-permute-done.3.refs_6_.refs_4_) | copy-start | bytes 3538948
  40.4 33.1 %copy-start.6 = (f32[768,384]{1,0:T(8,128)}, f32[768,384]{1,0:T(8,128)S(1)}, u32[]{:S(2)}) copy-start(f32[768,384]{1,0:T(8,128)S(1)} %collective-permute-done.4.refs_8_.refs_6_) | copy-start | bytes 3538948
  42.4 22.3 %copy-start.12 = (f32[2,192,768]{2,1,0:T(8,128)}, f32[2,192,768]{2,1,0:T(8,128)S(1)}, u32[]{:S(2)}) copy-start(f32[2,192,768]{2,1,0:T(8,128)S(1)} %collective-permute-done.1.refs_1_) | copy-start | bytes 3538948
  44.1 2.5 %copy-start.13 = (f32[2,192,768]{2,1,0:T(8,128)}, f32[2,192,768]{2,1,0:T(8,128)S(1)}, u32[]{:S(2)}) copy-start(f32[2,192,768]{2,1,0:T(8,128)S(1)} %collective-permute-done.2.refs_2_) | copy-start | bytes 3538948
  44.1 17.7 %collective-permute-start.10 = (f32[768,384]{1,0:T(8,128)}, f32[768,384]{1,0:T(8,128)}, u32[]{:S(2)}, u32[]{:S(2)}) collective-permute-start(f32[768,384]{1,0:T(8,128)} %collective-permute-done.6), channel_id=1, source_target_pairs={{0,2},{1,7},{2,4},{3,1},{4,6},{5,3},{6,0},{7,5},{8,10},{9,15},{10,... | collective-permute-start | bytes 3538952 | tf_op jit(solution)/shard_map/gather/ppermute | solution.py:30
  46.6 15.2 %collective-permute-start.11 = (f32[768,384]{1,0:T(8,128)S(1)}, f32[768,384]{1,0:T(8,128)S(1)}, u32[]{:S(2)}, u32[]{:S(2)}) collective-permute-start(f32[768,384]{1,0:T(8,128)S(1)} %collective-permute-done.4.refs_8_.refs_6_), channel_id=1, source_target_pairs={{0,1},{1,0},{2,3},{3,2},{4,5},{5,4},{6,7},{7,6},{8,9},{9,8},{10,11... | collective-permute-start | bytes 3538952 | tf_op jit(solution)/shard_map/gather/ppermute | solution.py:22
  46.7 15.2 %collective-permute-start.12 = (f32[768,384]{1,0:T(8,128)S(1)}, f32[768,384]{1,0:T(8,128)S(1)}, u32[]{:S(2)}, u32[]{:S(2)}) collective-permute-start(f32[768,384]{1,0:T(8,128)S(1)} %collective-permute-done.3.refs_6_.refs_4_), channel_id=1, source_target_pairs={{0,1},{1,0},{2,3},{3,2},{4,5},{5,4},{6,7},{7,6},{8,9},{9,8},{10,11... | collective-permute-start | bytes 3538952 | tf_op jit(solution)/shard_map/gather/ppermute | solution.py:22
  47.2 17.4 %collective-permute-start.8 = (f32[2,192,768]{2,1,0:T(8,128)S(1)}, f32[2,192,768]{2,1,0:T(8,128)S(1)}, u32[]{:S(2)}, u32[]{:S(2)}) collective-permute-start(f32[2,192,768]{2,1,0:T(8,128)S(1)} %collective-permute-done.1.refs_1_), channel_id=1, source_target_pairs={{0,8},{1,25},{8,16},{9,1},{16,24},{17,9},{24,0},{25,17},{2,10},{3,... | collective-permute-start | bytes 3538952 | tf_op jit(solution)/shard_map/gather/ppermute | solution.py:30
  47.2 17.5 %collective-permute-start.9 = (f32[768,384]{1,0:T(8,128)S(1)}, f32[768,384]{1,0:T(8,128)}, u32[]{:S(2)}, u32[]{:S(2)}) collective-permute-start(f32[768,384]{1,0:T(8,128)S(1)} %collective-permute-done.3.refs_6_.refs_4_), channel_id=1, source_target_pairs={{0,32},{1,97},{32,64},{33,1},{64,96},{65,33},{96,0},{97,65},{2,34}... | collective-permute-start | bytes 3538952 | tf_op jit(solution)/shard_map/gather/ppermute | solution.py:30
  61.9 11.6 %copy-start.7 = (f32[768,384]{1,0:T(8,128)}, f32[768,384]{1,0:T(8,128)S(1)}, u32[]{:S(2)}) copy-start(f32[768,384]{1,0:T(8,128)S(1)} %collective-permute-done.11.refs_7_.refs_5_) | copy-start | bytes 3538948
  61.9 2.8 %copy-start.8 = (f32[768,384]{1,0:T(8,128)}, f32[768,384]{1,0:T(8,128)S(1)}, u32[]{:S(2)}) copy-start(f32[768,384]{1,0:T(8,128)S(1)} %collective-permute-done.12.refs_9_.refs_7_) | copy-start | bytes 3538948
  64.6 1.0 copy-start.14
  64.7 8.7 %collective-permute-start.13 = (f32[768,384]{1,0:T(8,128)}, f32[768,384]{1,0:T(8,128)}, u32[]{:S(2)}, u32[]{:S(2)}) collective-permute-start(f32[768,384]{1,0:T(8,128)} %collective-permute-done.9.refs_10_.refs_8_), channel_id=1, source_target_pairs={{0,1},{1,0},{2,3},{3,2},{4,5},{5,4},{6,7},{7,6},{8,9},{9,8},{10,11... | collective-permute-start | bytes 3538952 | tf_op jit(solution)/shard_map/gather/ppermute | solution.py:22
  65.6 28.2 %collective-permute-start.15 = (f32[768,384]{1,0:T(8,128)}, f32[768,384]{1,0:T(8,128)}, u32[]{:S(2)}, u32[]{:S(2)}) collective-permute-start(f32[768,384]{1,0:T(8,128)} %collective-permute-done.10), channel_id=1, source_target_pairs={{0,32},{1,97},{34,66},{35,3},{68,100},{69,37},{102,6},{103,71},{8,... | collective-permute-start | bytes 3538952 | tf_op jit(solution)/shard_map/product/ppermute | solution.py:307
  69.3 39.3 %collective-permute-start.17 = (f32[768,384]{1,0:T(8,128)}, f32[768,384]{1,0:T(8,128)}, u32[]{:S(2)}, u32[]{:S(2)}) collective-permute-start(f32[768,384]{1,0:T(8,128)} %collective-permute-done.6), channel_id=1, source_target_pairs={{0,96},{1,33},{34,2},{35,67},{68,36},{69,101},{102,70},{103,7},{8,... | collective-permute-start | bytes 3538952 | tf_op jit(solution)/shard_map/product/ppermute | solution.py:307
  82.8 24.2 %collective-permute-start.14 = (f32[768,384]{1,0:T(8,128)}, f32[768,384]{1,0:T(8,128)S(1)}, u32[]{:S(2)}, u32[]{:S(2)}) collective-permute-start(f32[768,384]{1,0:T(8,128)} %get-tuple-element.58), channel_id=1, source_target_pairs={{0,2},{1,7},{2,4},{3,1},{4,6},{5,3},{6,0},{7,5},{8,10},{9,15},{10,... | collective-permute-start | bytes 3538952 | tf_op jit(solution)/shard_map/product/ppermute | solution.py:30
  91.0 17.6 %collective-permute-start.18 = (f32[768,384]{1,0:T(8,128)}, f32[768,384]{1,0:T(8,128)S(1)}, u32[]{:S(2)}, u32[]{:S(2)}) collective-permute-start(f32[768,384]{1,0:T(8,128)} %collective-permute-done.7), channel_id=1, source_target_pairs={{0,32},{1,97},{34,66},{35,3},{68,100},{69,37},{102,6},{103,71},{8,... | collective-permute-start | bytes 3538952 | tf_op jit(solution)/shard_map/product/ppermute | solution.py:307
  93.9 14.8 %collective-permute-start.16 = (f32[768,384]{1,0:T(8,128)}, f32[768,384]{1,0:T(8,128)S(1)}, u32[]{:S(2)}, u32[]{:S(2)}) collective-permute-start(f32[768,384]{1,0:T(8,128)} %collective-permute-done.15), channel_id=1, source_target_pairs={{32,64},{97,65},{66,98},{3,99},{100,4},{37,5},{6,38},{71,39},{40,7... | collective-permute-start | bytes 3538952 | tf_op jit(solution)/shard_map/product/ppermute | solution.py:307
  94.6 23.3 %collective-permute-start.19 = (f32[768,384]{1,0:T(8,128)}, f32[768,384]{1,0:T(8,128)}, u32[]{:S(2)}, u32[]{:S(2)}) collective-permute-start(f32[768,384]{1,0:T(8,128)} %next_product.3), channel_id=1, source_target_pairs={{0,6},{1,3},{2,0},{3,5},{4,2},{5,7},{6,4},{7,1},{8,14},{9,11},{10,... | collective-permute-start | bytes 3538952 | tf_op jit(solution)/shard_map/product/ppermute | solution.py:30
  107.0 1.6 copy-start.10
  108.6 18.0 %collective-permute-start.20 = (f32[768,384]{1,0:T(8,128)S(1)}, f32[768,384]{1,0:T(8,128)S(1)}, u32[]{:S(2)}, u32[]{:S(2)}) collective-permute-start(f32[768,384]{1,0:T(8,128)S(1)} %add.151), channel_id=1, source_target_pairs={{0,2},{1,7},{2,4},{3,1},{4,6},{5,3},{6,0},{7,5},{8,10},{9,15},{10,... | collective-permute-start | bytes 3538952 | tf_op jit(solution)/shard_map/product/ppermute | solution.py:30
  117.9 8.6 %collective-permute-start.24 = (f32[768,128]{1,0:T(8,128)S(1)}, f32[768,128]{1,0:T(8,128)S(1)}, u32[]{:S(2)}, u32[]{:S(2)}) collective-permute-start(f32[768,128]{1,0:T(8,128)S(1)} %slice.38), channel_id=1, source_target_pairs={{0,8},{8,0},{16,24},{24,16},{1,9},{9,1},{17,25},{25,17},{2,10},{10... | collective-permute-start | bytes 1179656 | tf_op jit(solution)/shard_map/turned/ppermute | solution.py:341
  126.5 1.3 copy-start.15
  129.3 3.1 %collective-permute-start.21 = (f32[384,384]{1,0:T(8,128)S(1)}, f32[384,384]{1,0:T(8,128)S(1)}, u32[]{:S(2)}, u32[]{:S(2)}) collective-permute-start(f32[384,384]{1,0:T(8,128)S(1)} %get-tuple-element.97), channel_id=1, source_target_pairs={{0,1},{1,0},{2,3},{3,2},{4,5},{5,4},{6,7},{7,6},{8,9},{9,8},{10,11... | collective-permute-start | bytes 1769480 | tf_op jit(solution)/shard_map/out/ppermute | solution.py:22
  131.9 4.3 %collective-permute-start.25 = (f32[128,640]{1,0:T(8,128)}, f32[128,640]{1,0:T(8,128)S(1)}, u32[]{:S(2)}, u32[]{:S(2)}) collective-permute-start(f32[128,640]{1,0:T(8,128)} %dynamic-slice_bitcast_fusion.2), channel_id=1, source_target_pairs={{0,1},{1,0},{2,3},{3,2},{4,5},{5,4},{6,7},{7,6},{8,9},{9,8},{10,11... | collective-permute-start | bytes 983048 | tf_op jit(solution)/shard_map/quad/ppermute | solution.py:22
  132.9 13.9 %collective-permute-start.23 = (f32[384,384]{0,1:T(8,128)S(1)}, f32[384,384]{0,1:T(8,128)S(1)}, u32[]{:S(2)}, u32[]{:S(2)}) collective-permute-start(f32[384,384]{0,1:T(8,128)S(1)} %bitcast.70), channel_id=1, source_target_pairs={{0,8},{1,24},{8,0},{9,16},{16,9},{17,25},{24,1},{25,17},{2,10},{3,... | collective-permute-start | bytes 1769480 | tf_op jit(solution)/shard_map/out/ppermute | solution.py:364
  134.8 12.0 %collective-permute-start.22 = (f32[384,384]{0,1:T(8,128)S(1)}, f32[384,384]{0,1:T(8,128)}, u32[]{:S(2)}, u32[]{:S(2)}) collective-permute-start(f32[384,384]{0,1:T(8,128)S(1)} %bitcast.69), channel_id=1, source_target_pairs={{0,0},{1,16},{8,8},{9,24},{16,1},{17,17},{24,9},{25,25},{2,2},{3,1... | collective-permute-start | bytes 1769480 | tf_op jit(solution)/shard_map/out/ppermute | solution.py:364
  136.3 10.4 %collective-permute-start.26 = (f32[128,640]{1,0:T(8,128)S(1)}, f32[128,640]{1,0:T(8,128)S(1)}, u32[]{:S(2)}, u32[]{:S(2)}) collective-permute-start(f32[128,640]{1,0:T(8,128)S(1)} %bitcast_add_fusion), channel_id=1, source_target_pairs={{0,32},{1,97},{32,64},{33,1},{64,96},{65,33},{96,0},{97,65},{2,34}... | collective-permute-start | bytes 983048 | tf_op jit(solution)/shard_map/quad/ppermute | solution.py:30
  136.5 11.5 %copy-start = (f32[2,256,256]{2,1,0:T(8,128)S(1)}, f32[2,256,256]{2,1,0:T(8,128)}, u32[]{:S(2)}) copy-start(f32[2,256,256]{2,1,0:T(8,128)} %refs_4_.1) | copy-start | bytes 1572868
  136.5 11.9 %collective-permute-start.27 = (f32[128,640]{1,0:T(8,128)S(1)}, f32[128,640]{1,0:T(8,128)S(1)}, u32[]{:S(2)}, u32[]{:S(2)}) collective-permute-start(f32[128,640]{1,0:T(8,128)S(1)} %bitcast_add_fusion), channel_id=1, source_target_pairs={{0,96},{1,33},{32,0},{33,65},{64,32},{65,97},{96,64},{97,1},{2,98}... | collective-permute-start | bytes 983048 | tf_op jit(solution)/shard_map/quad/ppermute | solution.py:30
  146.7 8.3 %collective-permute-start.28 = (f32[128,640]{1,0:T(8,128)S(1)}, f32[128,640]{1,0:T(8,128)S(1)}, u32[]{:S(2)}, u32[]{:S(2)}) collective-permute-start(f32[128,640]{1,0:T(8,128)S(1)} %collective-permute-done.26), channel_id=1, source_target_pairs={{0,32},{1,97},{32,64},{33,1},{64,96},{65,33},{96,0},{97,65},{2,34}... | collective-permute-start | bytes 983048 | tf_op jit(solution)/shard_map/quad/ppermute | solution.py:30
  155.8 15.0 %collective-permute-start.29 = (f32[128,640]{1,0:T(8,128)}, f32[128,640]{1,0:T(8,128)S(1)}, u32[]{:S(2)}, u32[]{:S(2)}) collective-permute-start(f32[128,640]{1,0:T(8,128)} %add_add_fusion.1), channel_id=1, source_target_pairs={{0,0},{1,8},{8,16},{9,24},{16,1},{17,9},{24,17},{25,25},{2,2},{3,1... | collective-permute-start | bytes 983048 | tf_op jit(solution)/shard_map/quad/ppermute | solution.py:287
  157.4 13.4 %collective-permute-start.30 = (f32[128,640]{1,0:T(8,128)}, f32[128,640]{1,0:T(8,128)S(1)}, u32[]{:S(2)}, u32[]{:S(2)}) collective-permute-start(f32[128,640]{1,0:T(8,128)} %add_add_fusion.1), channel_id=1, source_target_pairs={{0,8},{1,0},{8,24},{9,16},{16,9},{17,1},{24,25},{25,17},{2,10},{3,... | collective-permute-start | bytes 983048 | tf_op jit(solution)/shard_map/quad/ppermute | solution.py:287
  160.8 18.9 %collective-permute-start.31 = (f32[128,640]{1,0:T(8,128)}, f32[128,640]{1,0:T(8,128)S(1)}, u32[]{:S(2)}, u32[]{:S(2)}) collective-permute-start(f32[128,640]{1,0:T(8,128)} %add_add_fusion.1), channel_id=1, source_target_pairs={{0,16},{1,24},{8,0},{9,8},{16,17},{17,25},{24,1},{25,9},{2,18},{3,... | collective-permute-start | bytes 983048 | tf_op jit(solution)/shard_map/quad/ppermute | solution.py:287
  166.3 13.4 %collective-permute-start.32 = (f32[128,640]{1,0:T(8,128)}, f32[128,640]{1,0:T(8,128)S(1)}, u32[]{:S(2)}, u32[]{:S(2)}) collective-permute-start(f32[128,640]{1,0:T(8,128)} %add_add_fusion.1), channel_id=1, source_target_pairs={{0,24},{1,16},{8,8},{9,0},{16,25},{17,17},{24,9},{25,1},{2,26},{3,... | collective-permute-start | bytes 983048 | tf_op jit(solution)/shard_map/quad/ppermute | solution.py:287
  169.9 9.8 %copy-start.1 = (f32[2,256,256]{2,1,0:T(8,128)S(1)}, f32[2,256,256]{2,1,0:T(8,128)}, u32[]{:S(2)}) copy-start(f32[2,256,256]{2,1,0:T(8,128)} %refs_6_.1) | copy-start | bytes 1572868
  169.9 9.8 %copy-start.2 = (f32[1,256,256]{2,1,0:T(8,128)S(1)}, f32[1,256,256]{2,1,0:T(8,128)}, u32[]{:S(2)}) copy-start(f32[1,256,256]{2,1,0:T(8,128)} %refs_5_.1) | copy-start | bytes 786436

commit v4 on v3

--- a/solution.py
+++ b/solution.py
@@ -277,8 +277,8 @@
         a_far, l_far = send(a_first, "z", 1), send(l_first, "x", 1)
         t_far = send(after(t_first, t_second), "y", 1)
         first_other, second_other = swap(l_second), swap(l_first)
-        a_far, l_far, t_far, first_other, second_other = lax.optimization_barrier(
-            (a_far, l_far, t_far, first_other, second_other)
+        a_far, l_far, first_other, second_other = lax.optimization_barrier(
+            (a_far, l_far, first_other, second_other)
         )
         far_other = swap(l_far)
 

time: 183 us -> 187 us (1.022)
  starting transfers between devices: 49.4 us -> 56.9 us
  waiting for transfers between devices: 75.1 us -> 71.5 us
    ppermute x15, waiting for transfers between devices: 63.7 us -> 53.4 us  [send(): return lax.ppermute(value, (axis, 'core'), split_pairs(step))]
    ppermute x1, starting transfers between devices: 0.44 us -> 7.84 us  [local(): mate = lax.ppermute(own, 'z', [(0, 1), (1, 0), (2, 3), (3, 2)])]
    ppermute x2, waiting for transfers between devices: 0.01 us -> 2.75 us  [local(): lax.ppermute(pick(blocks, (z + turn_over) % 2), ('z', 'core'), pairs)]
    ppermute x15, starting transfers between devices: 21.5 us -> 18.9 us  [send(): return lax.ppermute(value, (axis, 'core'), split_pairs(step))]
    ppermute x4, starting transfers between devices: 12.4 us -> 15 us  [spread(): lax.ppermute(value, ('z', 'core'), [((2 * c + j) * 2 + h, (2 * j + h ^ tu...]
  transfers between devices with their start and end apart: 33 -> 33, of which waited for: 14 -> 19; matrix products, arithmetic and copies ran while one was open for 7% -> 7% of each run, Pallas kernels for 19% -> 18%
where the time goes in v4:
time: 187 us; the launch traced here: 185 us
  waiting for transfers between devices  71.5 us (38%)
  starting transfers between devices  56.9 us (30%)
  Pallas kernels  36.2 us (19%)
  local copies, waits for them, and re-layouts  8.9 us (5%)
  other arithmetic  8.22 us (4%)
  matrix products  2.55 us (1%)
    ppermute x15, waiting for transfers between devices, send(): return lax.ppermute(value, (axis, 'core'), split_pairs(step))  53.4 us
    pallas_call x4, Pallas kernels, product(): pl.pallas_call(first_kernel if first else next_kernel, out_shape=[parts,...  33.8 us
    ppermute x15, starting transfers between devices, send(): return lax.ppermute(value, (axis, 'core'), split_pairs(step))  18.9 us
    ppermute x4, starting transfers between devices, spread(): lax.ppermute(value, ('z', 'core'), [((2 * c + j) * 2 + h, (2 * j + h ^ tu...  15 us
    ppermute x4, starting transfers between devices, turn(): return lax.ppermute(value, ('x', 'y', 'core'), pairs)  11.4 us
    ppermute x4, waiting for transfers between devices, spread(): lax.ppermute(value, ('z', 'core'), [((2 * c + j) * 2 + h, (2 * j + h ^ tu...  8.88 us
    ppermute x1, starting transfers between devices, local(): mate = lax.ppermute(own, 'z', [(0, 1), (1, 0), (2, 3), (3, 2)])  7.84 us
    unnamed x38, local copies, waits for them, and re-layouts  4.5 us
  transfers between devices with their start and end apart: 33, of which 19 were waited for; matrix products, arithmetic and copies ran while one was open for 7% of the time, Pallas kernels for 18%

profile of v4, /device:TPU:0, one launch (start us, length us, event | category | flops | bytes accessed | tf_op | source)
XLA Modules:
  0.0 185.3 jit_solution(2493259976675699343)
XLA Ops:
  0.7 2.2 %constant_dynamic-slice_fusion.1 = (f32[1,192,768]{2,1,0:T(8,128)S(1)}, f32[192,768]{1,0:T(8,128)}) fusion(f32[2,192,768]{2,1,0:T(8,128)} %bitcast.67, s32[]{:T(128)S(6)} %select_n.238, s32[]{:T(128)S(6)} %select_n.239), kind=kLoop, calls=%fused_computation.45 | loop fusion | bytes 2359304 | tf_op jit(solution)/shard_map/gather/jit(dynamic_index_in_dim)/dynamic_slice | solution.py:38
  2.9 0.8 convert_bitcast_fusion.1
  4.3 0.9 collective-permute-done
  5.4 1.1 pad_maximum_fusion.refs_0_
  6.5 1.6 collective-permute-done.5.refs_5_.refs_3_
  8.2 0.9 copy-done.4
  9.2 1.7 collective-permute-start.6
  10.9 1.5 collective-permute-start.3
  12.4 1.7 collective-permute-start.4
  14.2 1.9 %collective-permute-start.1 = (f32[2,192,768]{2,1,0:T(8,128)S(1)}, f32[2,192,768]{2,1,0:T(8,128)S(1)}, u32[]{:S(2)}, u32[]{:S(2)}) collective-permute-start(f32[2,192,768]{2,1,0:T(8,128)S(1)} %pad_maximum_fusion.refs_0_), channel_id=1, source_target_pairs={{0,8},{1,25},{8,16},{9,1},{16,24},{17,9},{24,0},{25,17},{2,10},{3,... | collective-permute-start | bytes 3538952 | tf_op jit(solution)/shard_map/gather/ppermute | solution.py:30
  16.1 2.1 %collective-permute-start.2 = (f32[2,192,768]{2,1,0:T(8,128)S(1)}, f32[2,192,768]{2,1,0:T(8,128)S(1)}, u32[]{:S(2)}, u32[]{:S(2)}) collective-permute-start(f32[2,192,768]{2,1,0:T(8,128)S(1)} %pad_maximum_fusion.refs_0_), channel_id=1, source_target_pairs={{0,24},{1,9},{8,0},{9,17},{16,8},{17,25},{24,16},{25,1},{2,26},{3,... | collective-permute-start | bytes 3538952 | tf_op jit(solution)/shard_map/gather/ppermute | solution.py:30
  18.2 8.6 %collective-permute-done.6 = f32[768,384]{1,0:T(8,128)} collective-permute-done((f32[768,384]{1,0:T(8,128)S(1)}, f32[768,384]{1,0:T(8,128)}, u32[]{:S(2)}, u32[]{:S(2)}) %collective-permute-start.6) | collective-permute-done | bytes 1179680 | tf_op jit(solution)/shard_map/gather/ppermute | solution.py:30
  26.8 1.9 %collective-permute-start.7 = (f32[768,384]{1,0:T(8,128)S(1)}, f32[768,384]{1,0:T(8,128)}, u32[]{:S(2)}, u32[]{:S(2)}) collective-permute-start(f32[768,384]{1,0:T(8,128)S(1)} %bitcast.62), channel_id=1, source_target_pairs={{0,6},{1,3},{2,0},{3,5},{4,2},{5,7},{6,4},{7,1},{8,14},{9,11},{10,... | collective-permute-start | bytes 3538952 | tf_op jit(solution)/shard_map/gather/ppermute | solution.py:30
  28.7 9.4 %collective-permute-done.3.refs_6_.refs_4_ = f32[768,384]{1,0:T(8,128)S(1)} collective-permute-done((f32[768,384]{1,0:T(8,128)S(1)}, f32[768,384]{1,0:T(8,128)S(1)}, u32[]{:S(2)}, u32[]{:S(2)}) %collective-permute-start.3) | collective-permute-done | bytes 1179680 | tf_op jit(solution)/shard_map/gather/ppermute | solution.py:30
  38.1 2.3 %collective-permute-done.4.refs_8_.refs_6_ = f32[768,384]{1,0:T(8,128)S(1)} collective-permute-done((f32[768,384]{1,0:T(8,128)S(1)}, f32[768,384]{1,0:T(8,128)S(1)}, u32[]{:S(2)}, u32[]{:S(2)}) %collective-permute-start.4) | collective-permute-done | bytes 1179680 | tf_op jit(solution)/shard_map/gather/ppermute | solution.py:30
  40.4 2.1 %collective-permute-done.1.refs_1_ = f32[2,192,768]{2,1,0:T(8,128)S(1)} collective-permute-done((f32[2,192,768]{2,1,0:T(8,128)S(1)}, f32[2,192,768]{2,1,0:T(8,128)S(1)}, u32[]{:S(2)}, u32[]{:S(2)}) %collective-permute-start.1) | collective-permute-done | bytes 1179680 | tf_op jit(solution)/shard_map/gather/ppermute | solution.py:30
  42.4 1.7 collective-permute-done.2.refs_2_
  44.1 1.1 copy-done.13
  45.2 0.7 collective-permute-start.10
  46.3 0.8 collective-permute-start.9
  47.1 1.3 collective-permute-start.14
  48.4 1.7 collective-permute-done.11.refs_9_.refs_7_
  50.1 13.5 %collective-permute-done.8.refs_3_ = f32[2,192,768]{2,1,0:T(8,128)S(1)} collective-permute-done((f32[2,192,768]{2,1,0:T(8,128)S(1)}, f32[2,192,768]{2,1,0:T(8,128)S(1)}, u32[]{:S(2)}, u32[]{:S(2)}) %collective-permute-start.8) | collective-permute-done | bytes 1179680 | tf_op jit(solution)/shard_map/gather/ppermute | solution.py:30
  63.8 0.8 collective-permute-start.12
  64.8 4.4 %collective-permute-start.15 = (f32[768,384]{1,0:T(8,128)}, f32[768,384]{1,0:T(8,128)}, u32[]{:S(2)}, u32[]{:S(2)}) collective-permute-start(f32[768,384]{1,0:T(8,128)} %collective-permute-done.14), channel_id=1, source_target_pairs={{0,32},{1,97},{34,66},{35,3},{68,100},{69,37},{102,6},{103,71},{8,... | collective-permute-start | bytes 3538952 | tf_op jit(solution)/shard_map/product/ppermute | solution.py:307
  69.3 0.7 stack.55.places
  69.9 2.8 %collective-permute-start.17 = (f32[768,384]{1,0:T(8,128)}, f32[768,384]{1,0:T(8,128)}, u32[]{:S(2)}, u32[]{:S(2)}) collective-permute-start(f32[768,384]{1,0:T(8,128)} %collective-permute-done.6), channel_id=1, source_target_pairs={{0,96},{1,33},{34,2},{35,67},{68,36},{69,101},{102,70},{103,7},{8,... | collective-permute-start | bytes 3538952 | tf_op jit(solution)/shard_map/product/ppermute | solution.py:307
  72.7 9.4 %first_product.1 = (bf16[768,1536]{1,0:T(8,128)(2,1)}, bf16[768,1536]{1,0:T(8,128)(2,1)}, f32[768,384]{1,0:T(8,128)}) custom-call(s32[5]{0:T(128)} %stack.55.places, f32[2,192,768]{2,1,0:T(8,128)} %copy-done.11, f32[2,192,768]{2,1,0:T(8,128)} %copy-done.12, f32[2,192,768]{2,1,0:T(8,128)} %copy-done.13, f32[2,192,768]{2,1,0:T(8,128)} %copy-done.14, ...), custom_call_target="tpu_custom_call" | custom-call | flops 768 | bytes 768 | tf_op jit(solution)/shard_map/product/first_product/pallas_call | solution.py:148
  82.2 8.1 %next_product.3 = f32[768,384]{1,0:T(8,128)} custom-call(s32[1]{0:T(128)} %bitcast.20.places, bf16[768,1536]{1,0:T(8,128)(2,1)} %get-tuple-element.67.refs_0_, bf16[768,1536]{1,0:T(8,128)(2,1)} %get-tuple-element.68.refs_1_, f32[768,384]{1,0:T(8,128)} %copy-done.3, f32[768,384]{1,0:T(8,128)} %copy-done.4, f32[768,384]{1,0:T(8,128)} %copy-done.5, ...), custom_call_target="tpu_custom_call" | custom-call | flops 768 | bytes 768 | tf_op jit(solution)/shard_map/product/next_product/pallas_call | solution.py:148
  90.3 3.5 %collective-permute-start.18 = (f32[768,384]{1,0:T(8,128)}, f32[768,384]{1,0:T(8,128)S(1)}, u32[]{:S(2)}, u32[]{:S(2)}) collective-permute-start(f32[768,384]{1,0:T(8,128)} %collective-permute-done.7), channel_id=1, source_target_pairs={{0,32},{1,97},{34,66},{35,3},{68,100},{69,37},{102,6},{103,71},{8,... | collective-permute-start | bytes 3538952 | tf_op jit(solution)/shard_map/product/ppermute | solution.py:307
  93.8 0.7 collective-permute-start.16
  94.6 1.7 collective-permute-start.19
  96.3 8.1 %next_product.4 = f32[768,384]{1,0:T(8,128)} custom-call(s32[1]{0:T(128)} %bitcast.19.places, bf16[768,1536]{1,0:T(8,128)(2,1)} %get-tuple-element.67.refs_0_, bf16[768,1536]{1,0:T(8,128)(2,1)} %get-tuple-element.68.refs_1_, f32[768,384]{1,0:T(8,128)} %copy-done.3, f32[768,384]{1,0:T(8,128)} %copy-done.4, f32[768,384]{1,0:T(8,128)} %copy-done.5, ...), custom_call_target="tpu_custom_call" | custom-call | flops 768 | bytes 768 | tf_op jit(solution)/shard_map/product/next_product/pallas_call | solution.py:148
  104.5 1.5 add.151
  105.9 0.4 collective-permute-start.20
  106.4 1.4 collective-permute-done.18
  108.2 3.9 %collective-permute-done.19 = f32[768,384]{1,0:T(8,128)} collective-permute-done((f32[768,384]{1,0:T(8,128)}, f32[768,384]{1,0:T(8,128)}, u32[]{:S(2)}, u32[]{:S(2)}) %collective-permute-start.19) | collective-permute-done | bytes 1179680 | tf_op jit(solution)/shard_map/product/ppermute | solution.py:30
  112.1 7.8 %collective-permute-start.24 = (f32[768,128]{1,0:T(8,128)S(1)}, f32[768,128]{1,0:T(8,128)S(1)}, u32[]{:S(2)}, u32[]{:S(2)}) collective-permute-start(f32[768,128]{1,0:T(8,128)S(1)} %slice.38), channel_id=1, source_target_pairs={{0,8},{8,0},{16,24},{24,16},{1,9},{9,1},{17,25},{25,17},{2,10},{10... | collective-permute-start | bytes 1179656 | tf_op jit(solution)/shard_map/turned/ppermute | solution.py:341
  119.9 8.1 %next_product.5 = f32[768,384]{1,0:T(8,128)} custom-call(s32[1]{0:T(128)} %bitcast.places, bf16[768,1536]{1,0:T(8,128)(2,1)} %get-tuple-element.67.refs_0_, bf16[768,1536]{1,0:T(8,128)(2,1)} %get-tuple-element.68.refs_1_, f32[768,384]{1,0:T(8,128)} %copy-done.3, f32[768,384]{1,0:T(8,128)} %copy-done.4, f32[768,384]{1,0:T(8,128)} %copy-done.5, ...), custom_call_target="tpu_custom_call" | custom-call | flops 8000000000 | bytes 768 | tf_op jit(solution)/shard_map/total/next_product/pallas_call | solution.py:148
  128.1 0.8 collective-permute-done.24
  129.0 0.4 copy-done.15
  129.3 1.4 add_add_fusion
  131.0 0.9 fusion.3
  131.9 0.8 fusion
  132.8 0.8 dynamic-slice_bitcast_fusion.2
  133.5 0.5 collective-permute-start.25
  134.7 1.5 collective-permute-start.22
  136.3 1.7 collective-permute-start.26
  138.0 1.7 collective-permute-start.27
  139.7 5.0 %collective-permute-done.26 = f32[128,640]{1,0:T(8,128)S(1)} collective-permute-done((f32[128,640]{1,0:T(8,128)S(1)}, f32[128,640]{1,0:T(8,128)S(1)}, u32[]{:S(2)}, u32[]{:S(2)}) %collective-permute-start.26) | collective-permute-done | bytes 327712 | tf_op jit(solution)/shard_map/quad/ppermute | solution.py:30
  144.6 2.7 %collective-permute-done.23 = f32[384,384]{0,1:T(8,128)S(1)} collective-permute-done((f32[384,384]{0,1:T(8,128)S(1)}, f32[384,384]{0,1:T(8,128)S(1)}, u32[]{:S(2)}, u32[]{:S(2)}) %collective-permute-start.23) | collective-permute-done | bytes 589856 | tf_op jit(solution)/shard_map/out/ppermute | solution.py:364
  147.4 1.1 broadcast_select_fusion.3
  148.6 0.4 convolution_subtract_fusion.1
  149.0 6.6 %collective-permute-done.28 = f32[128,640]{1,0:T(8,128)S(1)} collective-permute-done((f32[128,640]{1,0:T(8,128)S(1)}, f32[128,640]{1,0:T(8,128)S(1)}, u32[]{:S(2)}, u32[]{:S(2)}) %collective-permute-start.28) | collective-permute-done | bytes 327712 | tf_op jit(solution)/shard_map/quad/ppermute | solution.py:30
  155.7 0.8 add_add_fusion.1
  156.5 1.6 collective-permute-start.29
  158.1 7.0 %collective-permute-start.30 = (f32[128,640]{1,0:T(8,128)}, f32[128,640]{1,0:T(8,128)S(1)}, u32[]{:S(2)}, u32[]{:S(2)}) collective-permute-start(f32[128,640]{1,0:T(8,128)} %add_add_fusion.1), channel_id=1, source_target_pairs={{0,8},{1,0},{8,24},{9,16},{16,9},{17,1},{24,25},{25,17},{2,10},{3,... | collective-permute-start | bytes 983048 | tf_op jit(solution)/shard_map/quad/ppermute | solution.py:287
  165.1 4.5 %collective-permute-start.31 = (f32[128,640]{1,0:T(8,128)}, f32[128,640]{1,0:T(8,128)S(1)}, u32[]{:S(2)}, u32[]{:S(2)}) collective-permute-start(f32[128,640]{1,0:T(8,128)} %add_add_fusion.1), channel_id=1, source_target_pairs={{0,16},{1,24},{8,0},{9,8},{16,17},{17,25},{24,1},{25,9},{2,18},{3,... | collective-permute-start | bytes 983048 | tf_op jit(solution)/shard_map/quad/ppermute | solution.py:287
  169.5 1.9 %collective-permute-start.32 = (f32[128,640]{1,0:T(8,128)}, f32[128,640]{1,0:T(8,128)S(1)}, u32[]{:S(2)}, u32[]{:S(2)}) collective-permute-start(f32[128,640]{1,0:T(8,128)} %add_add_fusion.1), channel_id=1, source_target_pairs={{0,24},{1,16},{8,8},{9,0},{16,25},{17,17},{24,9},{25,1},{2,26},{3,... | collective-permute-start | bytes 983048 | tf_op jit(solution)/shard_map/quad/ppermute | solution.py:287
  171.4 0.4 convolution_subtract_fusion
  171.9 1.1 copy.28
  173.1 0.9 copy.27
  174.0 8.9 %collective-permute-done.31.refs_2_ = f32[128,640]{1,0:T(8,128)S(1)} collective-permute-done((f32[128,640]{1,0:T(8,128)}, f32[128,640]{1,0:T(8,128)S(1)}, u32[]{:S(2)}, u32[]{:S(2)}) %collective-permute-start.31) | collective-permute-done | bytes 327712 | tf_op jit(solution)/shard_map/quad/ppermute | solution.py:287
  182.9 2.4 %finish.1 = (f32[1,256,256]{2,1,0:T(8,128)}, f32[2,256,256]{2,1,0:T(8,128)}, f32[2,256,256]{2,1,0:T(8,128)}) custom-call(s32[4]{0:T(128)S(1)} %pad_add_fusion.z, f32[128,640]{1,0:T(8,128)S(1)} %collective-permute-done.29.refs_0_, f32[128,640]{1,0:T(8,128)S(1)} %collective-permute-done.30.refs_1_, f32[128,640]{1,0:T(8,128)S(1)} %collective-permute-done.31.refs_2_, ...), custom_call_target="tpu_custom_call" | custom-call | flops 100000000 | bytes 1000000 | tf_op jit(solution)/shard_map/diag/finish/pallas_call | solution.py:203
  (83 shorter events, 3.5 us)
Async XLA Ops:
  0.6 3.2 %copy-start.17 = (f32[768,128]{1,0:T(8,128)S(1)}, f32[768,128]{1,0:T(8,128)}, u32[]{:S(2)}) copy-start(f32[768,128]{1,0:T(8,128)} %param.9) | copy-start | bytes 1179652
  0.6 3.4 %copy-start.16 = (f32[768,256]{1,0:T(8,128)S(1)}, f32[768,256]{1,0:T(8,128)}, u32[]{:S(2)}) copy-start(f32[768,256]{1,0:T(8,128)} %param.10) | copy-start | bytes 2359300
  2.9 2.3 %collective-permute-start = (f32[192,768]{1,0:T(8,128)}, f32[192,768]{1,0:T(8,128)}, u32[]{:S(2)}, u32[]{:S(2)}) collective-permute-start(f32[192,768]{1,0:T(8,128)} %get-tuple-element.98), channel_id=1, source_target_pairs={{0,1},{1,0},{2,3},{3,2},{4,5},{5,4},{6,7},{7,6},{8,9},{9,8},{10,11... | collective-permute-start | bytes 1769480 | tf_op jit(solution)/shard_map/gather/ppermute | solution.py:22
  4.3 8.1 %copy-start.3 = (f32[768,384]{1,0:T(8,128)}, f32[768,384]{1,0:T(8,128)S(1)}, u32[]{:S(2)}) copy-start(f32[768,384]{1,0:T(8,128)S(1)} %pad_maximum_fusion.1.refs_4_.refs_2_) | copy-start | bytes 3538948
  5.2 2.8 %collective-permute-start.5 = (f32[768,384]{1,0:T(8,128)S(1)}, f32[768,384]{1,0:T(8,128)S(1)}, u32[]{:S(2)}, u32[]{:S(2)}) collective-permute-start(f32[768,384]{1,0:T(8,128)S(1)} %pad_maximum_fusion.1.refs_4_.refs_2_), channel_id=1, source_target_pairs={{0,1},{1,0},{2,3},{3,2},{4,5},{5,4},{6,7},{7,6},{8,9},{9,8},{10,11... | collective-permute-start | bytes 3538952 | tf_op jit(solution)/shard_map/gather/ppermute | solution.py:22
  6.5 9.6 %copy-start.11 = (f32[2,192,768]{2,1,0:T(8,128)}, f32[2,192,768]{2,1,0:T(8,128)S(1)}, u32[]{:S(2)}) copy-start(f32[2,192,768]{2,1,0:T(8,128)S(1)} %pad_maximum_fusion.refs_0_) | copy-start | bytes 3538948
  8.1 1.0 copy-start.4
  9.2 55.4 %copy-start.9 = (f32[4,192,384]{2,1,0:T(8,128)}, f32[4,192,384]{2,1,0:T(8,128)S(1)}, u32[]{:S(2)}) copy-start(f32[4,192,384]{2,1,0:T(8,128)S(1)} %pad_maximum_fusion.2) | copy-start | bytes 3538948
  9.2 17.6 %collective-permute-start.6 = (f32[768,384]{1,0:T(8,128)S(1)}, f32[768,384]{1,0:T(8,128)}, u32[]{:S(2)}, u32[]{:S(2)}) collective-permute-start(f32[768,384]{1,0:T(8,128)S(1)} %bitcast.61), channel_id=1, source_target_pairs={{0,2},{1,7},{2,4},{3,1},{4,6},{5,3},{6,0},{7,5},{8,10},{9,15},{10,... | collective-permute-start | bytes 3538952 | tf_op jit(solution)/shard_map/gather/ppermute | solution.py:30
  10.9 27.2 %collective-permute-start.3 = (f32[768,384]{1,0:T(8,128)S(1)}, f32[768,384]{1,0:T(8,128)S(1)}, u32[]{:S(2)}, u32[]{:S(2)}) collective-permute-start(f32[768,384]{1,0:T(8,128)S(1)} %pad_maximum_fusion.1.refs_4_.refs_2_), channel_id=1, source_target_pairs={{0,32},{1,97},{32,64},{33,1},{64,96},{65,33},{96,0},{97,65},{2,34}... | collective-permute-start | bytes 3538952 | tf_op jit(solution)/shard_map/gather/ppermute | solution.py:30
  12.4 28.0 %collective-permute-start.4 = (f32[768,384]{1,0:T(8,128)S(1)}, f32[768,384]{1,0:T(8,128)S(1)}, u32[]{:S(2)}, u32[]{:S(2)}) collective-permute-start(f32[768,384]{1,0:T(8,128)S(1)} %pad_maximum_fusion.1.refs_4_.refs_2_), channel_id=1, source_target_pairs={{0,96},{1,33},{32,0},{33,65},{64,32},{65,97},{96,64},{97,1},{2,98}... | collective-permute-start | bytes 3538952 | tf_op jit(solution)/shard_map/gather/ppermute | solution.py:30
  14.2 28.3 %collective-permute-start.1 = (f32[2,192,768]{2,1,0:T(8,128)S(1)}, f32[2,192,768]{2,1,0:T(8,128)S(1)}, u32[]{:S(2)}, u32[]{:S(2)}) collective-permute-start(f32[2,192,768]{2,1,0:T(8,128)S(1)} %pad_maximum_fusion.refs_0_), channel_id=1, source_target_pairs={{0,8},{1,25},{8,16},{9,1},{16,24},{17,9},{24,0},{25,17},{2,10},{3,... | collective-permute-start | bytes 3538952 | tf_op jit(solution)/shard_map/gather/ppermute | solution.py:30
  16.1 28.0 %collective-permute-start.2 = (f32[2,192,768]{2,1,0:T(8,128)S(1)}, f32[2,192,768]{2,1,0:T(8,128)S(1)}, u32[]{:S(2)}, u32[]{:S(2)}) collective-permute-start(f32[2,192,768]{2,1,0:T(8,128)S(1)} %pad_maximum_fusion.refs_0_), channel_id=1, source_target_pairs={{0,24},{1,9},{8,0},{9,17},{16,8},{17,25},{24,16},{25,1},{2,26},{3,... | collective-permute-start | bytes 3538952 | tf_op jit(solution)/shard_map/gather/ppermute | solution.py:30
  26.8 17.4 %collective-permute-start.7 = (f32[768,384]{1,0:T(8,128)S(1)}, f32[768,384]{1,0:T(8,128)}, u32[]{:S(2)}, u32[]{:S(2)}) collective-permute-start(f32[768,384]{1,0:T(8,128)S(1)} %bitcast.62), channel_id=1, source_target_pairs={{0,6},{1,3},{2,0},{3,5},{4,2},{5,7},{6,4},{7,1},{8,14},{9,11},{10,... | collective-permute-start | bytes 3538952 | tf_op jit(solution)/shard_map/gather/ppermute | solution.py:30
  38.1 34.6 %copy-start.5 = (f32[768,384]{1,0:T(8,128)}, f32[768,384]{1,0:T(8,128)S(1)}, u32[]{:S(2)}) copy-start(f32[768,384]{1,0:T(8,128)S(1)} %collective-permute-done.3.refs_6_.refs_4_) | copy-start | bytes 3538948
  40.4 32.4 %copy-start.6 = (f32[768,384]{1,0:T(8,128)}, f32[768,384]{1,0:T(8,128)S(1)}, u32[]{:S(2)}) copy-start(f32[768,384]{1,0:T(8,128)S(1)} %collective-permute-done.4.refs_8_.refs_6_) | copy-start | bytes 3538948
  42.4 22.4 %copy-start.12 = (f32[2,192,768]{2,1,0:T(8,128)}, f32[2,192,768]{2,1,0:T(8,128)S(1)}, u32[]{:S(2)}) copy-start(f32[2,192,768]{2,1,0:T(8,128)S(1)} %collective-permute-done.1.refs_1_) | copy-start | bytes 3538948
  44.1 1.1 copy-start.13
  45.2 3.2 %collective-permute-start.10 = (f32[768,384]{1,0:T(8,128)S(1)}, f32[768,384]{1,0:T(8,128)S(1)}, u32[]{:S(2)}, u32[]{:S(2)}) collective-permute-start(f32[768,384]{1,0:T(8,128)S(1)} %collective-permute-done.4.refs_8_.refs_6_), channel_id=1, source_target_pairs={{0,1},{1,0},{2,3},{3,2},{4,5},{5,4},{6,7},{7,6},{8,9},{9,8},{10,11... | collective-permute-start | bytes 3538952 | tf_op jit(solution)/shard_map/gather/ppermute | solution.py:22
  46.0 4.2 %collective-permute-start.11 = (f32[768,384]{1,0:T(8,128)S(1)}, f32[768,384]{1,0:T(8,128)S(1)}, u32[]{:S(2)}, u32[]{:S(2)}) collective-permute-start(f32[768,384]{1,0:T(8,128)S(1)} %collective-permute-done.3.refs_6_.refs_4_), channel_id=1, source_target_pairs={{0,1},{1,0},{2,3},{3,2},{4,5},{5,4},{6,7},{7,6},{8,9},{9,8},{10,11... | collective-permute-start | bytes 3538952 | tf_op jit(solution)/shard_map/gather/ppermute | solution.py:22
  46.0 17.7 %collective-permute-start.8 = (f32[2,192,768]{2,1,0:T(8,128)S(1)}, f32[2,192,768]{2,1,0:T(8,128)S(1)}, u32[]{:S(2)}, u32[]{:S(2)}) collective-permute-start(f32[2,192,768]{2,1,0:T(8,128)S(1)} %collective-permute-done.1.refs_1_), channel_id=1, source_target_pairs={{0,8},{1,25},{8,16},{9,1},{16,24},{17,9},{24,0},{25,17},{2,10},{3,... | collective-permute-start | bytes 3538952 | tf_op jit(solution)/shard_map/gather/ppermute | solution.py:30
  46.3 17.5 %collective-permute-start.9 = (f32[768,384]{1,0:T(8,128)S(1)}, f32[768,384]{1,0:T(8,128)}, u32[]{:S(2)}, u32[]{:S(2)}) collective-permute-start(f32[768,384]{1,0:T(8,128)S(1)} %collective-permute-done.3.refs_6_.refs_4_), channel_id=1, source_target_pairs={{0,32},{1,97},{32,64},{33,1},{64,96},{65,33},{96,0},{97,65},{2,34}... | collective-permute-start | bytes 3538952 | tf_op jit(solution)/shard_map/gather/ppermute | solution.py:30
  47.1 17.7 %collective-permute-start.14 = (f32[768,384]{1,0:T(8,128)}, f32[768,384]{1,0:T(8,128)}, u32[]{:S(2)}, u32[]{:S(2)}) collective-permute-start(f32[768,384]{1,0:T(8,128)} %collective-permute-done.6), channel_id=1, source_target_pairs={{0,2},{1,7},{2,4},{3,1},{4,6},{5,3},{6,0},{7,5},{8,10},{9,15},{10,... | collective-permute-start | bytes 3538952 | tf_op jit(solution)/shard_map/gather/ppermute | solution.py:30
  48.4 24.3 %copy-start.7 = (f32[768,384]{1,0:T(8,128)}, f32[768,384]{1,0:T(8,128)S(1)}, u32[]{:S(2)}) copy-start(f32[768,384]{1,0:T(8,128)S(1)} %collective-permute-done.10.refs_7_.refs_5_) | copy-start | bytes 3538948
  50.1 13.7 %copy-start.8 = (f32[768,384]{1,0:T(8,128)}, f32[768,384]{1,0:T(8,128)S(1)}, u32[]{:S(2)}) copy-start(f32[768,384]{1,0:T(8,128)S(1)} %collective-permute-done.11.refs_9_.refs_7_) | copy-start | bytes 3538948
  63.6 1.2 copy-start.14
  63.8 8.9 %collective-permute-start.12 = (f32[768,384]{1,0:T(8,128)}, f32[768,384]{1,0:T(8,128)}, u32[]{:S(2)}, u32[]{:S(2)}) collective-permute-start(f32[768,384]{1,0:T(8,128)} %collective-permute-done.9.refs_10_.refs_8_), channel_id=1, source_target_pairs={{0,1},{1,0},{2,3},{3,2},{4,5},{5,4},{6,7},{7,6},{8,9},{9,8},{10,11... | collective-permute-start | bytes 3538952 | tf_op jit(solution)/shard_map/gather/ppermute | solution.py:22
  64.8 29.0 %collective-permute-start.15 = (f32[768,384]{1,0:T(8,128)}, f32[768,384]{1,0:T(8,128)}, u32[]{:S(2)}, u32[]{:S(2)}) collective-permute-start(f32[768,384]{1,0:T(8,128)} %collective-permute-done.14), channel_id=1, source_target_pairs={{0,32},{1,97},{34,66},{35,3},{68,100},{69,37},{102,6},{103,71},{8,... | collective-permute-start | bytes 3538952 | tf_op jit(solution)/shard_map/product/ppermute | solution.py:307
  69.9 36.5 %collective-permute-start.17 = (f32[768,384]{1,0:T(8,128)}, f32[768,384]{1,0:T(8,128)}, u32[]{:S(2)}, u32[]{:S(2)}) collective-permute-start(f32[768,384]{1,0:T(8,128)} %collective-permute-done.6), channel_id=1, source_target_pairs={{0,96},{1,33},{34,2},{35,67},{68,36},{69,101},{102,70},{103,7},{8,... | collective-permute-start | bytes 3538952 | tf_op jit(solution)/shard_map/product/ppermute | solution.py:307
  82.1 22.3 %collective-permute-start.13 = (f32[768,384]{1,0:T(8,128)}, f32[768,384]{1,0:T(8,128)S(1)}, u32[]{:S(2)}, u32[]{:S(2)}) collective-permute-start(f32[768,384]{1,0:T(8,128)} %get-tuple-element.55), channel_id=1, source_target_pairs={{0,2},{1,7},{2,4},{3,1},{4,6},{5,3},{6,0},{7,5},{8,10},{9,15},{10,... | collective-permute-start | bytes 3538952 | tf_op jit(solution)/shard_map/product/ppermute | solution.py:30
  90.3 17.4 %collective-permute-start.18 = (f32[768,384]{1,0:T(8,128)}, f32[768,384]{1,0:T(8,128)S(1)}, u32[]{:S(2)}, u32[]{:S(2)}) collective-permute-start(f32[768,384]{1,0:T(8,128)} %collective-permute-done.7), channel_id=1, source_target_pairs={{0,32},{1,97},{34,66},{35,3},{68,100},{69,37},{102,6},{103,71},{8,... | collective-permute-start | bytes 3538952 | tf_op jit(solution)/shard_map/product/ppermute | solution.py:307
  93.8 13.9 %collective-permute-start.16 = (f32[768,384]{1,0:T(8,128)}, f32[768,384]{1,0:T(8,128)S(1)}, u32[]{:S(2)}, u32[]{:S(2)}) collective-permute-start(f32[768,384]{1,0:T(8,128)} %collective-permute-done.15), channel_id=1, source_target_pairs={{32,64},{97,65},{66,98},{3,99},{100,4},{37,5},{6,38},{71,39},{40,7... | collective-permute-start | bytes 3538952 | tf_op jit(solution)/shard_map/product/ppermute | solution.py:307
  94.6 17.5 %collective-permute-start.19 = (f32[768,384]{1,0:T(8,128)}, f32[768,384]{1,0:T(8,128)}, u32[]{:S(2)}, u32[]{:S(2)}) collective-permute-start(f32[768,384]{1,0:T(8,128)} %next_product.3), channel_id=1, source_target_pairs={{0,6},{1,3},{2,0},{3,5},{4,2},{5,7},{6,4},{7,1},{8,14},{9,11},{10,... | collective-permute-start | bytes 3538952 | tf_op jit(solution)/shard_map/product/ppermute | solution.py:30
  104.4 3.3 %copy-start.10 = (f32[4,192,384]{2,1,0:T(8,128)S(1)}, f32[4,192,384]{2,1,0:T(8,128)}, u32[]{:S(2)}) copy-start(f32[4,192,384]{2,1,0:T(8,128)} %copy-done.9) | copy-start | bytes 3538948
  105.9 23.0 %collective-permute-start.20 = (f32[768,384]{1,0:T(8,128)S(1)}, f32[768,384]{1,0:T(8,128)S(1)}, u32[]{:S(2)}, u32[]{:S(2)}) collective-permute-start(f32[768,384]{1,0:T(8,128)S(1)} %add.151), channel_id=1, source_target_pairs={{0,2},{1,7},{2,4},{3,1},{4,6},{5,3},{6,0},{7,5},{8,10},{9,15},{10,... | collective-permute-start | bytes 3538952 | tf_op jit(solution)/shard_map/product/ppermute | solution.py:30
  112.1 16.8 %collective-permute-start.24 = (f32[768,128]{1,0:T(8,128)S(1)}, f32[768,128]{1,0:T(8,128)S(1)}, u32[]{:S(2)}, u32[]{:S(2)}) collective-permute-start(f32[768,128]{1,0:T(8,128)S(1)} %slice.38), channel_id=1, source_target_pairs={{0,8},{8,0},{16,24},{24,16},{1,9},{9,1},{17,25},{25,17},{2,10},{10... | collective-permute-start | bytes 1179656 | tf_op jit(solution)/shard_map/turned/ppermute | solution.py:341
  128.1 1.3 copy-start.15
  130.9 3.1 %collective-permute-start.21 = (f32[384,384]{1,0:T(8,128)S(1)}, f32[384,384]{1,0:T(8,128)S(1)}, u32[]{:S(2)}, u32[]{:S(2)}) collective-permute-start(f32[384,384]{1,0:T(8,128)S(1)} %get-tuple-element.95), channel_id=1, source_target_pairs={{0,1},{1,0},{2,3},{3,2},{4,5},{5,4},{6,7},{7,6},{8,9},{9,8},{10,11... | collective-permute-start | bytes 1769480 | tf_op jit(solution)/shard_map/out/ppermute | solution.py:22
  133.5 2.7 %collective-permute-start.25 = (f32[128,640]{1,0:T(8,128)}, f32[128,640]{1,0:T(8,128)S(1)}, u32[]{:S(2)}, u32[]{:S(2)}) collective-permute-start(f32[128,640]{1,0:T(8,128)} %dynamic-slice_bitcast_fusion.2), channel_id=1, source_target_pairs={{0,1},{1,0},{2,3},{3,2},{4,5},{5,4},{6,7},{7,6},{8,9},{9,8},{10,11... | collective-permute-start | bytes 983048 | tf_op jit(solution)/shard_map/quad/ppermute | solution.py:22
  134.4 13.0 %collective-permute-start.23 = (f32[384,384]{0,1:T(8,128)S(1)}, f32[384,384]{0,1:T(8,128)S(1)}, u32[]{:S(2)}, u32[]{:S(2)}) collective-permute-start(f32[384,384]{0,1:T(8,128)S(1)} %bitcast.70), channel_id=1, source_target_pairs={{0,8},{1,24},{8,0},{9,16},{16,9},{17,25},{24,1},{25,17},{2,10},{3,... | collective-permute-start | bytes 1769480 | tf_op jit(solution)/shard_map/out/ppermute | solution.py:364
  134.7 12.7 %collective-permute-start.22 = (f32[384,384]{0,1:T(8,128)S(1)}, f32[384,384]{0,1:T(8,128)}, u32[]{:S(2)}, u32[]{:S(2)}) collective-permute-start(f32[384,384]{0,1:T(8,128)S(1)} %bitcast.69), channel_id=1, source_target_pairs={{0,0},{1,16},{8,8},{9,24},{16,1},{17,17},{24,9},{25,25},{2,2},{3,1... | collective-permute-start | bytes 1769480 | tf_op jit(solution)/shard_map/out/ppermute | solution.py:364
  136.3 8.4 %collective-permute-start.26 = (f32[128,640]{1,0:T(8,128)S(1)}, f32[128,640]{1,0:T(8,128)S(1)}, u32[]{:S(2)}, u32[]{:S(2)}) collective-permute-start(f32[128,640]{1,0:T(8,128)S(1)} %bitcast_add_fusion), channel_id=1, source_target_pairs={{0,32},{1,97},{32,64},{33,1},{64,96},{65,33},{96,0},{97,65},{2,34}... | collective-permute-start | bytes 983048 | tf_op jit(solution)/shard_map/quad/ppermute | solution.py:30
  138.0 10.6 %copy-start = (f32[2,256,256]{2,1,0:T(8,128)S(1)}, f32[2,256,256]{2,1,0:T(8,128)}, u32[]{:S(2)}) copy-start(f32[2,256,256]{2,1,0:T(8,128)} %refs_4_.1) | copy-start | bytes 1572868
  138.0 11.0 %collective-permute-start.27 = (f32[128,640]{1,0:T(8,128)S(1)}, f32[128,640]{1,0:T(8,128)S(1)}, u32[]{:S(2)}, u32[]{:S(2)}) collective-permute-start(f32[128,640]{1,0:T(8,128)S(1)} %bitcast_add_fusion), channel_id=1, source_target_pairs={{0,96},{1,33},{32,0},{33,65},{64,32},{65,97},{96,64},{97,1},{2,98}... | collective-permute-start | bytes 983048 | tf_op jit(solution)/shard_map/quad/ppermute | solution.py:30
  147.4 8.3 %collective-permute-start.28 = (f32[128,640]{1,0:T(8,128)S(1)}, f32[128,640]{1,0:T(8,128)S(1)}, u32[]{:S(2)}, u32[]{:S(2)}) collective-permute-start(f32[128,640]{1,0:T(8,128)S(1)} %collective-permute-done.26), channel_id=1, source_target_pairs={{0,32},{1,97},{32,64},{33,1},{64,96},{65,33},{96,0},{97,65},{2,34}... | collective-permute-start | bytes 983048 | tf_op jit(solution)/shard_map/quad/ppermute | solution.py:30
  156.5 17.6 %collective-permute-start.29 = (f32[128,640]{1,0:T(8,128)}, f32[128,640]{1,0:T(8,128)S(1)}, u32[]{:S(2)}, u32[]{:S(2)}) collective-permute-start(f32[128,640]{1,0:T(8,128)} %add_add_fusion.1), channel_id=1, source_target_pairs={{0,0},{1,8},{8,16},{9,24},{16,1},{17,9},{24,17},{25,25},{2,2},{3,1... | collective-permute-start | bytes 983048 | tf_op jit(solution)/shard_map/quad/ppermute | solution.py:287
  158.1 15.9 %collective-permute-start.30 = (f32[128,640]{1,0:T(8,128)}, f32[128,640]{1,0:T(8,128)S(1)}, u32[]{:S(2)}, u32[]{:S(2)}) collective-permute-start(f32[128,640]{1,0:T(8,128)} %add_add_fusion.1), channel_id=1, source_target_pairs={{0,8},{1,0},{8,24},{9,16},{16,9},{17,1},{24,25},{25,17},{2,10},{3,... | collective-permute-start | bytes 983048 | tf_op jit(solution)/shard_map/quad/ppermute | solution.py:287
  165.1 17.8 %collective-permute-start.31 = (f32[128,640]{1,0:T(8,128)}, f32[128,640]{1,0:T(8,128)S(1)}, u32[]{:S(2)}, u32[]{:S(2)}) collective-permute-start(f32[128,640]{1,0:T(8,128)} %add_add_fusion.1), channel_id=1, source_target_pairs={{0,16},{1,24},{8,0},{9,8},{16,17},{17,25},{24,1},{25,9},{2,18},{3,... | collective-permute-start | bytes 983048 | tf_op jit(solution)/shard_map/quad/ppermute | solution.py:287
  169.5 13.4 %collective-permute-start.32 = (f32[128,640]{1,0:T(8,128)}, f32[128,640]{1,0:T(8,128)S(1)}, u32[]{:S(2)}, u32[]{:S(2)}) collective-permute-start(f32[128,640]{1,0:T(8,128)} %add_add_fusion.1), channel_id=1, source_target_pairs={{0,24},{1,16},{8,8},{9,0},{16,25},{17,17},{24,9},{25,1},{2,26},{3,... | collective-permute-start | bytes 983048 | tf_op jit(solution)/shard_map/quad/ppermute | solution.py:287
  173.1 9.8 %copy-start.1 = (f32[2,256,256]{2,1,0:T(8,128)S(1)}, f32[2,256,256]{2,1,0:T(8,128)}, u32[]{:S(2)}) copy-start(f32[2,256,256]{2,1,0:T(8,128)} %refs_6_.1) | copy-start | bytes 1572868
  173.1 9.8 %copy-start.2 = (f32[1,256,256]{2,1,0:T(8,128)S(1)}, f32[1,256,256]{2,1,0:T(8,128)}, u32[]{:S(2)}) copy-start(f32[1,256,256]{2,1,0:T(8,128)} %refs_5_.1) | copy-start | bytes 786436
